TPU v7x, 32 devices: a whole 2x2x4 slice. The times are simulated.
32 devices in a mesh: dp: 8 (over y, x, core), inner: 4 (over z).
Axes of the slice: x: 2, y: 2, z: 4, core: 2. Of those that a mesh axis runs over, the one named last changes fastest.
Arguments:
- frames_in: bfloat16 [32, 1024, 1024], P(('dp', 'inner')), may hold values from -6 to 6
- lengths: int32 [32], P(('dp', 'inner')), may hold values from 1 to 1024, 24576 in all
- first_gain: float32 [1024], replicated, may hold values from 0.1 to 1.9
- first_shift: float32 [1024], replicated, may hold values from -3 to 3
- attend_weight: bfloat16 [1024, 3072], P('dp', 'inner'), may hold values from -0.1875 to 0.1875
- attend_bias: float32 [2, 1024], replicated, may hold values from -3 to 3
- output_weight: bfloat16 [1024, 1024], P('dp', 'inner'), may hold values from -3 to 3
- output_bias: float32 [1024], replicated, may hold values from -3 to 3
- second_gain: float32 [1024], replicated, may hold values from 0.1 to 1.9
- second_shift: float32 [1024], replicated, may hold values from -3 to 3
- up_weight: bfloat16 [1024, 4096], P('dp', 'inner'), may hold values from -0.1875 to 0.1875
- up_bias: float32 [4096], replicated, may hold values from -3 to 3
- down_weight: bfloat16 [4096, 1024], P('dp', 'inner'), may hold values from -0.125 to 0.125
- down_bias: float32 [1024], replicated, may hold values from -3 to 3
- cotangent: bfloat16 [32, 1024, 1024], P(('dp', 'inner')), may hold values from -6 to 6
Outputs:
- frames_out: bfloat16 [32, 1024, 1024], P(('dp', 'inner'))
- gradient_frames: bfloat16 [32, 1024, 1024], P(('dp', 'inner'))
- gradient_first_gain: float32 [1024], replicated
- gradient_first_shift: float32 [1024], replicated
- gradient_attend_weight: float32 [1024, 3072], P('dp', 'inner')
- gradient_attend_bias: float32 [2, 1024], replicated
- gradient_output_weight: float32 [1024, 1024], P('dp', 'inner')
- gradient_output_bias: float32 [1024], replicated
- gradient_second_gain: float32 [1024], replicated
- gradient_second_shift: float32 [1024], replicated
- gradient_up_weight: float32 [1024, 4096], P('dp', 'inner')
- gradient_up_bias: float32 [4096], replicated
- gradient_down_weight: float32 [4096, 1024], P('dp', 'inner')
- gradient_down_bias: float32 [1024], replicated
Inputs may be any that keep to these rules, and one draw needn't show every extreme that they name: The longest utterance fills its slot of 1024 frames exactly, and the lengths fill three quarters of all slots.
All inputs are finite; a program needn't handle non-finite values. No bound on the sum of `lengths` on one device may be relied on, other than what follows from the above.
Results may differ from a plain program's by a relative error of at most 0.012.
Values may be sent and summed in bfloat16 or wider, within the bound.
No kernel may reach another device: no remote copies, remote signals or barrier semaphores. Data moves between devices by JAX's collectives and lax.ppermute only.
A program may use at most 320 MiB of HBM per device.

v0:
```python
import functools

import jax
import jax.numpy as jnp
from jax import lax
from jax.experimental import pallas as pl
from jax.experimental.pallas import tpu as pltpu
from jax.sharding import PartitionSpec as P

HEADS = 16
HEAD = 64
TILE = 1024
ROWS = 256
LOG2E = 1.4426950408889634
MASKED = -1e30
SCALE = HEAD ** (-0.5)
BF = jnp.bfloat16
F32 = jnp.float32
LIMIT = 60 * 2**20


def dot(left, right, on_left, on_right):
    return lax.dot_general(
        left, right, (((on_left,), (on_right,)), ((), ())), preferred_element_type=F32
    )


def normalise(values):
    center = values - jnp.mean(values, axis=-1, keepdims=True)
    spread = jnp.mean(center * center, axis=-1, keepdims=True)
    scale = lax.rsqrt(spread + 1e-05)
    return center * scale, scale


def params(name_limit=LIMIT):
    return pltpu.CompilerParams(vmem_limit_bytes=name_limit)


def estimate(flops, moved, exps=0):
    return pl.CostEstimate(
        flops=int(8 * flops), bytes_accessed=int(8 * moved), transcendentals=int(8 * exps)
    )


ANY = pl.BlockSpec(memory_space=pl.ANY)
SMEM = pl.BlockSpec(memory_space=pltpu.SMEM)


def whole(*shape):
    return pl.BlockSpec(shape, lambda *_: (0,) * len(shape))


def vec(size):
    return jax.ShapeDtypeStruct((1, size), F32)


PIECES = 8
SLOTS = 4
T_ROW = 0
T_COL = 8
T_SLOT_IN = 12
T_SLOT_OUT = 16
T_PAIR = 20
T_OUT = 24
T_PLACE = 32
T_CORE = 40
T_SIZE = 48


def make_table(spread, relative):
    if not spread:
        order = list(range(4))
        entries = [0] * T_SIZE
        entries[T_PAIR : T_PAIR + 4] = order
        entries[T_COL : T_COL + 4] = order
        return jnp.array(entries, jnp.int32)
    row = lax.axis_index("dp").astype(jnp.int32)
    column = lax.axis_index("inner").astype(jnp.int32)
    core = row & 1
    near = jnp.where(core == 0, 2, 4)
    far = 6 - near
    entries = [
        row,
        row ^ near,
        row ^ far,
        row ^ 6,
        row ^ 1,
        row ^ 1 ^ far,
        row ^ 1 ^ near,
        row ^ 7,
    ]
    if relative:
        entries += [(column - block) & 3 for block in range(4)] * 2
    else:
        entries += [0, 1, 2, 3] * 2
    entries += [(block - column) & 3 for block in range(4)]
    pair = row >> 1
    entries += [pair, pair ^ (near >> 1), pair ^ (far >> 1), pair ^ 3]
    for half in range(2):
        a, b = (far, near) if half == 0 else (near, far)
        own = row ^ half
        entries += [own ^ 6, own ^ a, own ^ b, own]
    for half in range(2):
        first = far if half == 0 else near
        for block in range(4):
            relative = (pair ^ block) << 1
            entries.append(
                jnp.where(
                    relative == 6,
                    0,
                    jnp.where(relative == 0, 3, jnp.where(relative == first, 1, 2)),
                )
            )
    entries += [core]
    entries += [jnp.int32(0)] * (T_SIZE - len(entries))
    return jnp.stack([jnp.asarray(entry, jnp.int32) for entry in entries])


def aligned(index, size):
    return pl.ds(pl.multiple_of(index * size, size), size)


def load_slot(pieces, tab, step, target, sems, width):
    if len(pieces) == 1:
        return load_columns(pieces, tab, tab[T_COL + step], target, sems, width)
    rows = pieces[0].shape[-2]
    copies = []
    for p in range(PIECES):
        source = pieces[p] if step == 0 else pieces[PIECES + p].at[step - 1]
        place = target.at[aligned(tab[T_ROW + p], rows), :]
        copies.append(pltpu.make_async_copy(source, place, sems.at[p]))
    return copies


def load_columns(pieces, tab, block, target, sems, width, first=0):
    if len(pieces) == 1:
        copies = [
            pltpu.make_async_copy(pieces[0].at[:, aligned(block, width)], target, sems.at[0])
        ]
        return copies
    slot = tab[T_SLOT_IN + block]
    rows = pieces[0].shape[1]
    return [
        pltpu.make_async_copy(
            pieces[p].at[slot, :, pl.ds(first, width)],
            target.at[aligned(tab[T_ROW + p], rows), :],
            sems.at[p],
        )
        for p in range(PIECES)
    ]


def load_rows(pieces, tab, step, target, sems):
    if len(pieces) == 1 and len(pieces[0].shape) == 2:
        return [
            pltpu.make_async_copy(
                pieces[0].at[aligned(tab[T_PAIR + step], TILE), :], target, sems.at[0]
            )
        ]
    rows, width = pieces[0].shape[-2:]
    if len(pieces) == 1:
        return [
            pltpu.make_async_copy(
                pieces[0].at[2 * tab[T_PAIR + step] + half, block],
                target.at[pl.ds(half * rows, rows), pl.ds(block * width, width)],
                sems.at[half * SLOTS + block],
            )
            for half in range(2)
            for block in range(4)
        ]
    partner = (4, 6, 5, 7)[step]
    copies = []
    for n, p in enumerate((step, partner)):
        half = tab[T_ROW + p] & 1
        for slot in range(SLOTS):
            copies.append(
                pltpu.make_async_copy(
                    pieces[p].at[slot],
                    target.at[aligned(half, rows), aligned(tab[T_COL + slot], width)],
                    sems.at[n * SLOTS + slot],
                )
            )
    return copies


def load_all(pieces, tab, target, sems, width, first=0):
    if len(pieces) == 1:
        return [pltpu.make_async_copy(pieces[0], target, sems.at[0])]
    rows = pieces[0].shape[1]
    return [
        pltpu.make_async_copy(
            pieces[p].at[slot, :, pl.ds(first, width)],
            target.at[aligned(tab[T_ROW + p], rows), aligned(tab[T_COL + slot], width)],
            sems.at[p * SLOTS + slot],
        )
        for p in range(PIECES)
        for slot in range(SLOTS)
    ]


def store_column_block(outs, tab, block, source, sems, width, first=0):
    if len(outs) == 1:
        return [pltpu.make_async_copy(source, outs[0].at[:, aligned(block, width)], sems.at[0])]
    rows = outs[0].shape[2]
    slot = tab[T_SLOT_OUT + block]
    return [
        pltpu.make_async_copy(
            source.at[aligned(tab[T_OUT + half * 4 + place], rows), :],
            outs[half].at[place, slot, :, pl.ds(first, width)],
            sems.at[half * 4 + place],
        )
        for half in range(2)
        for place in range(4)
    ]


def store_row_pair(outs, tab, pair, source, sems):
    if len(outs) == 1:
        return [pltpu.make_async_copy(source, outs[0].at[aligned(pair, TILE), :], sems.at[0])]
    rows, width = outs[0].shape[2:]
    copies = []
    for half in range(2):
        local = tab[T_CORE] ^ half
        for block in range(4):
            copies.append(
                pltpu.make_async_copy(
                    source.at[aligned(local, rows), pl.ds(block * width, width)],
                    outs[half].at[tab[T_PLACE + half * 4 + pair], tab[T_SLOT_OUT + block]],
                    sems.at[half * 4 + block],
                )
            )
    return copies


def chunks(extent, size, body, init=0):
    for first in range(0, extent, size):
        init = body(pl.ds(first, size), init)
    return init


def start(copies):
    for copy in copies:
        copy.start()


def wait(copies):
    for copy in copies:
        copy.wait()


def gradient_shapes(spread, rows, columns, dp, inner):
    if spread:
        return [jax.ShapeDtypeStruct((4, 4, rows // dp, columns // inner), BF)] * 2
    return [jax.ShapeDtypeStruct((rows, columns), BF)]


def project_kernel(count, tab, tokens, gain, shift, bias, *rest):
    pieces = rest[:count]
    normed, project, weight, sems = rest[count:]
    step = pl.program_id(0)
    width = project.shape[0]

    def fetch(index):
        slot = index % 2
        return load_slot(pieces, tab, index, weight.at[slot], sems.at[slot], width)

    @pl.when(step == 0)
    def _():
        start(fetch(0))

        def norm(rows, carry):
            unit, _ = normalise(tokens[rows, :].astype(F32))
            normed[rows, :] = (unit * gain[...] + shift[...]).astype(BF)
            return carry

        chunks(tokens.shape[0], ROWS, norm)

    def arrive(index):
        if index + 1 < 4:
            start(fetch(index + 1))
        wait(fetch(index))

    for index in range(4):
        pl.when(step == index)(functools.partial(arrive, index))

    column = jnp.transpose(jnp.broadcast_to(bias[...], (128, width)))[:, :1]

    project[...] = (dot(weight[lax.rem(step, 2)], normed[...], 0, 1) + column).astype(BF)


def project_call(tab, tokens, gain, shift, bias, pieces):
    extent, model = tokens.shape
    width = 3 * model // 4
    grid = pltpu.PrefetchScalarGridSpec(
        num_scalar_prefetch=1,
        grid=(4,),
        in_specs=[whole(extent, model), whole(1, model), whole(1, model)]
        + [pl.BlockSpec((1, width), lambda i, tab: (0, tab[T_COL + i]))]
        + [ANY] * len(pieces),
        out_specs=[
            whole(extent, model),
            pl.BlockSpec((width, extent), lambda i, tab: (tab[T_COL + i], 0)),
        ],
        scratch_shapes=[
            pltpu.VMEM((2, model, width), BF),
            pltpu.SemaphoreType.DMA((2, 8)),
        ],
    )
    return pl.pallas_call(
        functools.partial(project_kernel, len(pieces)),
        grid_spec=grid,
        out_shape=[
            jax.ShapeDtypeStruct((extent, model), BF),
            jax.ShapeDtypeStruct((3 * model, extent), BF),
        ],
        compiler_params=params(),
        cost_estimate=estimate(6 * extent * model * model, 16e6),
        name="project",
    )(tab, tokens, gain, shift, bias, *pieces)


def causal_bias(block):
    key = lax.broadcasted_iota(jnp.int32, (block, block), 0)
    query = lax.broadcasted_iota(jnp.int32, (block, block), 1)
    return jnp.where(key <= query, 0.0, MASKED)


def extend_rows(length, extent):
    first = lax.broadcasted_iota(jnp.int32, (16, extent), 0) == 0
    past = lax.broadcasted_iota(jnp.int32, (16, extent), 1) >= length
    key_rows = jnp.where(first & past, MASKED, 0.0).astype(BF)
    query_rows = jnp.where(first, 1.0, 0.0).astype(BF)
    return key_rows, query_rows


def attention_kernel(group, block, lengths, query, key, value, *rest):
    mixture, totals, keys, queries, causal = rest[-5:]
    extent = query.shape[1]

    @pl.when(pl.program_id(0) == 0)
    def _():
        causal[...] = causal_bias(block)

    key_rows, query_rows = extend_rows(lengths[0], extent)
    for head in range(group):
        part = pl.ds(HEAD * head, HEAD)
        keys[head, :HEAD, :] = key[part, :]
        keys[head, HEAD:, :] = key_rows
        queries[head, :HEAD, :] = query[part, :]
        queries[head, HEAD:, :] = query_rows
    for head in range(group):
        part = pl.ds(HEAD * head, HEAD)
        for tile in range(extent // block):
            place = pl.ds(tile * block, block)
            own = queries[head, :, place]
            scores = []
            for other in range(tile + 1):
                score = dot(keys[head, :, pl.ds(other * block, block)], own, 0, 0)
                scores.append(score + causal[...] if other == tile else score)
            highest = scores[0].max(0, keepdims=True)
            for score in scores[1:]:
                highest = jnp.maximum(highest, score.max(0, keepdims=True))
            offset = highest * (SCALE * LOG2E)
            summed = jnp.zeros((1, block), F32)
            total = jnp.zeros((HEAD, block), F32)
            for other, score in enumerate(scores):
                weight = jnp.exp2(score * (SCALE * LOG2E) - offset)
                summed = summed + weight.sum(0, keepdims=True)
                total = total + dot(value[part, pl.ds(other * block, block)], weight.astype(BF), 1, 0)
            mixture[part, place] = (total * (1.0 / summed)).astype(BF)
            totals[0, pl.ds(head, 1), place] = offset + jnp.log2(summed)


def attention_call(lengths, project, part_of=(0, 1), earlier=()):
    extent = project.shape[1]
    group, block = 2, min(512, extent)
    size, groups = HEAD * group, HEADS // group
    steps = groups // part_of[1]
    base = steps * part_of[0]

    def part(section):
        return pl.BlockSpec((size, extent), lambda i: (i + base + section * groups, 0))

    pairs = extent * extent * 5 // 8
    return pl.pallas_call(
        functools.partial(attention_kernel, group, block),
        grid=(steps,),
        in_specs=[SMEM, part(0), part(1), part(2)] + [ANY] * len(earlier),
        out_specs=[part(0), pl.BlockSpec((1, group, extent), lambda i: (i + base, 0, 0))],
        out_shape=[
            jax.ShapeDtypeStruct((HEADS * HEAD, extent), BF),
            jax.ShapeDtypeStruct((groups, group, extent), F32),
        ],
        input_output_aliases={4 + n: n for n in range(len(earlier))},
        scratch_shapes=[
            pltpu.VMEM((group, HEAD + 16, extent), BF),
            pltpu.VMEM((group, HEAD + 16, extent), BF),
            pltpu.VMEM((block, block), F32),
        ],
        compiler_params=params(),
        cost_estimate=estimate(16 * HEADS * pairs * HEAD / part_of[1], 8e6),
        name="attention",
    )(lengths, project, project, project, *earlier)


def gelu_parts(hidden):
    chance = 0.5 + 0.5 * lax.erf(hidden * 0.7071067811865476)
    density = jnp.exp2(hidden * hidden * (-0.5 * LOG2E)) * 0.3989422804014327
    return hidden * chance, chance + hidden * density


def out_kernel(
    count, tab, lengths, mixture, frames, cotangent, out_bias, gain, shift, *rest
):
    pieces = rest[:count]
    middle, normed, result, down_bias, out_weight, sems = rest[count:]
    step = pl.program_id(0)
    model = mixture.shape[0]

    size = frames.shape[0]

    def fetch():
        return load_all(pieces, tab, out_weight, sems, model // 4, TILE)

    @pl.when(step == 0)
    def _():
        start(fetch())
        down_bias[...] = jnp.zeros_like(down_bias)

    def mask(rows, sums):
        place = step * size + rows.start + lax.broadcasted_iota(jnp.int32, (ROWS, 1), 0)
        masked = jnp.where(place < lengths[0], cotangent[rows, :].astype(F32), 0.0)
        result[rows, :] = masked.astype(BF)
        return sums + masked.sum(0, keepdims=True)

    down_bias[...] += chunks(size, ROWS, mask, jnp.zeros((1, model), F32))

    @pl.when(step == 0)
    def _():
        wait(fetch())

    def branch(rows, carry):
        total = dot(mixture[:, rows], out_weight[...], 0, 0) + out_bias[...]
        total = frames[rows, :].astype(F32) + total
        middle[rows, :] = total
        unit, _ = normalise(total)
        normed[rows, :] = (unit * gain[...] + shift[...]).astype(BF)
        return carry

    chunks(size, ROWS, branch)


def out_call(tab, lengths, mixture, frames, cotangent, vectors, pieces):
    model, extent = mixture.shape
    size = min(512, extent)
    block = pl.BlockSpec((size, model), lambda i: (i, 0))
    return pl.pallas_call(
        functools.partial(out_kernel, len(pieces)),
        grid=(extent // size,),
        in_specs=[SMEM, SMEM]
        + [pl.BlockSpec((model, size), lambda i: (0, i)), block, block]
        + [whole(1, model)] * 3
        + [ANY] * len(pieces),
        out_specs=[block, block, block, whole(1, model)],
        out_shape=[
            jax.ShapeDtypeStruct((extent, model), F32),
            jax.ShapeDtypeStruct((extent, model), BF),
            jax.ShapeDtypeStruct((extent, model), BF),
            vec(model),
        ],
        scratch_shapes=[pltpu.VMEM((model, model), BF), pltpu.SemaphoreType.DMA((32,))],
        compiler_params=params(),
        cost_estimate=estimate(1, 1),
        name="out",
    )(tab, lengths, mixture, frames, cotangent, *vectors, *pieces)


def up_kernel(counts, base, tab, normed, result, up_bias, *rest):
    count_up, count_earlier, count_grad = counts
    up_pieces, rest = rest[:count_up], rest[count_up + count_earlier :]
    active, slope = rest[:2]
    grads, rest = rest[2 : 2 + count_grad], rest[2 + count_grad :]
    weight, staged, sems_up, sems_grad = rest
    step = pl.program_id(0)
    steps = pl.num_programs(0)
    extent = normed.shape[0]

    def fetch(index):
        slot = lax.rem(index, 2)
        return load_columns(
            up_pieces, tab, base + index, weight.at[slot], sems_up.at[slot], TILE
        )

    def send(index):
        slot = lax.rem(index, 2)
        return store_row_pair(grads, tab, base + index, staged.at[slot], sems_grad.at[slot])

    @pl.when(step == 0)
    def _():
        start(fetch(step))

    @pl.when(step + 1 < steps)
    def _():
        start(fetch(step + 1))

    wait(fetch(step))
    now = lax.rem(step, 2)

    def widen(rows, carry):
        hidden = dot(normed[rows, :], weight[now], 1, 0) + up_bias[...]
        value, grade = gelu_parts(hidden)
        active[rows, :] = value.astype(BF)
        slope[rows, :] = grade.astype(BF)
        return carry

    chunks(extent, ROWS, widen)

    @pl.when(step >= 2)
    def _():
        wait(send(step - 2))

    def weigh(columns, carry):
        staged[now, columns, :] = dot(active[:, columns], result[...], 0, 0).astype(BF)
        return carry

    chunks(TILE, ROWS, weigh)
    start(send(step))

    @pl.when(step == steps - 1)
    def _():
        wait(send(step - 1))
        wait(send(step))


def up_call(tab, normed, result, up_bias, up_pieces, spread, sizes, part_of=(0, 1), earlier=()):
    extent, model = normed.shape
    hidden = 4 * model
    grads = gradient_shapes(spread, hidden, model, *sizes)
    steps = hidden // TILE // part_of[1]
    base = steps * part_of[0]
    tile = pl.BlockSpec((extent, TILE), lambda i: (0, base + i))
    aliases = {4 + len(up_pieces) + n: n for n in range(len(earlier))}
    return pl.pallas_call(
        functools.partial(up_kernel, (len(up_pieces), len(earlier), len(grads)), base),
        grid=(steps,),
        in_specs=[SMEM, whole(extent, model), whole(extent, model)]
        + [pl.BlockSpec((1, TILE), lambda i: (0, base + i))]
        + [ANY] * (len(up_pieces) + len(earlier)),
        out_specs=[tile, tile] + [ANY] * len(grads),
        out_shape=[
            jax.ShapeDtypeStruct((extent, hidden), BF),
            jax.ShapeDtypeStruct((extent, hidden), BF),
        ]
        + grads,
        input_output_aliases=aliases,
        scratch_shapes=[
            pltpu.VMEM((2, model, TILE), BF),
            pltpu.VMEM((2, TILE, model), BF),
            pltpu.SemaphoreType.DMA((2, 8)),
            pltpu.SemaphoreType.DMA((2, 8)),
        ],
        compiler_params=params(),
        cost_estimate=estimate(16 * extent * model * model / part_of[1], 50e6, extent * hidden),
        name="up",
    )(tab, normed, result, up_bias, *up_pieces, *earlier)


def back_kernel(counts, tab, mixture, middle, normed, d_result, slope, *rest):
    count_out, count_up, count_down, count_grad = counts
    gain = rest[0]
    rest = rest[1:]
    out_pieces, rest = rest[:count_out], rest[count_out:]
    up_pieces, rest = rest[:count_up], rest[count_up:]
    down_pieces, rest = rest[:count_down], rest[count_down:]
    d_middle, d_mixture, up_bias, gain_grad, shift_grad, out_bias = rest[:6]
    rest = rest[6:]
    grads, rest = rest[:count_grad], rest[count_grad:]
    (
        mixed,
        out_weight,
        total,
        unit_rows,
        result,
        down,
        up,
        d_hidden,
        d_normed,
        staged,
        sems_in,
        sems_out,
        sems_down,
        sems_up,
        sems_grad,
    ) = rest
    spread = len(grads[0].shape) == 4
    if spread:
        up_grads = out_grads = grads
    else:
        up_grads, out_grads = grads[:1], grads[1:]
    step = pl.program_id(0)
    steps = pl.num_programs(0)
    extent, model = result.shape
    width = model // 4

    def fetch(index):
        slot = index % 2
        copies = load_rows(down_pieces, tab, index, down.at[slot], sems_down.at[slot])
        block = tab[T_PAIR + index]
        copies += load_columns(up_pieces, tab, block, up.at[slot], sems_up.at[slot], TILE)
        return copies

    def send(index):
        slot = index % 2
        block = tab[T_PAIR + index]
        return store_column_block(
            up_grads, tab, block, staged.at[slot], sems_grad.at[slot], TILE
        )

    def send_out(block):
        return store_column_block(
            out_grads,
            tab,
            block,
            staged.at[0, :, pl.ds(block * width, width)],
            sems_out.at[pl.ds(block * 8, 8)],
            width,
            TILE if spread else 0,
        )

    def early(n):
        pair = ((d_result, result), (normed, unit_rows))[n]
        return pltpu.make_async_copy(*pair, sems_in.at[n])

    def late():
        return [
            pltpu.make_async_copy(middle, total, sems_in.at[2]),
            pltpu.make_async_copy(mixture, mixed, sems_in.at[3]),
        ] + load_all(out_pieces, tab, out_weight, sems_out, width, TILE)

    now = lax.rem(step, 2)

    @pl.when(step == 0)
    def _():
        early(0).start()
        start(fetch(0))
        early(1).start()
        early(0).wait()
        d_normed[...] = jnp.zeros_like(d_normed)

    def arrive(index):
        if index == 2:
            start(late())
        if index + 1 < 4:
            start(fetch(index + 1))
        wait(fetch(index))
        if index >= 2:
            wait(send(index - 2))

    for index in range(4):
        pl.when(step == index)(functools.partial(arrive, index))

    def shrink(rows, sums):
        d_active = dot(result[rows, :], down[now], 1, 1)
        piece = (d_active * slope[rows, :].astype(F32)).astype(BF)
        d_hidden[rows, :] = piece
        return sums + piece.astype(F32).sum(0, keepdims=True)

    up_bias[...] = chunks(extent, ROWS, shrink, jnp.zeros((1, TILE), F32))

    @pl.when(step == 0)
    def _():
        early(1).wait()

    def weigh(columns, carry):
        staged[now, columns, :] = dot(unit_rows[:, columns], d_hidden[...], 0, 0).astype(BF)
        return carry

    chunks(model, ROWS, weigh)
    for index in range(4):
        pl.when(step == index)(lambda index=index: start(send(index)))

    def widen(rows, carry):
        d_normed[rows, :] += dot(d_hidden[rows, :], up[now], 1, 1)
        return carry

    @pl.when(step < steps - 1)
    def _():
        chunks(extent, ROWS, widen)

    @pl.when(step == steps - 1)
    def _():
        wait(late())
        none = jnp.zeros((1, model), F32)

        def norm(rows, sums):
            grade = d_normed[rows, :] + dot(d_hidden[rows, :], up[now], 1, 1)
            unit, scale = normalise(total[rows, :])
            gains = sums[0] + (grade * unit).sum(0, keepdims=True)
            shifts = sums[1] + grade.sum(0, keepdims=True)
            grade = grade * gain[...]
            level = jnp.mean(grade, axis=-1, keepdims=True)
            tilt = jnp.mean(grade * unit, axis=-1, keepdims=True)
            d_total = result[rows, :].astype(F32) + scale * (grade - level - unit * tilt)
            d_middle[rows, :] = d_total
            branch = d_total.astype(BF)
            unit_rows[rows, :] = branch
            return gains, shifts, sums[2] + branch.astype(F32).sum(0, keepdims=True)

        sums = chunks(extent, ROWS, norm, (none, none, none))
        gain_grad[...], shift_grad[...], out_bias[...] = sums
        wait(send(2))

        def weigh_out(rows, carry):
            staged[0, rows, :] = dot(mixed[rows, :], unit_rows[...], 1, 0).astype(BF)
            return carry

        chunks(model, ROWS, weigh_out)
        for block in range(4):
            start(send_out(block))

        def turn(rows, carry):
            d_mixture[rows, :] = dot(out_weight[rows, :], unit_rows[...], 1, 1).astype(BF)
            return carry

        chunks(model, ROWS, turn)
        wait(send(3))
        for block in range(4):
            wait(send_out(block))


def back_call(tab, mixture, middle, normed, d_result, slope, gain, pieces, spread, sizes):
    out_pieces, up_pieces, down_pieces = pieces
    model, extent = mixture.shape
    hidden = slope.shape[1]
    if spread:
        grads = gradient_shapes(spread, model, hidden + model, *sizes)
    else:
        grads = gradient_shapes(spread, model, hidden, *sizes)
        grads += gradient_shapes(spread, model, model, *sizes)
    steps = hidden // TILE
    grid = pltpu.PrefetchScalarGridSpec(
        num_scalar_prefetch=1,
        grid=(steps,),
        in_specs=[ANY, ANY, ANY, ANY]
        + [pl.BlockSpec((extent, TILE), lambda i, tab: (0, tab[T_PAIR + i]))]
        + [whole(1, model)]
        + [ANY] * (len(out_pieces) + len(up_pieces) + len(down_pieces)),
        out_specs=[
            whole(extent, model),
            whole(model, extent),
            pl.BlockSpec((1, TILE), lambda i, tab: (0, tab[T_PAIR + i])),
            whole(1, model),
            whole(1, model),
            whole(1, model),
        ]
        + [ANY] * len(grads),
        scratch_shapes=[
            pltpu.VMEM((model, extent), BF),
            pltpu.VMEM((model, model), BF),
            pltpu.VMEM((extent, model), F32),
            pltpu.VMEM((extent, model), BF),
            pltpu.VMEM((extent, model), BF),
            pltpu.VMEM((2, TILE, model), BF),
            pltpu.VMEM((2, model, TILE), BF),
            pltpu.VMEM((extent, TILE), BF),
            pltpu.VMEM((extent, model), F32),
            pltpu.VMEM((2, model, TILE), BF),
            pltpu.SemaphoreType.DMA((4,)),
            pltpu.SemaphoreType.DMA((32,)),
            pltpu.SemaphoreType.DMA((2, 8)),
            pltpu.SemaphoreType.DMA((2, 8)),
            pltpu.SemaphoreType.DMA((2, 8)),
        ],
    )
    return pl.pallas_call(
        functools.partial(
            back_kernel, (len(out_pieces), len(up_pieces), len(down_pieces), len(grads))
        ),
        grid_spec=grid,
        out_shape=[
            jax.ShapeDtypeStruct((extent, model), F32),
            jax.ShapeDtypeStruct((model, extent), BF),
            vec(hidden),
            vec(model),
            vec(model),
            vec(model),
        ]
        + grads,
        compiler_params=params(),
        cost_estimate=estimate(28 * extent * model * model, 60e6),
        name="back",
    )(
        tab,
        mixture,
        middle,
        normed,
        d_result,
        slope,
        gain,
        *out_pieces,
        *up_pieces,
        *down_pieces,
    )


def attention_back_kernel(
    group,
    block,
    lengths,
    query,
    key,
    value,
    mixture,
    d_mixture,
    totals,
    *rest,
):
    d_project, keys, queries, causal, d_keys, d_values = rest[-6:]
    extent = query.shape[1]

    @pl.when(pl.program_id(0) == 0)
    def _():
        causal[...] = causal_bias(block)

    key_rows, query_rows = extend_rows(lengths[0], extent)
    for head in range(group):
        part = pl.ds(HEAD * head, HEAD)
        keys[head, :HEAD, :] = key[part, :]
        keys[head, HEAD:, :] = key_rows
        queries[head, :HEAD, :] = query[part, :]
        queries[head, HEAD:, :] = query_rows
    for head in range(group):
        part = pl.ds(HEAD * head, HEAD)
        for tile in range(extent // block):
            place = pl.ds(tile * block, block)
            own = queries[head, :, place]
            grade = d_mixture[part, place]
            center = (grade.astype(F32) * mixture[part, place].astype(F32)).sum(0, keepdims=True)
            total = totals[0, pl.ds(head, 1), place]
            d_query = jnp.zeros((HEAD, block), F32)
            for other in range(tile + 1):
                span = pl.ds(other * block, block)
                score = dot(keys[head, :, span], own, 0, 0)
                if other == tile:
                    score = score + causal[...]
                weight = jnp.exp2(score * (SCALE * LOG2E) - total)
                d_weight = dot(value[part, span], grade, 0, 0)
                d_score = (weight * (d_weight - center)).astype(BF)
                d_value = dot(grade, weight.astype(BF), 1, 1)
                d_key = dot(query[part, place], d_score, 1, 1)
                d_query = d_query + dot(key[part, span], d_score, 1, 0)
                if other == tile:
                    d_values[:, span] = d_value
                    d_keys[:, span] = d_key
                else:
                    d_values[:, span] += d_value
                    d_keys[:, span] += d_key
            d_project[0, part, place] = (d_query * SCALE).astype(BF)
        d_project[1, part, :] = (d_keys[...] * SCALE).astype(BF)
        d_project[2, part, :] = d_values[...].astype(BF)


def attention_back_call(
    lengths, project, mixture, d_mixture, totals, base=0, ending=HEADS // 2, earlier=()
):
    extent = project.shape[1]
    group, block = 2, min(512, extent)
    size, groups = HEAD * group, HEADS // group
    steps = ending - base

    def part(section):
        return pl.BlockSpec((size, extent), lambda i: (i + base + section * groups, 0))

    pairs = extent * extent * 5 // 8
    return pl.pallas_call(
        functools.partial(attention_back_kernel, group, block),
        grid=(steps,),
        in_specs=[SMEM, part(0), part(1), part(2), part(0), part(0)]
        + [pl.BlockSpec((1, group, extent), lambda i: (i + base, 0, 0))]
        + [ANY] * len(earlier),
        out_specs=pl.BlockSpec((3, size, extent), lambda i: (0, i + base, 0)),
        out_shape=jax.ShapeDtypeStruct((3, HEADS * HEAD, extent), BF),
        input_output_aliases={7: 0} if earlier else {},
        scratch_shapes=[
            pltpu.VMEM((group, HEAD + 16, extent), BF),
            pltpu.VMEM((group, HEAD + 16, extent), BF),
            pltpu.VMEM((block, block), F32),
            pltpu.VMEM((HEAD, extent), F32),
            pltpu.VMEM((HEAD, extent), F32),
        ],
        compiler_params=params(),
        cost_estimate=estimate(4 * HEADS * pairs * HEAD * steps / groups, 1e6),
        name="attention_back",
    )(lengths, project, project, project, mixture, d_mixture, totals, *earlier)


def attend_grad_kernel(count_grad, tab, d_project, normed, *rest):
    bias_grad = rest[0]
    grads, rest = rest[1 : 1 + count_grad], rest[1 + count_grad :]
    staged, sems_grad = rest
    step = pl.program_id(0)
    steps = pl.num_programs(0)
    extent, model = normed.shape
    width = d_project.shape[0]

    def send(block):
        slot = lax.rem(block, 2)
        return store_column_block(grads, tab, block, staged.at[slot], sems_grad.at[slot], width)

    @pl.when(step >= 2)
    def _():
        wait(send(step - 2))

    now = lax.rem(step, 2)

    def weigh(columns, carry):
        staged[now, columns, :] = dot(normed[:, columns], d_project[...], 0, 1).astype(BF)
        return carry

    chunks(model, ROWS, weigh)
    start(send(step))
    bias_grad[...] = dot(jnp.ones((8, extent), BF), d_project[...], 1, 1)[:1, :]

    @pl.when(step == steps - 1)
    def _():
        wait(send(step - 1))
        wait(send(step))


def attend_grad_call(tab, d_project, normed, spread, sizes):
    extent, model = normed.shape
    width = 3 * model // 4
    grads = gradient_shapes(spread, model, 3 * model, *sizes)
    return pl.pallas_call(
        functools.partial(attend_grad_kernel, len(grads)),
        grid=(4,),
        in_specs=[SMEM, pl.BlockSpec((width, extent), lambda i: (i, 0)), whole(extent, model)],
        out_specs=[pl.BlockSpec((1, width), lambda i: (0, i))] + [ANY] * len(grads),
        out_shape=[vec(3 * model)] + grads,
        scratch_shapes=[
            pltpu.VMEM((2, model, width), BF),
            pltpu.SemaphoreType.DMA((2, 8)),
        ],
        compiler_params=params(),
        cost_estimate=estimate(6 * extent * model * model, 14e6),
        name="attend_grad",
    )(tab, d_project, normed)


def first_kernel(count_in, tab, d_project, frames, d_middle, gain, *rest):
    pieces, rest = rest[:count_in], rest[count_in:]
    bias_grad, *early = rest[:6]
    d_frames, small, weight, total, d_normed, sems, sem_total = rest[6:]
    step = pl.program_id(0)
    steps = pl.num_programs(0)
    extent, model = frames.shape
    width = d_project.shape[0]

    def fetch(index):
        slot = index % 2
        return load_slot(pieces, tab, index, weight.at[slot], sems.at[slot], width)

    def late():
        return pltpu.make_async_copy(d_middle, total, sem_total)

    @pl.when(step == 0)
    def _():
        start(fetch(0))
        late().start()
        d_normed[...] = jnp.zeros_like(d_normed)

    def arrive(index):
        if index + 1 < 4:
            start(fetch(index + 1))
        wait(fetch(index))

    for index in range(4):
        pl.when(step == index)(functools.partial(arrive, index))
    now = lax.rem(step, 2)

    def widen(rows, carry):
        d_normed[rows, :] += dot(d_project[:, rows], weight[now], 0, 1)
        return carry

    @pl.when(step < steps - 1)
    def _():
        chunks(extent, ROWS, widen)

    @pl.when(step == steps - 1)
    def _():
        late().wait()
        none = jnp.zeros((1, model), F32)

        def norm(rows, sums):
            grade = d_normed[rows, :] + dot(d_project[:, rows], weight[now], 0, 1)
            unit, scale = normalise(frames[rows, :].astype(F32))
            gains = sums[0] + (grade * unit).sum(0, keepdims=True)
            shifts = sums[1] + grade.sum(0, keepdims=True)
            grade = grade * gain[...]
            level = jnp.mean(grade, axis=-1, keepdims=True)
            tilt = jnp.mean(grade * unit, axis=-1, keepdims=True)
            d_frames[rows, :] = (total[rows, :] + scale * (grade - level - unit * tilt)).astype(BF)
            return gains, shifts

        gains, shifts = chunks(extent, ROWS, norm, (none, none))
        bias = bias_grad[...]
        vectors = [gains, shifts, bias[:, :model], bias[:, 2 * model :]]
        vectors += [vector[...] for vector in early]
        place = 0
        for vector in vectors:
            for column in range(0, vector.shape[1], 128):
                small[place : place + 1, :] = vector[:, column : column + 128]
                place += 1


def small_kernel(*refs):
    *terms, a, b, c, d, e, f, g, h = refs
    terms = [term[...] for term in terms]
    total = tree_sum(terms)
    place = 0
    for out in (a, b, c, d, e, f, g, h):
        out[...] = total[place : place + out.shape[0], :]
        place += out.shape[0]


def small_call(terms):
    unit = terms[0].shape[0] // 12
    sizes = [unit, unit, 2 * unit, unit, unit, unit, unit, 4 * unit]
    return pl.pallas_call(
        small_kernel,
        out_shape=[jax.ShapeDtypeStruct((size, 128), F32) for size in sizes],
        name="small",
    )(*terms)


def first_call(tab, d_project, frames, d_middle, gain, pieces, vectors):
    extent, model = frames.shape
    width = 3 * model // 4
    count = model + sum(vector.shape[1] for vector in vectors)
    grid = pltpu.PrefetchScalarGridSpec(
        num_scalar_prefetch=1,
        grid=(4,),
        in_specs=[pl.BlockSpec((width, extent), lambda i, tab: (tab[T_COL + i], 0))]
        + [whole(extent, model), ANY, whole(1, model)]
        + [ANY] * len(pieces)
        + [whole(*vector.shape) for vector in vectors],
        out_specs=[whole(extent, model), whole(count // 128, 128)],
        scratch_shapes=[
            pltpu.VMEM((2, model, width), BF),
            pltpu.VMEM((extent, model), F32),
            pltpu.VMEM((extent, model), F32),
            pltpu.SemaphoreType.DMA((2, 8)),
            pltpu.SemaphoreType.DMA,
        ],
    )
    return pl.pallas_call(
        functools.partial(first_kernel, len(pieces)),
        grid_spec=grid,
        out_shape=[
            jax.ShapeDtypeStruct((extent, model), BF),
            jax.ShapeDtypeStruct((count // 128, 128), F32),
        ],
        compiler_params=params(),
        cost_estimate=estimate(6 * extent * model * model, 24e6),
        name="first",
    )(tab, d_project, frames, d_middle, gain, *pieces, *vectors)


def down_kernel(count, base, ending, tab, active, middle, bias, *rest):
    pieces = rest[:count]
    frames_out, weight, total, sems = rest[count:]
    step = pl.program_id(0)
    steps = pl.num_programs(0)

    def fetch(index):
        slot = (index - base) % 2
        return load_rows(pieces, tab, index, weight.at[slot], sems.at[slot])

    def arrive(index):
        if index == base:
            start(fetch(index))
        if index + 1 < ending:
            start(fetch(index + 1))
        wait(fetch(index))

    for index in range(base, ending):
        pl.when(step == index - base)(functools.partial(arrive, index))

    @pl.when(step == 0)
    def _():
        total[...] = middle[...] + bias[...] if base == 0 else middle[...]

    def widen(rows, carry):
        total[rows, :] += dot(active[rows, :], weight[lax.rem(step, 2)], 1, 0)
        return carry

    chunks(total.shape[0], ROWS, widen)

    @pl.when(step == steps - 1)
    def _():
        frames_out[...] = total[...].astype(frames_out.dtype)


def down_call(tab, active, middle, bias, pieces, part_of=(0, 1)):
    extent, hidden = active.shape
    model = middle.shape[1]
    steps = hidden // TILE // part_of[1]
    base = steps * part_of[0]
    last = part_of[0] + 1 == part_of[1]
    grid = pltpu.PrefetchScalarGridSpec(
        num_scalar_prefetch=1,
        grid=(steps,),
        in_specs=[pl.BlockSpec((extent, TILE), lambda i, tab: (0, tab[T_PAIR + base + i]))]
        + [whole(extent, model), whole(1, model)]
        + [ANY] * len(pieces),
        out_specs=whole(extent, model),
        scratch_shapes=[
            pltpu.VMEM((2, TILE, model), BF),
            pltpu.VMEM((extent, model), F32),
            pltpu.SemaphoreType.DMA((2, 8)),
        ],
    )
    return pl.pallas_call(
        functools.partial(down_kernel, len(pieces), base, base + steps),
        grid_spec=grid,
        out_shape=jax.ShapeDtypeStruct((extent, model), BF if last else F32),
        compiler_params=params(),
        cost_estimate=estimate(8 * extent * model * model, 24e6),
        name="down",
    )(tab, active, middle, bias, *pieces)


def gather_plain(weight):
    wide = lax.all_gather(weight, "inner", axis=1, tiled=True)
    return [lax.all_gather(wide, "dp", axis=0, tiled=True)]


def scatter_plain(grads):
    wide = lax.psum_scatter(grads[0], "dp", scatter_dimension=0, tiled=True)
    return lax.psum_scatter(wide, "inner", scatter_dimension=1, tiled=True).astype(F32)


CORE, NEAR, FAR = 0, 1, 2


def swap(value, way):
    flips = {CORE: (1, 1), NEAR: (2, 4), FAR: (4, 2)}[way]
    return lax.ppermute(value, "dp", [(d, d ^ flips[d & 1]) for d in range(8)])


def shift(value, amount):
    return lax.ppermute(value, "inner", [(i, (i + amount) & 3) for i in range(4)])


def after(value, *done):
    return lax.optimization_barrier((value, done))[0]


def stack_spread(block):
    return jnp.stack([block] + [shift(block, amount) for amount in (1, 2, 3)])


def added(*values):
    total = values[0].astype(F32)
    for value in values[1:]:
        total = total + value.astype(F32)
    return total


def add_kernel(count, *refs):
    total = added(*[ref[...] for ref in refs[:count]])
    outs = refs[count:]
    if len(outs) == 1:
        outs[0][...] = total.reshape(outs[0].shape).astype(BF)
        return
    for index, out in enumerate(outs):

        @pl.when(pl.program_id(0) == index)
        def _(out=out):
            out[...] = total.reshape(out.shape).astype(out.dtype)


def add_call(terms, outs, grid):
    rows, columns = terms[0][0].shape[-2:]
    specs = []
    for term, place in terms:
        if term.ndim == 3:
            specs.append(pl.BlockSpec((1, rows, columns), lambda *at: (at[-1], 0, 0)))
        elif place is None:
            specs.append(pl.BlockSpec((1, 1, rows, columns), lambda p, k: (p, k, 0, 0)))
        else:
            specs.append(
                pl.BlockSpec((1, 1, rows, columns), lambda k, place=place: (place, k, 0, 0))
            )
    if len(outs) == 1:
        lead = (1,) * len(grid)
        out_specs = [pl.BlockSpec(lead + (rows, columns), lambda *at: at + (0, 0))]
    else:
        out_specs = [whole(rows, columns)] * len(outs)

    def kernel(*refs):
        ins = [
            ref.at[0] if len(ref.shape) == 3 else ref.at[0, 0] for ref in refs[: len(terms)]
        ]
        add_kernel(len(terms), *ins, *refs[len(terms) :])

    return pl.pallas_call(
        kernel,
        grid=grid,
        in_specs=specs,
        out_specs=out_specs,
        out_shape=outs,
        compiler_params=params(),
        cost_estimate=estimate(1e10, 1e7),
        name="add",
    )(*[term for term, _ in terms])


def add_first(keep, core):
    return added(keep[:2], core[:2]).astype(BF)


def add_second(keep, core, link):
    return added(keep[2], core[2], link[0]).astype(BF)


def add_third(keep, core, link, last):
    blocks = [added(keep[3, k], core[3, k], link[1, k], last[k]) for k in range(4)]
    return [blocks[0]] + [block.astype(BF) for block in blocks[1:]]


def add_third_kernel(keep, core, link, last):
    shapes = [jax.ShapeDtypeStruct(keep.shape[2:], F32)]
    shapes += [jax.ShapeDtypeStruct(keep.shape[2:], BF)] * 3
    return add_call([(keep, 3), (core, 3), (link, 1), (last, None)], shapes, (4,))


def shift_parts(parts):
    return [shift(parts[k], k) for k in (1, 2, 3)]


def exchange(values, axis, size):
    return [values] + [
        lax.ppermute(values, axis, [(i, i ^ flip) for i in range(size)])
        for flip in range(1, size)
    ]


def tree_sum(terms):
    while len(terms) > 1:
        terms = [terms[i] + terms[i + 1] for i in range(0, len(terms), 2)]
    return terms[0]


def shards(
    spread,
    sizes,
    frames_in,
    lengths,
    first_gain,
    first_shift,
    attend_weight,
    attend_bias,
    output_weight,
    output_bias,
    second_gain,
    second_shift,
    up_weight,
    up_bias,
    down_weight,
    down_bias,
    cotangent,
):
    _, extent, model = frames_in.shape
    frames = frames_in.reshape(extent, model)
    upstream = cotangent.reshape(extent, model)
    tab = make_table(spread, True)
    tab_plain = make_table(spread, False)

    def row(vector):
        return vector.reshape(1, -1)

    if not spread:
        attend_pieces = gather_plain(attend_weight)
        out_pieces = gather_plain(output_weight)
        up_pieces = gather_plain(up_weight)
        down_pieces = gather_plain(down_weight)
    else:
        others = [shift(attend_weight, amount) for amount in (1, 2, 3)]
        near, far = swap(attend_weight, NEAR), swap(attend_weight, FAR)
        others = jnp.stack(others)
        far, near = after((far, near), near, far)
        diagonal = swap(near, FAR)
        attend_pieces = [attend_weight, near, far, diagonal]
        attend_pieces += [swap(piece, CORE) for piece in attend_pieces]
        others = after(others, diagonal)
        near, far = swap(others, NEAR), swap(others, FAR)
        up_block = after(jnp.concatenate([up_weight, output_weight], axis=1), others)
        up_own = lax.all_gather(up_block, "inner")
        near, far = after((near, far), near, far)
        diagonal = swap(near, FAR)
        others = [others, near, far, diagonal]
        attend_pieces += others + [swap(piece, CORE) for piece in others]
        up_own = after(up_own, diagonal)
        up_near, up_far = swap(up_own, NEAR), swap(up_own, FAR)
        down_own = lax.all_gather(after(down_weight, up_own), "inner")
    bias_row = jnp.concatenate([attend_bias[0], jnp.zeros_like(attend_bias[0]), attend_bias[1]])
    vectors = (row(first_gain), row(first_shift), row(bias_row))
    tokens = after(frames, up_own) if spread else frames
    normed, project = project_call(tab, tokens, *vectors, attend_pieces)
    if spread:
        mixture, totals = attention_call(lengths, after(project, up_own), (0, 2))
        up_near, up_far = after((up_near, up_far), totals)
        up_diagonal = swap(up_near, FAR)
        ahead = [swap(piece, CORE) for piece in (after(up_own, totals), up_near, up_far)]
        mixture, totals = attention_call(
            lengths, after(project, up_near, up_far), (1, 2), (mixture, totals)
        )
        up_pieces = [up_own, up_near, up_far, up_diagonal]
        up_pieces += ahead + [swap(after(up_diagonal, totals), CORE)]
        out_pieces = up_pieces
    else:
        mixture, totals = attention_call(lengths, project)
    vectors = (row(output_bias), row(second_gain), row(second_shift))
    middle, normed_two, d_result, grad_down_bias = out_call(
        tab_plain, lengths, mixture, frames, upstream, vectors, out_pieces
    )
    if spread:
        down_own = after(down_own, normed_two)
        down_near, down_far = swap(down_own, NEAR), swap(down_own, FAR)
        *halves, half_grad = up_call(
            tab_plain, normed_two, d_result, row(up_bias), up_pieces, False, sizes, (0, 2)
        )
        down_near, down_far = after((down_near, down_far), halves)
        down_diagonal = swap(down_near, FAR)
        ahead = [swap(piece, CORE) for piece in (after(down_own, totals), down_near, down_far)]
        active, slope, *down_grads = up_call(
            tab_plain,
            after(normed_two, down_near, down_far),
            d_result,
            row(up_bias),
            up_pieces,
            False,
            sizes,
            (1, 2),
            (*halves, half_grad),
        )
    else:
        active, slope, *down_grads = up_call(
            tab_plain, normed_two, d_result, row(up_bias), up_pieces, False, sizes
        )
    if spread:
        down_pieces = [down_own, down_near, down_far, down_diagonal]
        down_pieces += ahead + [swap(after(down_diagonal, slope), CORE)]
        down_wide = lax.psum_scatter(down_grads[0], "dp", scatter_dimension=0, tiled=True)
    else:
        down_owned = scatter_plain(down_grads)
    (
        d_middle,
        d_mixture,
        grad_up_bias,
        grad_second_gain,
        grad_second_shift,
        grad_output_bias,
        *back_grads,
    ) = back_call(
        tab_plain,
        mixture,
        middle,
        normed_two,
        d_result,
        slope,
        row(second_gain),
        (out_pieces, up_pieces, down_pieces),
        spread,
        sizes,
    )
    early = [grad_output_bias, grad_second_gain, grad_second_shift, grad_down_bias, grad_up_bias]
    if spread:
        back_keep, back_send = back_grads
        back_core = swap(back_send, CORE)
        d_project = attention_back_call(lengths, project, mixture, d_mixture, totals, 0, 2)
        back_core = after(back_core, d_project)
        back_first = add_first(back_keep, back_core)
        back_link = swap(back_first, FAR)
        d_mixture = after(d_mixture, back_first)
        d_project = attention_back_call(
            lengths, project, mixture, d_mixture, totals, 2, HEADS // 2, (d_project,)
        )
        back_link, down_wide = after((back_link, down_wide), d_project)
        down_owned = lax.psum_scatter(down_wide, "inner", scatter_dimension=1, tiled=True)
        back_second = add_second(back_keep, back_core, back_link)
        back_last = swap(back_second, NEAR)
        d_rows = after(d_project, back_second, down_wide).reshape(3 * model, extent)
        grad_bias, attend_keep, attend_send = attend_grad_call(tab, d_rows, normed, spread, sizes)
        attend_core = swap(attend_send, CORE)
        back_last = after(back_last, grad_bias)
        back_parts = add_third_kernel(back_keep, back_core, back_link, back_last)
        back_others = shift_parts(back_parts)
        attend_core = after(attend_core, back_parts)
        attend_first = add_first(attend_keep, attend_core)
        attend_link = swap(attend_first, FAR)
        d_frames, small = first_call(
            tab,
            after(d_rows, attend_first),
            frames,
            d_middle,
            row(first_gain),
            attend_pieces,
            [grad_bias] + early,
        )
        attend_link, down_owned = after((attend_link, down_owned), d_frames)
        attend_second = add_second(attend_keep, attend_core, attend_link)
        attend_last = swap(attend_second, NEAR)
        small_terms = exchange(small, "inner", 4)
        active, middle = after((active, middle), attend_second, down_owned)
        frames_out = down_call(tab_plain, active, middle, row(down_bias), down_pieces)
        attend_last, back_others, small_terms = after(
            (attend_last, back_others, small_terms), frames_out
        )
        back_owned = added(back_parts[0], *back_others)
        small = tree_sum(small_terms)
        attend_parts = add_third(attend_keep, attend_core, attend_link, attend_last)
        attend_parts, small = after((attend_parts, small), back_owned, small, attend_parts)
        others = shift_parts(attend_parts)
        small_terms = exchange(small, "dp", 8)
        attend_owned = added(attend_parts[0], *others)
        small = small_call(after(small_terms, attend_owned))
        down_owned = down_owned.astype(F32)
        up_owned, output_owned = back_owned[:, :TILE], back_owned[:, TILE:]
    else:
        d_project = attention_back_call(lengths, project, mixture, d_mixture, totals)
        d_rows = d_project.reshape(3 * model, extent)
        grad_bias, *attend_grads = attend_grad_call(tab, d_rows, normed, spread, sizes)
        d_frames, small = first_call(
            tab,
            d_rows,
            frames,
            d_middle,
            row(first_gain),
            attend_pieces,
            [grad_bias] + early,
        )
        frames_out = down_call(tab_plain, active, middle, row(down_bias), down_pieces)
        up_owned = scatter_plain(back_grads[:1])
        output_owned = scatter_plain(back_grads[1:])
        attend_owned = scatter_plain(attend_grads)
        small = small_call([lax.psum(small, ("dp", "inner"))])
    small = [vector.reshape(-1) for vector in small]

    return (
        frames_out.reshape(frames_in.shape),
        d_frames.reshape(frames_in.shape),
        small[0],
        small[1],
        attend_owned,
        small[2].reshape(2, model),
        output_owned,
        small[3],
        small[4],
        small[5],
        up_owned,
        small[7],
        down_owned,
        small[6],
    )


def solution(mesh):
    sizes = (mesh.shape["dp"], mesh.shape["inner"])
    spread = sizes == (8, 4)
    return jax.shard_map(
        functools.partial(shards, spread, sizes),
        mesh=mesh,
        in_specs=(
            P(("dp", "inner"), None, None),
            P(("dp", "inner")),
            P(),
            P(),
            P("dp", "inner"),
            P(),
            P("dp", "inner"),
            P(),
            P(),
            P(),
            P("dp", "inner"),
            P(),
            P("dp", "inner"),
            P(),
            P(("dp", "inner"), None, None),
        ),
        out_specs=(
            P(("dp", "inner"), None, None),
            P(("dp", "inner"), None, None),
            P(),
            P(),
            P("dp", "inner"),
            P(),
            P("dp", "inner"),
            P(),
            P(),
            P(),
            P("dp", "inner"),
            P(),
            P("dp", "inner"),
            P(),
        ),
        check_vma=False,
    )
```

profile of v0, /device:TPU:0, one launch (start us, length us, event | category | flops | bytes accessed | tf_op | source)
XLA Modules:
  0.0 383.1 jit_solution(408625192906820612)
XLA Ops:
  7.2 3.0 collective-permute-start.3
  10.3 1.5 collective-permute-start.4
  11.7 1.6 collective-permute-start
  13.3 2.6 collective-permute-start.1
  18.2 1.7 pad_maximum_fusion.1
  20.0 1.7 collective-permute-done
  21.7 6.8 %collective-permute-done.1 = bf16[128,768]{1,0:T(8,128)(2,1)S(1)} collective-permute-done((bf16[128,768]{1,0:T(8,128)(2,1)}, bf16[128,768]{1,0:T(8,128)(2,1)S(1)}, u32[]{:S(2)}, u32[]{:S(2)}) %collective-permute-start.1) | collective-permute-done | bytes 196640 | tf_op jit(solution)/shard_map/ppermute | solution.py:1152
  29.7 14.3 %collective-permute-done.6.rest_9_ = bf16[3,128,768]{2,1,0:T(8,128)(2,1)S(1)} collective-permute-done((bf16[3,128,768]{2,1,0:T(8,128)(2,1)S(1)}, bf16[3,128,768]{2,1,0:T(8,128)(2,1)S(1)}, u32[]{:S(2)}, u32[]{:S(2)}) %collective-permute-start.6) | collective-permute-done | bytes 589856 | tf_op jit(solution)/shard_map/ppermute | solution.py:1148
  47.3 6.8 %collective-permute-done.8.rest_11_ = bf16[3,128,768]{2,1,0:T(8,128)(2,1)} collective-permute-done((bf16[3,128,768]{2,1,0:T(8,128)(2,1)S(1)}, bf16[3,128,768]{2,1,0:T(8,128)(2,1)}, u32[]{:S(2)}, u32[]{:S(2)}) %collective-permute-start.8) | collective-permute-done | bytes 589856 | tf_op jit(solution)/shard_map/ppermute | solution.py:1148
  54.7 1.8 collective-permute-done.11.rest_6_
  60.1 2.8 all-gather.5.cloned.1.call-done
  62.9 1.5 collective-permute-start.17
  64.5 1.5 collective-permute-start.18
  66.0 12.9 %project.1 = (bf16[1024,1024]{1,0:T(8,128)(2,1)}, bf16[3072,1024]{1,0:T(8,128)(2,1)}) custom-call(s32[48]{0:T(128)} %stack.183.tab, bf16[1024,1024]{1,0:T(8,128)(2,1)} %bitcast.84, f32[1,1024]{1,0:T(1,128)} %bitcast.114, f32[1,1024]{1,0:T(1,128)} %bitcast.113, f32[1,3072]{1,0:T(1,128)} %bitcast.100, bf16[128,768]{1,0:T(8,128)(2,1)} %rest_0_.3, ...), custom_call_target="tpu_custom_call" | custom-call | flops 51539607552 | bytes 128000000 | tf_op jit(solution)/shard_map/project/pallas_call | solution.py:309
  78.9 13.5 %attention.2 = (bf16[1024,1024]{1,0:T(8,128)(2,1)}, f32[8,2,1024]{2,1,0:T(2,128)}) custom-call(s32[1]{0:T(128)S(6)} %copy.41.lengths, bf16[3072,1024]{1,0:T(8,128)(2,1)} %get-tuple-element.122.query.key.value, bf16[3072,1024]{1,0:T(8,128)(2,1)} %get-tuple-element.122.query.key.value, bf16[3072,1024]{1,0:T(8,128)(2,1)} %get-tuple-element.122.query.key.value), custom_call_target="tpu_custom_call" | custom-call | flops 42949672960 | bytes 64000000 | tf_op jit(solution)/shard_map/attention/pallas_call | solution.py:385
  95.3 13.4 %attention.3 = (bf16[1024,1024]{1,0:T(8,128)(2,1)}, f32[8,2,1024]{2,1,0:T(2,128)}) custom-call(s32[1]{0:T(128)S(6)} %copy.41.lengths, bf16[3072,1024]{1,0:T(8,128)(2,1)} %get-tuple-element.122.query.key.value, bf16[3072,1024]{1,0:T(8,128)(2,1)} %get-tuple-element.122.query.key.value, ...), custom_call_target="tpu_custom_call", output_to_operand_aliasing={{0}: (4, {}), {1}: (5, {})} | custom-call | flops 42949672960 | bytes 64000000 | tf_op jit(solution)/shard_map/attention/pallas_call | solution.py:385
  108.8 3.2 collective-permute-done.19.rest_3_.rest_4_.rest_12_
  112.7 2.7 collective-permute-done.23.rest_7_.rest_8_.rest_16_
  115.4 9.4 %out.1 = (f32[1024,1024]{1,0:T(8,128)}, bf16[1024,1024]{1,0:T(8,128)(2,1)}, bf16[1024,1024]{1,0:T(8,128)(2,1)}, f32[1,1024]{1,0:T(1,128)}) custom-call(s32[48]{0:T(128)} %stack.178.tab, s32[1]{0:T(128)S(6)} %copy.41.lengths, bf16[1024,1024]{1,0:T(8,128)(2,1)} %get-tuple-element.124.mixture, bf16[1024,1024]{1,0:T(8,128)(2,1)} %bitcast.85, ...), custom_call_target="tpu_custom_call" | custom-call | flops 8 | bytes 8 | tf_op jit(solution)/shard_map/out/pallas_call | solution.py:457
  124.8 1.5 collective-permute-start.24
  126.9 19.8 %up.2 = (bf16[1024,4096]{1,0:T(8,128)(2,1)}, bf16[1024,4096]{1,0:T(8,128)(2,1)}, bf16[4096,1024]{1,0:T(8,128)(2,1)}) custom-call(s32[48]{0:T(128)} %stack.178.tab, bf16[1024,1024]{1,0:T(8,128)(2,1)} %get-tuple-element.136.normed, bf16[1024,1024]{1,0:T(8,128)(2,1)} %get-tuple-element.131.result.d_result, f32[1,4096]{1,0:T(1,128)} %bitcast.110, ...), custom_call_target="tpu_custom_call" | custom-call | flops 68719476736 | bytes 400000000 | tf_op jit(solution)/shard_map/up/pallas_call | solution.py:543
  146.7 3.9 %collective-permute-done.24.rest_18_.rest_1_ = bf16[4,512,256]{2,1,0:T(8,128)(2,1)S(1)} collective-permute-done((bf16[4,512,256]{2,1,0:T(8,128)(2,1)}, bf16[4,512,256]{2,1,0:T(8,128)(2,1)S(1)}, u32[]{:S(2)}, u32[]{:S(2)}) %collective-permute-start.24) | collective-permute-done | bytes 1048608 | tf_op jit(solution)/shard_map/ppermute | solution.py:1148
  152.0 19.8 %up.3 = (bf16[1024,4096]{1,0:T(8,128)(2,1)}, bf16[1024,4096]{1,0:T(8,128)(2,1)}, bf16[4096,1024]{1,0:T(8,128)(2,1)}) custom-call(s32[48]{0:T(128)} %stack.178.tab, bf16[1024,1024]{1,0:T(8,128)(2,1)} %get-tuple-element.136.normed, ...), custom_call_target="tpu_custom_call", output_to_operand_aliasing={{0}: (12, {}), {1}: (13, {}), {2}: (14, {})} | custom-call | flops 68719476736 | bytes 400000000 | tf_op jit(solution)/shard_map/up/pallas_call | solution.py:543
  172.1 2.9 collective-permute-done.30.rest_24_.rest_7_
  174.9 47.8 %back.1 = (f32[1024,1024]{1,0:T(8,128)}, bf16[1024,1024]{1,0:T(8,128)(2,1)}, f32[1,4096]{1,0:T(1,128)}, f32[1,1024]{1,0:T(1,128)}, f32[1,1024]{1,0:T(1,128)}, /*...) custom-call(s32[48]{0:T(128)} %stack.178.tab, ...), custom_call_target="tpu_custom_call" | custom-call | flops 240518168576 | bytes 480000000 | tf_op jit(solution)/shard_map/back/pallas_call | solution.py:775
  222.8 10.3 %attention_back.2.rest_0_ = bf16[3,1024,1024]{2,1,0:T(8,128)(2,1)} custom-call(s32[1]{0:T(128)S(6)} %copy.41.lengths, bf16[3072,1024]{1,0:T(8,128)(2,1)} %get-tuple-element.122.query.key.value, bf16[3072,1024]{1,0:T(8,128)(2,1)} %get-tuple-element.122.query.key.value, bf16[3072,1024]{1,0:T(8,128)(2,1)} %get-tuple-element.122.query.key.value, ...), custom_call_target="tpu_custom_call" | custom-call | flops 5368709120 | bytes 8000000 | tf_op jit(solution)/shard_map/attention_back/pallas_call | solution.py:875
  233.1 3.2 add_convert_fusion
  237.2 26.5 %attention_back.3 = bf16[3,1024,1024]{2,1,0:T(8,128)(2,1)} custom-call(s32[1]{0:T(128)S(6)} %copy.41.lengths, bf16[3072,1024]{1,0:T(8,128)(2,1)} %get-tuple-element.122.query.key.value, bf16[3072,1024]{1,0:T(8,128)(2,1)} %get-tuple-element.122.query.key.value, bf16[3072,1024]{1,0:T(8,128)(2,1)} %get-tuple-element.122.query.key.value, ...), custom_call_target="tpu_custom_call", output_to_operand_aliasing={{}: (7, {})} | custom-call | flops 16106127360 | bytes 8000000 | tf_op jit(solution)/shard_map/attention_back/pallas_call | solution.py:875
  263.6 6.0 %collective-permute-done.32.refs_2_ = bf16[2,4,128,1280]{3,2,1,0:T(8,128)(2,1)} collective-permute-done((bf16[2,4,128,1280]{3,2,1,0:T(8,128)(2,1)S(1)}, bf16[2,4,128,1280]{3,2,1,0:T(8,128)(2,1)}, u32[]{:S(2)}, u32[]{:S(2)}) %collective-permute-start.32) | collective-permute-done | bytes 2621472 | tf_op jit(solution)/shard_map/ppermute | solution.py:1148
  269.7 2.6 fusion
  272.3 1.5 collective-permute-start.34
  273.8 12.7 %attend_grad.1 = (f32[1,3072]{1,0:T(1,128)}, bf16[4,4,128,768]{3,2,1,0:T(8,128)(2,1)}, bf16[4,4,128,768]{3,2,1,0:T(8,128)(2,1)}) custom-call(s32[48]{0:T(128)} %stack.183.tab, bf16[3072,1024]{1,0:T(8,128)(2,1)} %bitcast.81, bf16[1024,1024]{1,0:T(8,128)(2,1)} %get-tuple-element.152.normed), custom_call_target="tpu_custom_call" | custom-call | flops 51539607552 | bytes 112000000 | tf_op jit(solution)/shard_map/attend_grad/pallas_call | solution.py:934
  286.6 3.3 collective-permute-done.34.refs_3_
  291.0 5.0 %add.183 = (f32[128,1280]{1,0:T(8,128)}, bf16[128,1280]{1,0:T(8,128)(2,1)}, bf16[128,1280]{1,0:T(8,128)(2,1)}, bf16[128,1280]{1,0:T(8,128)(2,1)}) custom-call(bf16[4,4,128,1280]{3,2,1,0:T(8,128)(2,1)} %get-tuple-element.144.refs_0_, bf16[4,4,128,1280]{3,2,1,0:T(8,128)(2,1)} %collective-permute-done.31.refs_1_, ...), custom_call_target="tpu_custom_call" | custom-call | flops 80000000000 | bytes 80000000 | tf_op jit(solution)/shard_map/add/pallas_call | solution.py:1207
  296.0 1.5 collective-permute-start.37
  297.5 2.3 collective-permute-start.38
  301.3 2.9 add_convert_fusion.1
  304.8 16.1 %first.1 = (bf16[1024,1024]{1,0:T(8,128)(2,1)}, f32[96,128]{1,0:T(8,128)}) custom-call(s32[48]{0:T(128)} %stack.183.tab, bf16[3072,1024]{1,0:T(8,128)(2,1)} %bitcast.82, bf16[1024,1024]{1,0:T(8,128)(2,1)} %bitcast.86, f32[1024,1024]{1,0:T(8,128)} %get-tuple-element.163.d_middle, f32[1,1024]{1,0:T(1,128)} %bitcast.115, bf16[128,768]{1,0:T(8,128)(2,1)} %rest_0_.3, ...), custom_call_target="tpu_custom_call" | custom-call | flops 51539607552 | bytes 192000000 | tf_op jit(solution)/shard_map/first/pallas_call | solution.py:1056
  321.5 3.5 collective-permute-done.35
  325.5 2.6 fusion.1
  328.1 2.4 collective-permute-start.42
  330.5 1.5 collective-permute-start.36
  332.0 16.8 %down.1 = bf16[1024,1024]{1,0:T(8,128)(2,1)} custom-call(s32[48]{0:T(128)} %stack.178.tab, bf16[1024,4096]{1,0:T(8,128)(2,1)} %get-tuple-element.172.active, f32[1024,1024]{1,0:T(8,128)} %get-tuple-element.173.middle, f32[1,1024]{1,0:T(1,128)} %bitcast.116, bf16[4,512,256]{2,1,0:T(8,128)(2,1)} %bitcast.109, bf16[4,512,256]{2,1,0:T(8,128)(2,1)} %copy-done.16, ...), custom_call_target="tpu_custom_call" | custom-call | flops 68719476736 | bytes 192000000 | tf_op jit(solution)/shard_map/down/pallas_call | solution.py:1123
  348.8 2.1 fusion.2
  355.1 1.9 collective-permute-start.52
  362.8 4.2 %collective-permute-done.51 = bf16[128,768]{1,0:T(8,128)(2,1)S(1)} collective-permute-done((bf16[128,768]{1,0:T(8,128)(2,1)S(1)}, bf16[128,768]{1,0:T(8,128)(2,1)S(1)}, u32[]{:S(2)}, u32[]{:S(2)}) %collective-permute-start.51) | collective-permute-done | bytes 196640 | tf_op jit(solution)/shard_map/ppermute | solution.py:1152
  368.6 3.6 collective-permute-done.48.refs_6_
  373.4 1.6 small.1
  (159 shorter events, 35.3 us)
Async XLA Ops:
  7.2 55.7 %all-gather.5.cloned.1.call-start = ((), (), s32[]{:S(2)}) async-start(), calls=%async_computation.4 | async-start | bytes 1638400 | tf_op jit(solution)/shard_map/all_gather | solution.py:1299
  7.2 10.0 %collective-permute-start.3 = (bf16[128,768]{1,0:T(8,128)(2,1)}, bf16[128,768]{1,0:T(8,128)(2,1)S(1)}, u32[]{:S(2)}, u32[]{:S(2)}) collective-permute-start(bf16[128,768]{1,0:T(8,128)(2,1)} %rest_0_.3), channel_id=1, source_target_pairs={{0,16},{4,12},{8,24},{12,4},{16,0},{20,28},{24,8},{28,20},{1,17},{... | collective-permute-start | bytes 589832 | tf_op jit(solution)/shard_map/ppermute | solution.py:1148
  10.3 7.0 %collective-permute-start.4 = (bf16[128,768]{1,0:T(8,128)(2,1)}, bf16[128,768]{1,0:T(8,128)(2,1)S(1)}, u32[]{:S(2)}, u32[]{:S(2)}) collective-permute-start(bf16[128,768]{1,0:T(8,128)(2,1)} %rest_0_.3), channel_id=1, source_target_pairs={{0,8},{4,20},{8,0},{12,28},{16,24},{20,4},{24,16},{28,12},{1,9},{5... | collective-permute-start | bytes 589832 | tf_op jit(solution)/shard_map/ppermute | solution.py:1148
  11.7 9.9 %collective-permute-start = (bf16[128,768]{1,0:T(8,128)(2,1)}, bf16[128,768]{1,0:T(8,128)(2,1)S(1)}, u32[]{:S(2)}, u32[]{:S(2)}) collective-permute-start(bf16[128,768]{1,0:T(8,128)(2,1)} %rest_0_.3), channel_id=1, source_target_pairs={{0,1},{1,2},{2,3},{3,0},{4,5},{5,6},{6,7},{7,4},{8,9},{9,10},{10,1... | collective-permute-start | bytes 589832 | tf_op jit(solution)/shard_map/ppermute | solution.py:1152
  13.3 15.1 %collective-permute-start.1 = (bf16[128,768]{1,0:T(8,128)(2,1)}, bf16[128,768]{1,0:T(8,128)(2,1)S(1)}, u32[]{:S(2)}, u32[]{:S(2)}) collective-permute-start(bf16[128,768]{1,0:T(8,128)(2,1)} %rest_0_.3), channel_id=1, source_target_pairs={{0,2},{1,3},{2,0},{3,1},{4,6},{5,7},{6,4},{7,5},{8,10},{9,11},{10,... | collective-permute-start | bytes 589832 | tf_op jit(solution)/shard_map/ppermute | solution.py:1152
  15.9 12.5 %collective-permute-start.2 = (bf16[128,768]{1,0:T(8,128)(2,1)}, bf16[128,768]{1,0:T(8,128)(2,1)S(1)}, u32[]{:S(2)}, u32[]{:S(2)}) collective-permute-start(bf16[128,768]{1,0:T(8,128)(2,1)} %rest_0_.3), channel_id=1, source_target_pairs={{0,3},{1,0},{2,1},{3,2},{4,7},{5,4},{6,5},{7,6},{8,11},{9,8},{10,9... | collective-permute-start | bytes 589832 | tf_op jit(solution)/shard_map/ppermute | solution.py:1152
  17.3 11.3 %collective-permute-start.5 = (bf16[128,768]{1,0:T(8,128)(2,1)S(1)}, bf16[128,768]{1,0:T(8,128)(2,1)S(1)}, u32[]{:S(2)}, u32[]{:S(2)}) collective-permute-start(bf16[128,768]{1,0:T(8,128)(2,1)S(1)} %collective-permute-done.4.rest_1_), channel_id=1, source_target_pairs={{0,16},{4,12},{8,24},{12,4},{16,0},{20,28},{24,8},{28,20},{1,17},{... | collective-permute-start | bytes 589832 | tf_op jit(solution)/shard_map/ppermute | solution.py:1148
  28.6 96.2 %all-gather.7.cloned.1.call-start = ((), (), s32[]{:S(2)}) async-start(), calls=%async_computation.5 | async-start | bytes 1310720 | tf_op jit(solution)/shard_map/all_gather | solution.py:1306
  28.6 15.4 %collective-permute-start.6 = (bf16[3,128,768]{2,1,0:T(8,128)(2,1)S(1)}, bf16[3,128,768]{2,1,0:T(8,128)(2,1)S(1)}, u32[]{:S(2)}, u32[]{:S(2)}) collective-permute-start(bf16[3,128,768]{2,1,0:T(8,128)(2,1)S(1)} %pad_maximum_fusion.rest_8_), channel_id=1, source_target_pairs={{0,8},{4,20},{8,0},{12,28},{16,24},{20,4},{24,16},{28,12},{1,9},{5... | collective-permute-start | bytes 1769480 | tf_op jit(solution)/shard_map/ppermute | solution.py:1148
  29.2 14.9 %collective-permute-start.7 = (bf16[3,128,768]{2,1,0:T(8,128)(2,1)S(1)}, bf16[3,128,768]{2,1,0:T(8,128)(2,1)S(1)}, u32[]{:S(2)}, u32[]{:S(2)}) collective-permute-start(bf16[3,128,768]{2,1,0:T(8,128)(2,1)S(1)} %pad_maximum_fusion.rest_8_), channel_id=1, source_target_pairs={{0,16},{4,12},{8,24},{12,4},{16,0},{20,28},{24,8},{28,20},{1,17},{... | collective-permute-start | bytes 1769480 | tf_op jit(solution)/shard_map/ppermute | solution.py:1148
  44.1 10.0 %collective-permute-start.8 = (bf16[3,128,768]{2,1,0:T(8,128)(2,1)S(1)}, bf16[3,128,768]{2,1,0:T(8,128)(2,1)}, u32[]{:S(2)}, u32[]{:S(2)}) collective-permute-start(bf16[3,128,768]{2,1,0:T(8,128)(2,1)S(1)} %collective-permute-done.6.rest_9_), channel_id=1, source_target_pairs={{0,16},{4,12},{8,24},{12,4},{16,0},{20,28},{24,8},{28,20},{1,17},{... | collective-permute-start | bytes 1769480 | tf_op jit(solution)/shard_map/ppermute | solution.py:1148
  45.3 8.9 %collective-permute-start.10 = (bf16[128,768]{1,0:T(8,128)(2,1)S(1)}, bf16[128,768]{1,0:T(8,128)(2,1)S(1)}, u32[]{:S(2)}, u32[]{:S(2)}) collective-permute-start(bf16[128,768]{1,0:T(8,128)(2,1)S(1)} %collective-permute-done.4.rest_1_), channel_id=1, source_target_pairs={{0,4},{4,0},{8,12},{12,8},{16,20},{20,16},{24,28},{28,24},{1,5},{5... | collective-permute-start | bytes 589832 | tf_op jit(solution)/shard_map/ppermute | solution.py:1148
  45.8 18.7 %collective-permute-start.13 = (bf16[3,128,768]{2,1,0:T(8,128)(2,1)S(1)}, bf16[3,128,768]{2,1,0:T(8,128)(2,1)}, u32[]{:S(2)}, u32[]{:S(2)}) collective-permute-start(bf16[3,128,768]{2,1,0:T(8,128)(2,1)S(1)} %pad_maximum_fusion.rest_8_), channel_id=1, source_target_pairs={{0,4},{4,0},{8,12},{12,8},{16,20},{20,16},{24,28},{28,24},{1,5},{5... | collective-permute-start | bytes 1769480 | tf_op jit(solution)/shard_map/ppermute | solution.py:1148
  45.8 20.2 %collective-permute-start.14 = (bf16[3,128,768]{2,1,0:T(8,128)(2,1)S(1)}, bf16[3,128,768]{2,1,0:T(8,128)(2,1)}, u32[]{:S(2)}, u32[]{:S(2)}) collective-permute-start(bf16[3,128,768]{2,1,0:T(8,128)(2,1)S(1)} %collective-permute-done.6.rest_9_), channel_id=1, source_target_pairs={{0,4},{4,0},{8,12},{12,8},{16,20},{20,16},{24,28},{28,24},{1,5},{5... | collective-permute-start | bytes 1769480 | tf_op jit(solution)/shard_map/ppermute | solution.py:1148
  47.2 18.8 %collective-permute-start.15 = (bf16[3,128,768]{2,1,0:T(8,128)(2,1)S(1)}, bf16[3,128,768]{2,1,0:T(8,128)(2,1)}, u32[]{:S(2)}, u32[]{:S(2)}) collective-permute-start(bf16[3,128,768]{2,1,0:T(8,128)(2,1)S(1)} %collective-permute-done.7.rest_10_), channel_id=1, source_target_pairs={{0,4},{4,0},{8,12},{12,8},{16,20},{20,16},{24,28},{28,24},{1,5},{5... | collective-permute-start | bytes 1769480 | tf_op jit(solution)/shard_map/ppermute | solution.py:1148
  54.1 11.8 %collective-permute-start.16 = (bf16[3,128,768]{2,1,0:T(8,128)(2,1)}, bf16[3,128,768]{2,1,0:T(8,128)(2,1)}, u32[]{:S(2)}, u32[]{:S(2)}) collective-permute-start(bf16[3,128,768]{2,1,0:T(8,128)(2,1)} %collective-permute-done.8.rest_11_), channel_id=1, source_target_pairs={{0,4},{4,0},{8,12},{12,8},{16,20},{20,16},{24,28},{28,24},{1,5},{5... | collective-permute-start | bytes 1769480 | tf_op jit(solution)/shard_map/ppermute | solution.py:1148
  62.9 31.3 %collective-permute-start.17 = (bf16[4,128,1280]{2,1,0:T(8,128)(2,1)}, bf16[4,128,1280]{2,1,0:T(8,128)(2,1)S(1)}, u32[]{:S(2)}, u32[]{:S(2)}) collective-permute-start(bf16[4,128,1280]{2,1,0:T(8,128)(2,1)} %bitcast.87), channel_id=1, source_target_pairs={{0,8},{4,20},{8,0},{12,28},{16,24},{20,4},{24,16},{28,12},{1,9},{5... | collective-permute-start | bytes 3932168 | tf_op jit(solution)/shard_map/ppermute | solution.py:1148
  64.5 29.8 %collective-permute-start.18 = (bf16[4,128,1280]{2,1,0:T(8,128)(2,1)}, bf16[4,128,1280]{2,1,0:T(8,128)(2,1)}, u32[]{:S(2)}, u32[]{:S(2)}) collective-permute-start(bf16[4,128,1280]{2,1,0:T(8,128)(2,1)} %bitcast.88), channel_id=1, source_target_pairs={{0,16},{4,12},{8,24},{12,4},{16,0},{20,28},{24,8},{28,20},{1,17},{... | collective-permute-start | bytes 3932168 | tf_op jit(solution)/shard_map/ppermute | solution.py:1148
  92.4 20.2 %collective-permute-start.20 = (bf16[4,128,1280]{2,1,0:T(8,128)(2,1)S(1)}, bf16[4,128,1280]{2,1,0:T(8,128)(2,1)}, u32[]{:S(2)}, u32[]{:S(2)}) collective-permute-start(bf16[4,128,1280]{2,1,0:T(8,128)(2,1)S(1)} %bitcast.94), channel_id=1, source_target_pairs={{0,4},{4,0},{8,12},{12,8},{16,20},{20,16},{24,28},{28,24},{1,5},{5... | collective-permute-start | bytes 3932168 | tf_op jit(solution)/shard_map/ppermute | solution.py:1148
  92.5 177.2 %reduce-scatter.3.cloned.1.call-start = ((), (), s32[]{:S(2)}) async-start(), calls=%async_computation.2 | async-start | bytes 9437184 | tf_op jit(solution)/shard_map/reduce_scatter | solution.py:1355
  94.3 17.7 %collective-permute-start.19 = (bf16[4,128,1280]{2,1,0:T(8,128)(2,1)S(1)}, bf16[4,128,1280]{2,1,0:T(8,128)(2,1)}, u32[]{:S(2)}, u32[]{:S(2)}) collective-permute-start(bf16[4,128,1280]{2,1,0:T(8,128)(2,1)S(1)} %collective-permute-done.17.rest_1_.rest_2_.rest_10_), channel_id=1, source_target_pairs={{0,16},{4,12},{8,24},{12,4},{16,0},{20,28},{24,8},{28,20},{1,17},{... | collective-permute-start | bytes 3932168 | tf_op jit(solution)/shard_map/ppermute | solution.py:1148
  94.8 17.8 %collective-permute-start.21 = (bf16[4,128,1280]{2,1,0:T(8,128)(2,1)S(1)}, bf16[4,128,1280]{2,1,0:T(8,128)(2,1)}, u32[]{:S(2)}, u32[]{:S(2)}) collective-permute-start(bf16[4,128,1280]{2,1,0:T(8,128)(2,1)S(1)} %collective-permute-done.17.rest_1_.rest_2_.rest_10_), channel_id=1, source_target_pairs={{0,4},{4,0},{8,12},{12,8},{16,20},{20,16},{24,28},{28,24},{1,5},{5... | collective-permute-start | bytes 3932168 | tf_op jit(solution)/shard_map/ppermute | solution.py:1148
  95.0 17.7 %collective-permute-start.22 = (bf16[4,128,1280]{2,1,0:T(8,128)(2,1)}, bf16[4,128,1280]{2,1,0:T(8,128)(2,1)}, u32[]{:S(2)}, u32[]{:S(2)}) collective-permute-start(bf16[4,128,1280]{2,1,0:T(8,128)(2,1)} %collective-permute-done.18.rest_2_.rest_3_.rest_11_), channel_id=1, source_target_pairs={{0,4},{4,0},{8,12},{12,8},{16,20},{20,16},{24,28},{28,24},{1,5},{5... | collective-permute-start | bytes 3932168 | tf_op jit(solution)/shard_map/ppermute | solution.py:1148
  124.8 25.8 %collective-permute-start.24 = (bf16[4,512,256]{2,1,0:T(8,128)(2,1)}, bf16[4,512,256]{2,1,0:T(8,128)(2,1)S(1)}, u32[]{:S(2)}, u32[]{:S(2)}) collective-permute-start(bf16[4,512,256]{2,1,0:T(8,128)(2,1)} %bitcast.105), channel_id=1, source_target_pairs={{0,8},{4,20},{8,0},{12,28},{16,24},{20,4},{24,16},{28,12},{1,9},{5... | collective-permute-start | bytes 3145736 | tf_op jit(solution)/shard_map/ppermute | solution.py:1148
  126.4 24.2 %collective-permute-start.25 = (bf16[4,512,256]{2,1,0:T(8,128)(2,1)}, bf16[4,512,256]{2,1,0:T(8,128)(2,1)S(1)}, u32[]{:S(2)}, u32[]{:S(2)}) collective-permute-start(bf16[4,512,256]{2,1,0:T(8,128)(2,1)} %bitcast.106), channel_id=1, source_target_pairs={{0,16},{4,12},{8,24},{12,4},{16,0},{20,28},{24,8},{28,20},{1,17},{... | collective-permute-start | bytes 3145736 | tf_op jit(solution)/shard_map/ppermute | solution.py:1148
  126.9 45.2 %collective-permute-start.27 = (bf16[4,512,256]{2,1,0:T(8,128)(2,1)}, bf16[4,512,256]{2,1,0:T(8,128)(2,1)S(1)}, u32[]{:S(2)}, u32[]{:S(2)}) collective-permute-start(bf16[4,512,256]{2,1,0:T(8,128)(2,1)} %bitcast.107), channel_id=1, source_target_pairs={{0,4},{4,0},{8,12},{12,8},{16,20},{20,16},{24,28},{28,24},{1,5},{5... | collective-permute-start | bytes 3145736 | tf_op jit(solution)/shard_map/ppermute | solution.py:1148
  150.6 21.3 %collective-permute-start.26 = (bf16[4,512,256]{2,1,0:T(8,128)(2,1)S(1)}, bf16[4,512,256]{2,1,0:T(8,128)(2,1)}, u32[]{:S(2)}, u32[]{:S(2)}) collective-permute-start(bf16[4,512,256]{2,1,0:T(8,128)(2,1)S(1)} %collective-permute-done.24.rest_18_.rest_1_), channel_id=1, source_target_pairs={{0,16},{4,12},{8,24},{12,4},{16,0},{20,28},{24,8},{28,20},{1,17},{... | collective-permute-start | bytes 3145736 | tf_op jit(solution)/shard_map/ppermute | solution.py:1148
  151.5 20.6 %collective-permute-start.28 = (bf16[4,512,256]{2,1,0:T(8,128)(2,1)S(1)}, bf16[4,512,256]{2,1,0:T(8,128)(2,1)}, u32[]{:S(2)}, u32[]{:S(2)}) collective-permute-start(bf16[4,512,256]{2,1,0:T(8,128)(2,1)S(1)} %collective-permute-done.24.rest_18_.rest_1_), channel_id=1, source_target_pairs={{0,4},{4,0},{8,12},{12,8},{16,20},{20,16},{24,28},{28,24},{1,5},{5... | collective-permute-start | bytes 3145736 | tf_op jit(solution)/shard_map/ppermute | solution.py:1148
  151.5 20.6 %collective-permute-start.29 = (bf16[4,512,256]{2,1,0:T(8,128)(2,1)S(1)}, bf16[4,512,256]{2,1,0:T(8,128)(2,1)}, u32[]{:S(2)}, u32[]{:S(2)}) collective-permute-start(bf16[4,512,256]{2,1,0:T(8,128)(2,1)S(1)} %collective-permute-done.25.rest_19_.rest_2_), channel_id=1, source_target_pairs={{0,4},{4,0},{8,12},{12,8},{16,20},{20,16},{24,28},{28,24},{1,5},{5... | collective-permute-start | bytes 3145736 | tf_op jit(solution)/shard_map/ppermute | solution.py:1148
  172.0 153.5 %reduce-scatter.5.cloned.1.call-start = ((), (), s32[]{:S(2)}) async-start(), calls=%async_computation.3 | async-start | bytes 1310720 | tf_op jit(solution)/shard_map/reduce_scatter | solution.py:1391
  222.7 10.4 %collective-permute-start.31 = (bf16[4,4,128,1280]{3,2,1,0:T(8,128)(2,1)}, bf16[4,4,128,1280]{3,2,1,0:T(8,128)(2,1)}, u32[]{:S(2)}, u32[]{:S(2)}) collective-permute-start(bf16[4,4,128,1280]{3,2,1,0:T(8,128)(2,1)} %get-tuple-element.145), channel_id=1, source_target_pairs={{0,4},{4,0},{8,12},{12,8},{16,20},{20,16},{24,28},{28,24},{1,5},{5... | collective-permute-start | bytes 15728648 | tf_op jit(solution)/shard_map/ppermute | solution.py:1148
  236.3 33.3 %collective-permute-start.32 = (bf16[2,4,128,1280]{3,2,1,0:T(8,128)(2,1)S(1)}, bf16[2,4,128,1280]{3,2,1,0:T(8,128)(2,1)}, u32[]{:S(2)}, u32[]{:S(2)}) collective-permute-start(bf16[2,4,128,1280]{3,2,1,0:T(8,128)(2,1)S(1)} %add_convert_fusion), channel_id=1, source_target_pairs={{0,16},{4,12},{8,24},{12,4},{16,0},{20,28},{24,8},{28,20},{1,17},{... | collective-permute-start | bytes 7864328 | tf_op jit(solution)/shard_map/ppermute | solution.py:1148
  272.3 17.7 %collective-permute-start.34 = (bf16[4,128,1280]{2,1,0:T(8,128)(2,1)S(1)}, bf16[4,128,1280]{2,1,0:T(8,128)(2,1)S(1)}, u32[]{:S(2)}, u32[]{:S(2)}) collective-permute-start(bf16[4,128,1280]{2,1,0:T(8,128)(2,1)S(1)} %fusion), channel_id=1, source_target_pairs={{0,8},{4,20},{8,0},{12,28},{16,24},{20,4},{24,16},{28,12},{1,9},{5... | collective-permute-start | bytes 3932168 | tf_op jit(solution)/shard_map/ppermute | solution.py:1148
  286.6 14.7 %collective-permute-start.33 = (bf16[4,4,128,768]{3,2,1,0:T(8,128)(2,1)}, bf16[4,4,128,768]{3,2,1,0:T(8,128)(2,1)}, u32[]{:S(2)}, u32[]{:S(2)}) collective-permute-start(bf16[4,4,128,768]{3,2,1,0:T(8,128)(2,1)} %get-tuple-element.154), channel_id=1, source_target_pairs={{0,4},{4,0},{8,12},{12,8},{16,20},{20,16},{24,28},{28,24},{1,5},{5... | collective-permute-start | bytes 9437192 | tf_op jit(solution)/shard_map/ppermute | solution.py:1148
  296.0 32.1 %collective-permute-start.37 = (bf16[128,1280]{1,0:T(8,128)(2,1)}, bf16[128,1280]{1,0:T(8,128)(2,1)S(1)}, u32[]{:S(2)}, u32[]{:S(2)}) collective-permute-start(bf16[128,1280]{1,0:T(8,128)(2,1)} %get-tuple-element.158), channel_id=1, source_target_pairs={{0,1},{1,2},{2,3},{3,0},{4,5},{5,6},{6,7},{7,4},{8,9},{9,10},{10,1... | collective-permute-start | bytes 983048 | tf_op jit(solution)/shard_map/ppermute | solution.py:1152
  297.5 33.0 %collective-permute-start.38 = (bf16[128,1280]{1,0:T(8,128)(2,1)}, bf16[128,1280]{1,0:T(8,128)(2,1)}, u32[]{:S(2)}, u32[]{:S(2)}) collective-permute-start(bf16[128,1280]{1,0:T(8,128)(2,1)} %get-tuple-element.159), channel_id=1, source_target_pairs={{0,2},{1,3},{2,0},{3,1},{4,6},{5,7},{6,4},{7,5},{8,10},{9,11},{10,... | collective-permute-start | bytes 983048 | tf_op jit(solution)/shard_map/ppermute | solution.py:1152
  299.9 48.9 %collective-permute-start.39 = (bf16[128,1280]{1,0:T(8,128)(2,1)}, bf16[128,1280]{1,0:T(8,128)(2,1)}, u32[]{:S(2)}, u32[]{:S(2)}) collective-permute-start(bf16[128,1280]{1,0:T(8,128)(2,1)} %get-tuple-element.160), channel_id=1, source_target_pairs={{0,3},{1,0},{2,1},{3,2},{4,7},{5,4},{6,5},{7,6},{8,11},{9,8},{10,9... | collective-permute-start | bytes 983048 | tf_op jit(solution)/shard_map/ppermute | solution.py:1152
  304.2 20.7 %collective-permute-start.35 = (bf16[2,4,128,768]{3,2,1,0:T(8,128)(2,1)}, bf16[2,4,128,768]{3,2,1,0:T(8,128)(2,1)}, u32[]{:S(2)}, u32[]{:S(2)}) collective-permute-start(bf16[2,4,128,768]{3,2,1,0:T(8,128)(2,1)} %add_convert_fusion.1), channel_id=1, source_target_pairs={{0,16},{4,12},{8,24},{12,4},{16,0},{20,28},{24,8},{28,20},{1,17},{... | collective-permute-start | bytes 4718600 | tf_op jit(solution)/shard_map/ppermute | solution.py:1148
  320.9 27.9 %collective-permute-start.40 = (f32[96,128]{1,0:T(8,128)}, f32[96,128]{1,0:T(8,128)}, u32[]{:S(2)}, u32[]{:S(2)}) collective-permute-start(f32[96,128]{1,0:T(8,128)} %get-tuple-element.176), channel_id=1, source_target_pairs={{0,1},{1,0},{2,3},{3,2},{4,5},{5,4},{6,7},{7,6},{8,9},{9,8},{10,11... | collective-permute-start | bytes 147464 | tf_op jit(solution)/shard_map/ppermute | solution.py:1244
  325.0 23.8 %collective-permute-start.41 = (f32[96,128]{1,0:T(8,128)}, f32[96,128]{1,0:T(8,128)}, u32[]{:S(2)}, u32[]{:S(2)}) collective-permute-start(f32[96,128]{1,0:T(8,128)} %get-tuple-element.176), channel_id=1, source_target_pairs={{0,2},{1,3},{2,0},{3,1},{4,6},{5,7},{6,4},{7,5},{8,10},{9,11},{10,... | collective-permute-start | bytes 147464 | tf_op jit(solution)/shard_map/ppermute | solution.py:1244
  328.1 20.7 %collective-permute-start.42 = (f32[96,128]{1,0:T(8,128)S(1)}, f32[96,128]{1,0:T(8,128)S(1)}, u32[]{:S(2)}, u32[]{:S(2)}) collective-permute-start(f32[96,128]{1,0:T(8,128)S(1)} %copy-done.14), channel_id=1, source_target_pairs={{0,3},{1,2},{2,1},{3,0},{4,7},{5,6},{6,5},{7,4},{8,11},{9,10},{10,... | collective-permute-start | bytes 147464 | tf_op jit(solution)/shard_map/ppermute | solution.py:1244
  330.5 18.3 %collective-permute-start.36 = (bf16[4,128,768]{2,1,0:T(8,128)(2,1)}, bf16[4,128,768]{2,1,0:T(8,128)(2,1)}, u32[]{:S(2)}, u32[]{:S(2)}) collective-permute-start(bf16[4,128,768]{2,1,0:T(8,128)(2,1)} %fusion.1), channel_id=1, source_target_pairs={{0,8},{4,20},{8,0},{12,28},{16,24},{20,4},{24,16},{28,12},{1,9},{5... | collective-permute-start | bytes 2359304 | tf_op jit(solution)/shard_map/ppermute | solution.py:1148
  353.0 9.6 %collective-permute-start.50 = (bf16[128,768]{1,0:T(8,128)(2,1)S(1)}, bf16[128,768]{1,0:T(8,128)(2,1)S(1)}, u32[]{:S(2)}, u32[]{:S(2)}) collective-permute-start(bf16[128,768]{1,0:T(8,128)(2,1)S(1)} %get-tuple-element.185), channel_id=1, source_target_pairs={{0,1},{1,2},{2,3},{3,0},{4,5},{5,6},{6,7},{7,4},{8,9},{9,10},{10,1... | collective-permute-start | bytes 589832 | tf_op jit(solution)/shard_map/ppermute | solution.py:1152
  353.6 13.3 %collective-permute-start.51 = (bf16[128,768]{1,0:T(8,128)(2,1)S(1)}, bf16[128,768]{1,0:T(8,128)(2,1)S(1)}, u32[]{:S(2)}, u32[]{:S(2)}) collective-permute-start(bf16[128,768]{1,0:T(8,128)(2,1)S(1)} %get-tuple-element.186), channel_id=1, source_target_pairs={{0,2},{1,3},{2,0},{3,1},{4,6},{5,7},{6,4},{7,5},{8,10},{9,11},{10,... | collective-permute-start | bytes 589832 | tf_op jit(solution)/shard_map/ppermute | solution.py:1152
  355.1 12.7 %collective-permute-start.52 = (bf16[128,768]{1,0:T(8,128)(2,1)S(1)}, bf16[128,768]{1,0:T(8,128)(2,1)S(1)}, u32[]{:S(2)}, u32[]{:S(2)}) collective-permute-start(bf16[128,768]{1,0:T(8,128)(2,1)S(1)} %get-tuple-element.187), channel_id=1, source_target_pairs={{0,3},{1,0},{2,1},{3,2},{4,7},{5,4},{6,5},{7,6},{8,11},{9,8},{10,9... | collective-permute-start | bytes 589832 | tf_op jit(solution)/shard_map/ppermute | solution.py:1152
  359.8 8.8 %collective-permute-start.45 = (f32[96,128]{1,0:T(8,128)S(1)}, f32[96,128]{1,0:T(8,128)S(1)}, u32[]{:S(2)}, u32[]{:S(2)}) collective-permute-start(f32[96,128]{1,0:T(8,128)S(1)} %add_add_fusion.refs_0_), channel_id=1, source_target_pairs={{0,12},{4,8},{8,4},{12,0},{16,28},{20,24},{24,20},{28,16},{1,13},{... | collective-permute-start | bytes 147464 | tf_op jit(solution)/shard_map/ppermute | solution.py:1244
  361.1 7.5 %collective-permute-start.46 = (f32[96,128]{1,0:T(8,128)S(1)}, f32[96,128]{1,0:T(8,128)S(1)}, u32[]{:S(2)}, u32[]{:S(2)}) collective-permute-start(f32[96,128]{1,0:T(8,128)S(1)} %add_add_fusion.refs_0_), channel_id=1, source_target_pairs={{0,16},{4,20},{8,24},{12,28},{16,0},{20,4},{24,8},{28,12},{1,17},{... | collective-permute-start | bytes 147464 | tf_op jit(solution)/shard_map/ppermute | solution.py:1244
  362.6 6.0 %collective-permute-start.47 = (f32[96,128]{1,0:T(8,128)S(1)}, f32[96,128]{1,0:T(8,128)S(1)}, u32[]{:S(2)}, u32[]{:S(2)}) collective-permute-start(f32[96,128]{1,0:T(8,128)S(1)} %add_add_fusion.refs_0_), channel_id=1, source_target_pairs={{0,20},{4,16},{8,28},{12,24},{16,4},{20,0},{24,12},{28,8},{1,21},{... | collective-permute-start | bytes 147464 | tf_op jit(solution)/shard_map/ppermute | solution.py:1244
  (36 other events, 432.6 us)
Sparse Core Ops, SparseCore 0:
  28.7 34.1 all-gather.4
  92.6 25.7 all-gather.6
  172.1 71.9 reduce-scatter.2
  273.9 26.2 reduce-scatter.4
where the time goes:
time: 390 us; the launch traced here: 383 us
  Pallas kernels  226 us (58%)
  waiting for transfers between devices  71.2 us (18%)
  starting transfers between devices  44.1 us (11%)
  other arithmetic  19.6 us (5%)
  between operations  15.2 us (4%)
  local copies, waits for them, and re-layouts  7.43 us (2%)
    ppermute x34, waiting for transfers between devices, swap(): return lax.ppermute(value, 'dp', [(d, d ^ flips[d & 1]) for d in range(8)])  50.6 us
    pallas_call x1, Pallas kernels, back_call(): pl.pallas_call(functools.partial(back_kernel, (len(out_pieces), len(up_pi...  47.8 us
    pallas_call x2, Pallas kernels, up_call(): pl.pallas_call(functools.partial(up_kernel, (len(up_pieces), len(earlier)...  39.6 us
    pallas_call x2, Pallas kernels, attention_back_call(): pl.pallas_call(functools.partial(attention_back_kernel, group, block), gr...  36.7 us
    pallas_call x2, Pallas kernels, attention_call(): pl.pallas_call(functools.partial(attention_kernel, group, block), grid=(s...  27 us
    ppermute x34, starting transfers between devices, swap(): return lax.ppermute(value, 'dp', [(d, d ^ flips[d & 1]) for d in range(8)])  21.8 us
    pallas_call x1, Pallas kernels, down_call(): pl.pallas_call(functools.partial(down_kernel, len(pieces), base, base + s...  16.8 us
    pallas_call x1, Pallas kernels, first_call(): pl.pallas_call(functools.partial(first_kernel, len(pieces)), grid_spec=gr...  16.1 us
  transfers between devices with their start and end apart: 57, of which 19 were waited for; matrix products, arithmetic and copies ran while one was open for 4% of the time, Pallas kernels for 58%

commit v1 on v0

--- a/solution.py
+++ b/solution.py
@@ -314,14 +314,14 @@
             jax.ShapeDtypeStruct((3 * model, extent), BF),
         ],
         compiler_params=params(),
-        cost_estimate=estimate(6 * extent * model * model, 16e6),
+        cost_estimate=estimate(1e6, 1e4),
         name="project",
     )(tab, tokens, gain, shift, bias, *pieces)
 
 
-def causal_bias(block):
-    key = lax.broadcasted_iota(jnp.int32, (block, block), 0)
-    query = lax.broadcasted_iota(jnp.int32, (block, block), 1)
+def causal_bias(keys, queries):
+    key = lax.broadcasted_iota(jnp.int32, (keys, queries), 0)
+    query = lax.broadcasted_iota(jnp.int32, (keys, queries), 1)
     return jnp.where(key <= query, 0.0, MASKED)
 
 
@@ -337,9 +337,11 @@
     mixture, totals, keys, queries, causal = rest[-5:]
     extent = query.shape[1]
 
+    half = block // 2
+
     @pl.when(pl.program_id(0) == 0)
     def _():
-        causal[...] = causal_bias(block)
+        causal[...] = causal_bias(half, block)
 
     key_rows, query_rows = extend_rows(lengths[0], extent)
     for head in range(group):
@@ -351,27 +353,36 @@
     for head in range(group):
         part = pl.ds(HEAD * head, HEAD)
         for tile in range(extent // block):
-            place = pl.ds(tile * block, block)
+            first = tile * block
+            place = pl.ds(first, block)
+            later = pl.ds(first + half, half)
+            spans = [pl.ds(other * block, block) for other in range(tile)] + [pl.ds(first, half)]
             own = queries[head, :, place]
-            scores = []
-            for other in range(tile + 1):
-                score = dot(keys[head, :, pl.ds(other * block, block)], own, 0, 0)
-                scores.append(score + causal[...] if other == tile else score)
+            scores = [dot(keys[head, :, span], own, 0, 0) for span in spans]
+            scores[-1] = scores[-1] + causal[...]
+            corner = dot(keys[head, :, later], queries[head, :, later], 0, 0) + causal[:, :half]
             highest = scores[0].max(0, keepdims=True)
             for score in scores[1:]:
                 highest = jnp.maximum(highest, score.max(0, keepdims=True))
+            corner_highest = jnp.maximum(highest[:, half:], corner.max(0, keepdims=True))
+            highest = jnp.concatenate([highest[:, :half], corner_highest], axis=1)
             offset = highest * (SCALE * LOG2E)
+            weight = jnp.exp2(corner * (SCALE * LOG2E) - offset[:, half:])
+            corner_summed = weight.sum(0, keepdims=True)
+            corner_total = dot(value[part, later], weight.astype(BF), 1, 0)
             summed = jnp.zeros((1, block), F32)
             total = jnp.zeros((HEAD, block), F32)
-            for other, score in enumerate(scores):
+            for span, score in zip(spans, scores):
                 weight = jnp.exp2(score * (SCALE * LOG2E) - offset)
                 summed = summed + weight.sum(0, keepdims=True)
-                total = total + dot(value[part, pl.ds(other * block, block)], weight.astype(BF), 1, 0)
+                total = total + dot(value[part, span], weight.astype(BF), 1, 0)
+            summed = jnp.concatenate([summed[:, :half], summed[:, half:] + corner_summed], axis=1)
+            total = jnp.concatenate([total[:, :half], total[:, half:] + corner_total], axis=1)
             mixture[part, place] = (total * (1.0 / summed)).astype(BF)
             totals[0, pl.ds(head, 1), place] = offset + jnp.log2(summed)
 
 
-def attention_call(lengths, project, part_of=(0, 1), earlier=()):
+def attention_call(lengths, project, part_of=(0, 1), earlier=(), weight=0.001):
     extent = project.shape[1]
     group, block = 2, min(512, extent)
     size, groups = HEAD * group, HEADS // group
@@ -395,10 +406,10 @@
         scratch_shapes=[
             pltpu.VMEM((group, HEAD + 16, extent), BF),
             pltpu.VMEM((group, HEAD + 16, extent), BF),
-            pltpu.VMEM((block, block), F32),
+            pltpu.VMEM((block // 2, block), F32),
         ],
         compiler_params=params(),
-        cost_estimate=estimate(16 * HEADS * pairs * HEAD / part_of[1], 8e6),
+        cost_estimate=estimate(weight * 16 * HEADS * pairs * HEAD / part_of[1], weight * 8e6),
         name="attention",
     )(lengths, project, project, project, *earlier)
 
@@ -480,10 +491,13 @@
     up_pieces, rest = rest[:count_up], rest[count_up + count_earlier :]
     active, slope = rest[:2]
     grads, rest = rest[2 : 2 + count_grad], rest[2 + count_grad :]
-    weight, staged, sems_up, sems_grad = rest
+    weight, staged, graded, sems_up, sems_grad, sem_in = rest
     step = pl.program_id(0)
     steps = pl.num_programs(0)
     extent = normed.shape[0]
+
+    def late():
+        return pltpu.make_async_copy(result, graded, sem_in)
 
     def fetch(index):
         slot = lax.rem(index, 2)
@@ -498,6 +512,7 @@
     @pl.when(step == 0)
     def _():
         start(fetch(step))
+        late().start()
 
     @pl.when(step + 1 < steps)
     def _():
@@ -515,12 +530,16 @@
 
     chunks(extent, ROWS, widen)
 
+    @pl.when(step == 0)
+    def _():
+        late().wait()
+
     @pl.when(step >= 2)
     def _():
         wait(send(step - 2))
 
     def weigh(columns, carry):
-        staged[now, columns, :] = dot(active[:, columns], result[...], 0, 0).astype(BF)
+        staged[now, columns, :] = dot(active[:, columns], graded[...], 0, 0).astype(BF)
         return carry
 
     chunks(TILE, ROWS, weigh)
@@ -532,7 +551,9 @@
         wait(send(step))
 
 
-def up_call(tab, normed, result, up_bias, up_pieces, spread, sizes, part_of=(0, 1), earlier=()):
+def up_call(
+    tab, normed, result, up_bias, up_pieces, spread, sizes, part_of=(0, 1), earlier=(), weight=1.0
+):
     extent, model = normed.shape
     hidden = 4 * model
     grads = gradient_shapes(spread, hidden, model, *sizes)
@@ -543,7 +564,7 @@
     return pl.pallas_call(
         functools.partial(up_kernel, (len(up_pieces), len(earlier), len(grads)), base),
         grid=(steps,),
-        in_specs=[SMEM, whole(extent, model), whole(extent, model)]
+        in_specs=[SMEM, whole(extent, model), ANY]
         + [pl.BlockSpec((1, TILE), lambda i: (0, base + i))]
         + [ANY] * (len(up_pieces) + len(earlier)),
         out_specs=[tile, tile] + [ANY] * len(grads),
@@ -556,11 +577,13 @@
         scratch_shapes=[
             pltpu.VMEM((2, model, TILE), BF),
             pltpu.VMEM((2, TILE, model), BF),
+            pltpu.VMEM((extent, model), BF),
             pltpu.SemaphoreType.DMA((2, 8)),
             pltpu.SemaphoreType.DMA((2, 8)),
+            pltpu.SemaphoreType.DMA,
         ],
         compiler_params=params(),
-        cost_estimate=estimate(16 * extent * model * model / part_of[1], 50e6, extent * hidden),
+        cost_estimate=estimate(weight * 16 * extent * model * model / part_of[1], weight * 50e6),
         name="up",
     )(tab, normed, result, up_bias, *up_pieces, *earlier)
 
@@ -604,10 +627,12 @@
 
     def fetch(index):
         slot = index % 2
-        copies = load_rows(down_pieces, tab, index, down.at[slot], sems_down.at[slot])
+        return load_rows(down_pieces, tab, index, down.at[slot], sems_down.at[slot])
+
+    def fetch_up(index):
+        slot = index % 2
         block = tab[T_PAIR + index]
-        copies += load_columns(up_pieces, tab, block, up.at[slot], sems_up.at[slot], TILE)
-        return copies
+        return load_columns(up_pieces, tab, block, up.at[slot], sems_up.at[slot], TILE)
 
     def send(index):
         slot = index % 2
@@ -644,6 +669,7 @@
         early(0).start()
         start(fetch(0))
         early(1).start()
+        start(fetch_up(0))
         early(0).wait()
         d_normed[...] = jnp.zeros_like(d_normed)
 
@@ -652,6 +678,7 @@
             start(late())
         if index + 1 < 4:
             start(fetch(index + 1))
+            start(fetch_up(index + 1))
         wait(fetch(index))
         if index >= 2:
             wait(send(index - 2))
@@ -676,8 +703,12 @@
         return carry
 
     chunks(model, ROWS, weigh)
+    def leave(index):
+        start(send(index))
+        wait(fetch_up(index))
+
     for index in range(4):
-        pl.when(step == index)(lambda index=index: start(send(index)))
+        pl.when(step == index)(functools.partial(leave, index))
 
     def widen(rows, carry):
         d_normed[rows, :] += dot(d_hidden[rows, :], up[now], 1, 1)
@@ -820,7 +851,7 @@
 
     @pl.when(pl.program_id(0) == 0)
     def _():
-        causal[...] = causal_bias(block)
+        causal[...] = causal_bias(block, block)
 
     key_rows, query_rows = extend_rows(lengths[0], extent)
     for head in range(group):
@@ -919,7 +950,8 @@
 
     chunks(model, ROWS, weigh)
     start(send(step))
-    bias_grad[...] = dot(jnp.ones((8, extent), BF), d_project[...], 1, 1)[:1, :]
+    sums = d_project[...].astype(F32).sum(1, keepdims=True)
+    bias_grad[...] = jnp.transpose(jnp.broadcast_to(sums, (width, 128)))[:1, :]
 
     @pl.when(step == steps - 1)
     def _():
@@ -1066,68 +1098,81 @@
     )(tab, d_project, frames, d_middle, gain, *pieces, *vectors)
 
 
-def down_kernel(count, base, ending, tab, active, middle, bias, *rest):
+def down_kernel(count, count_earlier, row, tab, active, middle, bias, *rest):
     pieces = rest[:count]
-    frames_out, weight, total, sems = rest[count:]
+    frames_out, weight, total, base, sems, sem_base = rest[count + count_earlier :]
     step = pl.program_id(0)
     steps = pl.num_programs(0)
+    extent = total.shape[0]
 
     def fetch(index):
-        slot = (index - base) % 2
+        slot = index % 2
         return load_rows(pieces, tab, index, weight.at[slot], sems.at[slot])
 
+    def late():
+        return pltpu.make_async_copy(middle.at[pl.ds(row * extent, extent), :], base, sem_base)
+
     def arrive(index):
-        if index == base:
+        if index == 0:
             start(fetch(index))
-        if index + 1 < ending:
+            late().start()
+        if index + 1 < 4:
             start(fetch(index + 1))
         wait(fetch(index))
 
-    for index in range(base, ending):
-        pl.when(step == index - base)(functools.partial(arrive, index))
-
-    @pl.when(step == 0)
-    def _():
-        total[...] = middle[...] + bias[...] if base == 0 else middle[...]
-
-    def widen(rows, carry):
-        total[rows, :] += dot(active[rows, :], weight[lax.rem(step, 2)], 1, 0)
-        return carry
-
-    chunks(total.shape[0], ROWS, widen)
+    for index in range(4):
+        pl.when(step == index)(functools.partial(arrive, index))
+    now = lax.rem(step, 2)
+
+    @pl.when(step < steps - 1)
+    def _():
+        def widen(rows, carry):
+            before = jnp.where(step == 0, 0.0, total[rows, :])
+            total[rows, :] = before + dot(active[rows, :], weight[now], 1, 0)
+            return carry
+
+        chunks(extent, ROWS, widen)
 
     @pl.when(step == steps - 1)
     def _():
-        frames_out[...] = total[...].astype(frames_out.dtype)
-
-
-def down_call(tab, active, middle, bias, pieces, part_of=(0, 1)):
+        late().wait()
+
+        def finish(rows, carry):
+            result = total[rows, :] + dot(active[rows, :], weight[now], 1, 0)
+            frames_out[rows, :] = (result + (base[rows, :] + bias[...])).astype(BF)
+            return carry
+
+        chunks(extent, ROWS, finish)
+
+
+def down_call(tab, active, middle, bias, pieces, part_of=(0, 1), earlier=()):
     extent, hidden = active.shape
     model = middle.shape[1]
-    steps = hidden // TILE // part_of[1]
-    base = steps * part_of[0]
-    last = part_of[0] + 1 == part_of[1]
+    row, size = part_of[0], extent // part_of[1]
     grid = pltpu.PrefetchScalarGridSpec(
         num_scalar_prefetch=1,
-        grid=(steps,),
-        in_specs=[pl.BlockSpec((extent, TILE), lambda i, tab: (0, tab[T_PAIR + base + i]))]
-        + [whole(extent, model), whole(1, model)]
-        + [ANY] * len(pieces),
-        out_specs=whole(extent, model),
+        grid=(hidden // TILE,),
+        in_specs=[pl.BlockSpec((size, TILE), lambda i, tab: (row, tab[T_PAIR + i]))]
+        + [ANY, whole(1, model)]
+        + [ANY] * (len(pieces) + len(earlier)),
+        out_specs=pl.BlockSpec((size, model), lambda i, tab: (row, 0)),
         scratch_shapes=[
             pltpu.VMEM((2, TILE, model), BF),
-            pltpu.VMEM((extent, model), F32),
+            pltpu.VMEM((size, model), F32),
+            pltpu.VMEM((size, model), F32),
             pltpu.SemaphoreType.DMA((2, 8)),
+            pltpu.SemaphoreType.DMA,
         ],
     )
     return pl.pallas_call(
-        functools.partial(down_kernel, len(pieces), base, base + steps),
+        functools.partial(down_kernel, len(pieces), len(earlier), row),
         grid_spec=grid,
-        out_shape=jax.ShapeDtypeStruct((extent, model), BF if last else F32),
+        out_shape=jax.ShapeDtypeStruct((extent, model), BF),
+        input_output_aliases={4 + len(pieces): 0} if earlier else {},
         compiler_params=params(),
-        cost_estimate=estimate(8 * extent * model * model, 24e6),
+        cost_estimate=estimate(8 * size * model * model, 24e6),
         name="down",
-    )(tab, active, middle, bias, *pieces)
+    )(tab, active, middle, bias, *pieces, *earlier)
 
 
 def gather_plain(weight):
@@ -1287,6 +1332,7 @@
         down_pieces = gather_plain(down_weight)
     else:
         others = [shift(attend_weight, amount) for amount in (1, 2, 3)]
+        up_block = jnp.concatenate([up_weight, output_weight], axis=1)
         near, far = swap(attend_weight, NEAR), swap(attend_weight, FAR)
         others = jnp.stack(others)
         far, near = after((far, near), near, far)
@@ -1295,13 +1341,13 @@
         attend_pieces += [swap(piece, CORE) for piece in attend_pieces]
         others = after(others, diagonal)
         near, far = swap(others, NEAR), swap(others, FAR)
-        up_block = after(jnp.concatenate([up_weight, output_weight], axis=1), others)
+        up_block = after(up_block, others)
         up_own = lax.all_gather(up_block, "inner")
         near, far = after((near, far), near, far)
         diagonal = swap(near, FAR)
         others = [others, near, far, diagonal]
         attend_pieces += others + [swap(piece, CORE) for piece in others]
-        up_own = after(up_own, diagonal)
+        up_own = after(up_own, *attend_pieces)
         up_near, up_far = swap(up_own, NEAR), swap(up_own, FAR)
         down_own = lax.all_gather(after(down_weight, up_own), "inner")
     bias_row = jnp.concatenate([attend_bias[0], jnp.zeros_like(attend_bias[0]), attend_bias[1]])
@@ -1314,7 +1360,7 @@
         up_diagonal = swap(up_near, FAR)
         ahead = [swap(piece, CORE) for piece in (after(up_own, totals), up_near, up_far)]
         mixture, totals = attention_call(
-            lengths, after(project, up_near, up_far), (1, 2), (mixture, totals)
+            lengths, after(project, up_near, up_far, down_own), (1, 2), (mixture, totals)
         )
         up_pieces = [up_own, up_near, up_far, up_diagonal]
         up_pieces += ahead + [swap(after(up_diagonal, totals), CORE)]
@@ -1322,14 +1368,21 @@
     else:
         mixture, totals = attention_call(lengths, project)
     vectors = (row(output_bias), row(second_gain), row(second_shift))
+    if spread:
+        down_near, down_far = swap(down_own, NEAR), swap(down_own, FAR)
     middle, normed_two, d_result, grad_down_bias = out_call(
         tab_plain, lengths, mixture, frames, upstream, vectors, out_pieces
     )
     if spread:
-        down_own = after(down_own, normed_two)
-        down_near, down_far = swap(down_own, NEAR), swap(down_own, FAR)
         *halves, half_grad = up_call(
-            tab_plain, normed_two, d_result, row(up_bias), up_pieces, False, sizes, (0, 2)
+            tab_plain,
+            normed_two,
+            d_result,
+            row(up_bias),
+            up_pieces,
+            False,
+            sizes,
+            (0, 2),
         )
         down_near, down_far = after((down_near, down_far), halves)
         down_diagonal = swap(down_near, FAR)

time: 390 us -> 377 us (0.967); the launches traced: 383 us -> 374 us
  Pallas kernels: 226 us -> 219 us
    pallas_call x2, Pallas kernels: 27 us -> 22.9 us  [attention_call(): pl.pallas_call(functools.partial(attention_kernel, group, block), grid=(s...]
where the time goes in v1:
time: 377 us; the launch traced here: 374 us
  Pallas kernels  219 us (58%)
  waiting for transfers between devices  68.9 us (18%)
  starting transfers between devices  44.1 us (12%)
  other arithmetic  19.5 us (5%)
  between operations  15.1 us (4%)
  local copies, waits for them, and re-layouts  8.17 us (2%)
    pallas_call x1, Pallas kernels, back_call(): pl.pallas_call(functools.partial(back_kernel, (len(out_pieces), len(up_pi...  48 us
    ppermute x34, waiting for transfers between devices, swap(): return lax.ppermute(value, 'dp', [(d, d ^ flips[d & 1]) for d in range(8)])  47.7 us
    pallas_call x2, Pallas kernels, up_call(): pl.pallas_call(functools.partial(up_kernel, (len(up_pieces), len(earlier)...  38.9 us
    pallas_call x2, Pallas kernels, attention_back_call(): pl.pallas_call(functools.partial(attention_back_kernel, group, block), gr...  36.8 us
    pallas_call x2, Pallas kernels, attention_call(): pl.pallas_call(functools.partial(attention_kernel, group, block), grid=(s...  22.9 us
    ppermute x34, starting transfers between devices, swap(): return lax.ppermute(value, 'dp', [(d, d ^ flips[d & 1]) for d in range(8)])  22.2 us
    pallas_call x1, Pallas kernels, first_call(): pl.pallas_call(functools.partial(first_kernel, len(pieces)), grid_spec=gr...  16.1 us
    pallas_call x1, Pallas kernels, down_call(): pl.pallas_call(functools.partial(down_kernel, len(pieces), len(earlier),...  15.1 us
  transfers between devices with their start and end apart: 57, of which 19 were waited for; matrix products, arithmetic and copies ran while one was open for 4% of the time, Pallas kernels for 58%

profile of v1, /device:TPU:0, one launch (start us, length us, event | category | flops | bytes accessed | tf_op | source)
XLA Modules:
  0.0 374.4 jit_solution(9077232550098468833)
XLA Ops:
  7.2 3.0 collective-permute-start.3
  10.3 1.5 collective-permute-start.4
  11.8 1.6 collective-permute-start
  13.3 2.6 collective-permute-start.1
  18.2 1.7 pad_maximum_fusion.1
  20.0 1.7 collective-permute-done
  21.7 6.8 %collective-permute-done.1 = bf16[128,768]{1,0:T(8,128)(2,1)S(1)} collective-permute-done((bf16[128,768]{1,0:T(8,128)(2,1)}, bf16[128,768]{1,0:T(8,128)(2,1)S(1)}, u32[]{:S(2)}, u32[]{:S(2)}) %collective-permute-start.1) | collective-permute-done | bytes 196640 | tf_op jit(solution)/shard_map/ppermute | solution.py:1197
  29.7 14.3 %collective-permute-done.10.rest_9_ = bf16[3,128,768]{2,1,0:T(8,128)(2,1)S(1)} collective-permute-done((bf16[3,128,768]{2,1,0:T(8,128)(2,1)S(1)}, bf16[3,128,768]{2,1,0:T(8,128)(2,1)S(1)}, u32[]{:S(2)}, u32[]{:S(2)}) %collective-permute-start.10) | collective-permute-done | bytes 589856 | tf_op jit(solution)/shard_map/ppermute | solution.py:1193
  47.5 6.6 %collective-permute-done.12.rest_11_ = bf16[3,128,768]{2,1,0:T(8,128)(2,1)S(1)} collective-permute-done((bf16[3,128,768]{2,1,0:T(8,128)(2,1)S(1)}, bf16[3,128,768]{2,1,0:T(8,128)(2,1)S(1)}, u32[]{:S(2)}, u32[]{:S(2)}) %collective-permute-start.12) | collective-permute-done | bytes 589856 | tf_op jit(solution)/shard_map/ppermute | solution.py:1193
  54.6 1.8 collective-permute-done.8.rest_6_
  59.5 3.4 all-gather.5.cloned.1.call-done
  62.9 1.5 collective-permute-start.17
  64.4 1.5 collective-permute-start.18
  68.2 12.9 %project.1 = (bf16[1024,1024]{1,0:T(8,128)(2,1)}, bf16[3072,1024]{1,0:T(8,128)(2,1)}) custom-call(s32[48]{0:T(128)} %stack.183.tab, bf16[1024,1024]{1,0:T(8,128)(2,1)} %bitcast.81, f32[1,1024]{1,0:T(1,128)} %bitcast.106, f32[1,1024]{1,0:T(1,128)} %bitcast.101, f32[1,3072]{1,0:T(1,128)} %bitcast.98, bf16[128,768]{1,0:T(8,128)(2,1)} %rest_0_.3, ...), custom_call_target="tpu_custom_call" | custom-call | flops 8000000 | bytes 80000 | tf_op jit(solution)/shard_map/project/pallas_call | solution.py:309
  81.1 11.5 %attention.2 = (bf16[1024,1024]{1,0:T(8,128)(2,1)}, f32[8,2,1024]{2,1,0:T(2,128)}) custom-call(s32[1]{0:T(128)S(6)} %copy.41.lengths, bf16[3072,1024]{1,0:T(8,128)(2,1)} %get-tuple-element.122.query.key.value, bf16[3072,1024]{1,0:T(8,128)(2,1)} %get-tuple-element.122.query.key.value, bf16[3072,1024]{1,0:T(8,128)(2,1)} %get-tuple-element.122.query.key.value), custom_call_target="tpu_custom_call" | custom-call | flops 42949672 | bytes 64000 | tf_op jit(solution)/shard_map/attention/pallas_call | solution.py:396
  92.6 1.6 collective-permute-done.17.rest_1_.rest_2_.rest_10_
  95.5 11.4 %attention.3 = (bf16[1024,1024]{1,0:T(8,128)(2,1)}, f32[8,2,1024]{2,1,0:T(2,128)}) custom-call(s32[1]{0:T(128)S(6)} %copy.41.lengths, bf16[3072,1024]{1,0:T(8,128)(2,1)} %get-tuple-element.122.query.key.value, bf16[3072,1024]{1,0:T(8,128)(2,1)} %get-tuple-element.122.query.key.value, ...), custom_call_target="tpu_custom_call", output_to_operand_aliasing={{0}: (4, {}), {1}: (5, {})} | custom-call | flops 42949672 | bytes 64000 | tf_op jit(solution)/shard_map/attention/pallas_call | solution.py:396
  106.9 5.0 %collective-permute-done.19.rest_3_.rest_4_.rest_12_ = bf16[4,128,1280]{2,1,0:T(8,128)(2,1)} collective-permute-done((bf16[4,128,1280]{2,1,0:T(8,128)(2,1)S(1)}, bf16[4,128,1280]{2,1,0:T(8,128)(2,1)}, u32[]{:S(2)}, u32[]{:S(2)}) %collective-permute-start.19) | collective-permute-done | bytes 1310752 | tf_op jit(solution)/shard_map/ppermute | solution.py:1193
  112.6 1.5 collective-permute-start.24
  115.3 9.5 %out.1 = (f32[1024,1024]{1,0:T(8,128)}, bf16[1024,1024]{1,0:T(8,128)(2,1)}, bf16[1024,1024]{1,0:T(8,128)(2,1)}, f32[1,1024]{1,0:T(1,128)}) custom-call(s32[48]{0:T(128)} %stack.178.tab, s32[1]{0:T(128)S(6)} %copy.41.lengths, bf16[1024,1024]{1,0:T(8,128)(2,1)} %get-tuple-element.124.mixture, bf16[1024,1024]{1,0:T(8,128)(2,1)} %bitcast.82, ...), custom_call_target="tpu_custom_call" | custom-call | flops 8 | bytes 8 | tf_op jit(solution)/shard_map/out/pallas_call | solution.py:468
  124.8 19.7 %up.2 = (bf16[1024,4096]{1,0:T(8,128)(2,1)}, bf16[1024,4096]{1,0:T(8,128)(2,1)}, bf16[4096,1024]{1,0:T(8,128)(2,1)}) custom-call(s32[48]{0:T(128)} %stack.178.tab, bf16[1024,1024]{1,0:T(8,128)(2,1)} %get-tuple-element.134.normed, bf16[1024,1024]{1,0:T(8,128)(2,1)} %get-tuple-element.129.result.d_result, f32[1,4096]{1,0:T(1,128)} %bitcast.113, ...), custom_call_target="tpu_custom_call" | custom-call | flops 68719476736 | bytes 400000000 | tf_op jit(solution)/shard_map/up/pallas_call | solution.py:564
  145.9 19.2 %up.3 = (bf16[1024,4096]{1,0:T(8,128)(2,1)}, bf16[1024,4096]{1,0:T(8,128)(2,1)}, bf16[4096,1024]{1,0:T(8,128)(2,1)}) custom-call(s32[48]{0:T(128)} %stack.178.tab, bf16[1024,1024]{1,0:T(8,128)(2,1)} %get-tuple-element.134.normed, ...), custom_call_target="tpu_custom_call", output_to_operand_aliasing={{0}: (12, {}), {1}: (13, {}), {2}: (14, {})} | custom-call | flops 68719476736 | bytes 400000000 | tf_op jit(solution)/shard_map/up/pallas_call | solution.py:564
  166.1 2.0 collective-permute-done.30.rest_24_.rest_7_
  168.1 48.0 %back.1 = (f32[1024,1024]{1,0:T(8,128)}, bf16[1024,1024]{1,0:T(8,128)(2,1)}, f32[1,4096]{1,0:T(1,128)}, f32[1,1024]{1,0:T(1,128)}, f32[1,1024]{1,0:T(1,128)}, /*...) custom-call(s32[48]{0:T(128)} %stack.178.tab, ...), custom_call_target="tpu_custom_call" | custom-call | flops 240518168576 | bytes 480000000 | tf_op jit(solution)/shard_map/back/pallas_call | solution.py:806
  216.8 10.3 %attention_back.2.rest_0_ = bf16[3,1024,1024]{2,1,0:T(8,128)(2,1)} custom-call(s32[1]{0:T(128)S(6)} %copy.41.lengths, bf16[3072,1024]{1,0:T(8,128)(2,1)} %get-tuple-element.122.query.key.value, bf16[3072,1024]{1,0:T(8,128)(2,1)} %get-tuple-element.122.query.key.value, bf16[3072,1024]{1,0:T(8,128)(2,1)} %get-tuple-element.122.query.key.value, ...), custom_call_target="tpu_custom_call" | custom-call | flops 5368709120 | bytes 8000000 | tf_op jit(solution)/shard_map/attention_back/pallas_call | solution.py:906
  227.1 3.2 add_convert_fusion
  230.4 26.5 %attention_back.3 = bf16[3,1024,1024]{2,1,0:T(8,128)(2,1)} custom-call(s32[1]{0:T(128)S(6)} %copy.41.lengths, bf16[3072,1024]{1,0:T(8,128)(2,1)} %get-tuple-element.122.query.key.value, bf16[3072,1024]{1,0:T(8,128)(2,1)} %get-tuple-element.122.query.key.value, bf16[3072,1024]{1,0:T(8,128)(2,1)} %get-tuple-element.122.query.key.value, ...), custom_call_target="tpu_custom_call", output_to_operand_aliasing={{}: (7, {})} | custom-call | flops 16106127360 | bytes 8000000 | tf_op jit(solution)/shard_map/attention_back/pallas_call | solution.py:906
  256.9 5.8 %collective-permute-done.32.refs_2_ = bf16[2,4,128,1280]{3,2,1,0:T(8,128)(2,1)} collective-permute-done((bf16[2,4,128,1280]{3,2,1,0:T(8,128)(2,1)S(1)}, bf16[2,4,128,1280]{3,2,1,0:T(8,128)(2,1)}, u32[]{:S(2)}, u32[]{:S(2)}) %collective-permute-start.32) | collective-permute-done | bytes 2621472 | tf_op jit(solution)/shard_map/ppermute | solution.py:1193
  262.7 2.6 fusion
  265.3 1.5 collective-permute-start.34
  266.8 11.9 %attend_grad.1 = (f32[1,3072]{1,0:T(1,128)}, bf16[4,4,128,768]{3,2,1,0:T(8,128)(2,1)}, bf16[4,4,128,768]{3,2,1,0:T(8,128)(2,1)}) custom-call(s32[48]{0:T(128)} %stack.183.tab, bf16[3072,1024]{1,0:T(8,128)(2,1)} %bitcast.84, bf16[1024,1024]{1,0:T(8,128)(2,1)} %get-tuple-element.150.normed), custom_call_target="tpu_custom_call" | custom-call | flops 51539607552 | bytes 112000000 | tf_op jit(solution)/shard_map/attend_grad/pallas_call | solution.py:966
  278.8 4.1 %collective-permute-done.34.refs_3_ = bf16[4,128,1280]{2,1,0:T(8,128)(2,1)S(1)} collective-permute-done((bf16[4,128,1280]{2,1,0:T(8,128)(2,1)S(1)}, bf16[4,128,1280]{2,1,0:T(8,128)(2,1)S(1)}, u32[]{:S(2)}, u32[]{:S(2)}) %collective-permute-start.34) | collective-permute-done | bytes 1310752 | tf_op jit(solution)/shard_map/ppermute | solution.py:1193
  284.0 5.0 %add.183 = (f32[128,1280]{1,0:T(8,128)}, bf16[128,1280]{1,0:T(8,128)(2,1)}, bf16[128,1280]{1,0:T(8,128)(2,1)}, bf16[128,1280]{1,0:T(8,128)(2,1)}) custom-call(bf16[4,4,128,1280]{3,2,1,0:T(8,128)(2,1)} %get-tuple-element.142.refs_0_, bf16[4,4,128,1280]{3,2,1,0:T(8,128)(2,1)} %collective-permute-done.31.refs_1_, ...), custom_call_target="tpu_custom_call" | custom-call | flops 80000000000 | bytes 80000000 | tf_op jit(solution)/shard_map/add/pallas_call | solution.py:1252
  289.0 1.5 collective-permute-start.37
  290.5 2.4 collective-permute-start.38
  292.9 1.4 collective-permute-start.39
  294.3 2.9 add_convert_fusion.1
  297.9 16.1 %first.1 = (bf16[1024,1024]{1,0:T(8,128)(2,1)}, f32[96,128]{1,0:T(8,128)}) custom-call(s32[48]{0:T(128)} %stack.183.tab, bf16[3072,1024]{1,0:T(8,128)(2,1)} %bitcast.85, bf16[1024,1024]{1,0:T(8,128)(2,1)} %bitcast.83, f32[1024,1024]{1,0:T(8,128)} %get-tuple-element.161.d_middle, f32[1,1024]{1,0:T(1,128)} %bitcast.107, bf16[128,768]{1,0:T(8,128)(2,1)} %rest_0_.3, ...), custom_call_target="tpu_custom_call" | custom-call | flops 51539607552 | bytes 192000000 | tf_op jit(solution)/shard_map/first/pallas_call | solution.py:1088
  314.5 3.4 collective-permute-done.35
  318.5 2.5 fusion.1
  321.1 2.4 collective-permute-start.42
  323.5 1.5 collective-permute-start.36
  325.0 15.1 %down.1 = bf16[1024,1024]{1,0:T(8,128)(2,1)} custom-call(s32[48]{0:T(128)} %stack.178.tab, bf16[1024,4096]{1,0:T(8,128)(2,1)} %get-tuple-element.170.active, f32[1024,1024]{1,0:T(8,128)} %get-tuple-element.171.middle, f32[1,1024]{1,0:T(1,128)} %bitcast.116, bf16[4,512,256]{2,1,0:T(8,128)(2,1)} %bitcast.112, ...), custom_call_target="tpu_custom_call" | custom-call | flops 68719476736 | bytes 192000000 | tf_op jit(solution)/shard_map/down/pallas_call | solution.py:1167
  340.2 2.1 fusion.2
  346.4 1.9 collective-permute-start.52
  354.1 4.2 %collective-permute-done.51 = bf16[128,768]{1,0:T(8,128)(2,1)S(1)} collective-permute-done((bf16[128,768]{1,0:T(8,128)(2,1)S(1)}, bf16[128,768]{1,0:T(8,128)(2,1)S(1)}, u32[]{:S(2)}, u32[]{:S(2)}) %collective-permute-start.51) | collective-permute-done | bytes 196640 | tf_op jit(solution)/shard_map/ppermute | solution.py:1197
  360.0 3.6 collective-permute-done.48.refs_6_
  364.8 1.6 small.1
  (169 shorter events, 35.5 us)
Async XLA Ops:
  7.2 55.7 %all-gather.5.cloned.1.call-start = ((), (), s32[]{:S(2)}) async-start(), calls=%async_computation.4 | async-start | bytes 1638400 | tf_op jit(solution)/shard_map/all_gather | solution.py:1345
  7.2 10.0 %collective-permute-start.3 = (bf16[128,768]{1,0:T(8,128)(2,1)}, bf16[128,768]{1,0:T(8,128)(2,1)S(1)}, u32[]{:S(2)}, u32[]{:S(2)}) collective-permute-start(bf16[128,768]{1,0:T(8,128)(2,1)} %rest_0_.3), channel_id=1, source_target_pairs={{0,16},{4,12},{8,24},{12,4},{16,0},{20,28},{24,8},{28,20},{1,17},{... | collective-permute-start | bytes 589832 | tf_op jit(solution)/shard_map/ppermute | solution.py:1193
  10.3 7.0 %collective-permute-start.4 = (bf16[128,768]{1,0:T(8,128)(2,1)}, bf16[128,768]{1,0:T(8,128)(2,1)S(1)}, u32[]{:S(2)}, u32[]{:S(2)}) collective-permute-start(bf16[128,768]{1,0:T(8,128)(2,1)} %rest_0_.3), channel_id=1, source_target_pairs={{0,8},{4,20},{8,0},{12,28},{16,24},{20,4},{24,16},{28,12},{1,9},{5... | collective-permute-start | bytes 589832 | tf_op jit(solution)/shard_map/ppermute | solution.py:1193
  11.8 9.9 %collective-permute-start = (bf16[128,768]{1,0:T(8,128)(2,1)}, bf16[128,768]{1,0:T(8,128)(2,1)S(1)}, u32[]{:S(2)}, u32[]{:S(2)}) collective-permute-start(bf16[128,768]{1,0:T(8,128)(2,1)} %rest_0_.3), channel_id=1, source_target_pairs={{0,1},{1,2},{2,3},{3,0},{4,5},{5,6},{6,7},{7,4},{8,9},{9,10},{10,1... | collective-permute-start | bytes 589832 | tf_op jit(solution)/shard_map/ppermute | solution.py:1197
  13.3 15.1 %collective-permute-start.1 = (bf16[128,768]{1,0:T(8,128)(2,1)}, bf16[128,768]{1,0:T(8,128)(2,1)S(1)}, u32[]{:S(2)}, u32[]{:S(2)}) collective-permute-start(bf16[128,768]{1,0:T(8,128)(2,1)} %rest_0_.3), channel_id=1, source_target_pairs={{0,2},{1,3},{2,0},{3,1},{4,6},{5,7},{6,4},{7,5},{8,10},{9,11},{10,... | collective-permute-start | bytes 589832 | tf_op jit(solution)/shard_map/ppermute | solution.py:1197
  15.9 12.5 %collective-permute-start.2 = (bf16[128,768]{1,0:T(8,128)(2,1)}, bf16[128,768]{1,0:T(8,128)(2,1)S(1)}, u32[]{:S(2)}, u32[]{:S(2)}) collective-permute-start(bf16[128,768]{1,0:T(8,128)(2,1)} %rest_0_.3), channel_id=1, source_target_pairs={{0,3},{1,0},{2,1},{3,2},{4,7},{5,4},{6,5},{7,6},{8,11},{9,8},{10,9... | collective-permute-start | bytes 589832 | tf_op jit(solution)/shard_map/ppermute | solution.py:1197
  17.3 11.3 %collective-permute-start.5 = (bf16[128,768]{1,0:T(8,128)(2,1)S(1)}, bf16[128,768]{1,0:T(8,128)(2,1)S(1)}, u32[]{:S(2)}, u32[]{:S(2)}) collective-permute-start(bf16[128,768]{1,0:T(8,128)(2,1)S(1)} %collective-permute-done.4.rest_1_), channel_id=1, source_target_pairs={{0,16},{4,12},{8,24},{12,4},{16,0},{20,28},{24,8},{28,20},{1,17},{... | collective-permute-start | bytes 589832 | tf_op jit(solution)/shard_map/ppermute | solution.py:1193
  28.6 66.9 %all-gather.7.cloned.1.call-start = ((), (), s32[]{:S(2)}) async-start(), calls=%async_computation.5 | async-start | bytes 1310720 | tf_op jit(solution)/shard_map/all_gather | solution.py:1352
  28.6 15.4 %collective-permute-start.10 = (bf16[3,128,768]{2,1,0:T(8,128)(2,1)S(1)}, bf16[3,128,768]{2,1,0:T(8,128)(2,1)S(1)}, u32[]{:S(2)}, u32[]{:S(2)}) collective-permute-start(bf16[3,128,768]{2,1,0:T(8,128)(2,1)S(1)} %pad_maximum_fusion.rest_8_), channel_id=1, source_target_pairs={{0,8},{4,20},{8,0},{12,28},{16,24},{20,4},{24,16},{28,12},{1,9},{5... | collective-permute-start | bytes 1769480 | tf_op jit(solution)/shard_map/ppermute | solution.py:1193
  29.2 14.9 %collective-permute-start.11 = (bf16[3,128,768]{2,1,0:T(8,128)(2,1)S(1)}, bf16[3,128,768]{2,1,0:T(8,128)(2,1)S(1)}, u32[]{:S(2)}, u32[]{:S(2)}) collective-permute-start(bf16[3,128,768]{2,1,0:T(8,128)(2,1)S(1)} %pad_maximum_fusion.rest_8_), channel_id=1, source_target_pairs={{0,16},{4,12},{8,24},{12,4},{16,0},{20,28},{24,8},{28,20},{1,17},{... | collective-permute-start | bytes 1769480 | tf_op jit(solution)/shard_map/ppermute | solution.py:1193
  44.1 9.9 %collective-permute-start.12 = (bf16[3,128,768]{2,1,0:T(8,128)(2,1)S(1)}, bf16[3,128,768]{2,1,0:T(8,128)(2,1)S(1)}, u32[]{:S(2)}, u32[]{:S(2)}) collective-permute-start(bf16[3,128,768]{2,1,0:T(8,128)(2,1)S(1)} %collective-permute-done.10.rest_9_), channel_id=1, source_target_pairs={{0,16},{4,12},{8,24},{12,4},{16,0},{20,28},{24,8},{28,20},{1,17},{... | collective-permute-start | bytes 1769480 | tf_op jit(solution)/shard_map/ppermute | solution.py:1193
  45.3 8.8 %collective-permute-start.7 = (bf16[128,768]{1,0:T(8,128)(2,1)S(1)}, bf16[128,768]{1,0:T(8,128)(2,1)S(1)}, u32[]{:S(2)}, u32[]{:S(2)}) collective-permute-start(bf16[128,768]{1,0:T(8,128)(2,1)S(1)} %collective-permute-done.4.rest_1_), channel_id=1, source_target_pairs={{0,4},{4,0},{8,12},{12,8},{16,20},{20,16},{24,28},{28,24},{1,5},{5... | collective-permute-start | bytes 589832 | tf_op jit(solution)/shard_map/ppermute | solution.py:1193
  45.8 12.0 %collective-permute-start.13 = (bf16[3,128,768]{2,1,0:T(8,128)(2,1)S(1)}, bf16[3,128,768]{2,1,0:T(8,128)(2,1)S(1)}, u32[]{:S(2)}, u32[]{:S(2)}) collective-permute-start(bf16[3,128,768]{2,1,0:T(8,128)(2,1)S(1)} %pad_maximum_fusion.rest_8_), channel_id=1, source_target_pairs={{0,4},{4,0},{8,12},{12,8},{16,20},{20,16},{24,28},{28,24},{1,5},{5... | collective-permute-start | bytes 1769480 | tf_op jit(solution)/shard_map/ppermute | solution.py:1193
  45.8 12.0 %collective-permute-start.14 = (bf16[3,128,768]{2,1,0:T(8,128)(2,1)S(1)}, bf16[3,128,768]{2,1,0:T(8,128)(2,1)S(1)}, u32[]{:S(2)}, u32[]{:S(2)}) collective-permute-start(bf16[3,128,768]{2,1,0:T(8,128)(2,1)S(1)} %collective-permute-done.10.rest_9_), channel_id=1, source_target_pairs={{0,4},{4,0},{8,12},{12,8},{16,20},{20,16},{24,28},{28,24},{1,5},{5... | collective-permute-start | bytes 1769480 | tf_op jit(solution)/shard_map/ppermute | solution.py:1193
  47.3 10.5 %collective-permute-start.15 = (bf16[3,128,768]{2,1,0:T(8,128)(2,1)S(1)}, bf16[3,128,768]{2,1,0:T(8,128)(2,1)S(1)}, u32[]{:S(2)}, u32[]{:S(2)}) collective-permute-start(bf16[3,128,768]{2,1,0:T(8,128)(2,1)S(1)} %collective-permute-done.11.rest_10_), channel_id=1, source_target_pairs={{0,4},{4,0},{8,12},{12,8},{16,20},{20,16},{24,28},{28,24},{1,5},{5... | collective-permute-start | bytes 1769480 | tf_op jit(solution)/shard_map/ppermute | solution.py:1193
  54.0 5.4 %collective-permute-start.16 = (bf16[3,128,768]{2,1,0:T(8,128)(2,1)S(1)}, bf16[3,128,768]{2,1,0:T(8,128)(2,1)}, u32[]{:S(2)}, u32[]{:S(2)}) collective-permute-start(bf16[3,128,768]{2,1,0:T(8,128)(2,1)S(1)} %collective-permute-done.12.rest_11_), channel_id=1, source_target_pairs={{0,4},{4,0},{8,12},{12,8},{16,20},{20,16},{24,28},{28,24},{1,5},{5... | collective-permute-start | bytes 1769480 | tf_op jit(solution)/shard_map/ppermute | solution.py:1193
  62.9 31.3 %collective-permute-start.17 = (bf16[4,128,1280]{2,1,0:T(8,128)(2,1)}, bf16[4,128,1280]{2,1,0:T(8,128)(2,1)S(1)}, u32[]{:S(2)}, u32[]{:S(2)}) collective-permute-start(bf16[4,128,1280]{2,1,0:T(8,128)(2,1)} %bitcast.87), channel_id=1, source_target_pairs={{0,8},{4,20},{8,0},{12,28},{16,24},{20,4},{24,16},{28,12},{1,9},{5... | collective-permute-start | bytes 3932168 | tf_op jit(solution)/shard_map/ppermute | solution.py:1193
  64.4 29.8 %collective-permute-start.18 = (bf16[4,128,1280]{2,1,0:T(8,128)(2,1)}, bf16[4,128,1280]{2,1,0:T(8,128)(2,1)}, u32[]{:S(2)}, u32[]{:S(2)}) collective-permute-start(bf16[4,128,1280]{2,1,0:T(8,128)(2,1)} %bitcast.88), channel_id=1, source_target_pairs={{0,16},{4,12},{8,24},{12,4},{16,0},{20,28},{24,8},{28,20},{1,17},{... | collective-permute-start | bytes 3932168 | tf_op jit(solution)/shard_map/ppermute | solution.py:1193
  67.3 195.4 %reduce-scatter.3.cloned.1.call-start = ((), (), s32[]{:S(2)}) async-start(), calls=%async_computation.2 | async-start | bytes 9437184 | tf_op jit(solution)/shard_map/reduce_scatter | solution.py:1408
  94.2 17.7 %collective-permute-start.19 = (bf16[4,128,1280]{2,1,0:T(8,128)(2,1)S(1)}, bf16[4,128,1280]{2,1,0:T(8,128)(2,1)}, u32[]{:S(2)}, u32[]{:S(2)}) collective-permute-start(bf16[4,128,1280]{2,1,0:T(8,128)(2,1)S(1)} %collective-permute-done.17.rest_1_.rest_2_.rest_10_), channel_id=1, source_target_pairs={{0,16},{4,12},{8,24},{12,4},{16,0},{20,28},{24,8},{28,20},{1,17},{... | collective-permute-start | bytes 3932168 | tf_op jit(solution)/shard_map/ppermute | solution.py:1193
  94.8 19.3 %collective-permute-start.20 = (bf16[4,128,1280]{2,1,0:T(8,128)(2,1)S(1)}, bf16[4,128,1280]{2,1,0:T(8,128)(2,1)}, u32[]{:S(2)}, u32[]{:S(2)}) collective-permute-start(bf16[4,128,1280]{2,1,0:T(8,128)(2,1)S(1)} %bitcast.94), channel_id=1, source_target_pairs={{0,4},{4,0},{8,12},{12,8},{16,20},{20,16},{24,28},{28,24},{1,5},{5... | collective-permute-start | bytes 3932168 | tf_op jit(solution)/shard_map/ppermute | solution.py:1193
  94.9 19.7 %collective-permute-start.21 = (bf16[4,128,1280]{2,1,0:T(8,128)(2,1)S(1)}, bf16[4,128,1280]{2,1,0:T(8,128)(2,1)}, u32[]{:S(2)}, u32[]{:S(2)}) collective-permute-start(bf16[4,128,1280]{2,1,0:T(8,128)(2,1)S(1)} %collective-permute-done.17.rest_1_.rest_2_.rest_10_), channel_id=1, source_target_pairs={{0,4},{4,0},{8,12},{12,8},{16,20},{20,16},{24,28},{28,24},{1,5},{5... | collective-permute-start | bytes 3932168 | tf_op jit(solution)/shard_map/ppermute | solution.py:1193
  95.3 19.4 %collective-permute-start.22 = (bf16[4,128,1280]{2,1,0:T(8,128)(2,1)}, bf16[4,128,1280]{2,1,0:T(8,128)(2,1)}, u32[]{:S(2)}, u32[]{:S(2)}) collective-permute-start(bf16[4,128,1280]{2,1,0:T(8,128)(2,1)} %collective-permute-done.18.rest_2_.rest_3_.rest_11_), channel_id=1, source_target_pairs={{0,4},{4,0},{8,12},{12,8},{16,20},{20,16},{24,28},{28,24},{1,5},{5... | collective-permute-start | bytes 3932168 | tf_op jit(solution)/shard_map/ppermute | solution.py:1193
  112.6 31.9 %collective-permute-start.24 = (bf16[4,512,256]{2,1,0:T(8,128)(2,1)}, bf16[4,512,256]{2,1,0:T(8,128)(2,1)}, u32[]{:S(2)}, u32[]{:S(2)}) collective-permute-start(bf16[4,512,256]{2,1,0:T(8,128)(2,1)} %bitcast.108), channel_id=1, source_target_pairs={{0,8},{4,20},{8,0},{12,28},{16,24},{20,4},{24,16},{28,12},{1,9},{5... | collective-permute-start | bytes 3145736 | tf_op jit(solution)/shard_map/ppermute | solution.py:1193
  114.1 30.4 %collective-permute-start.25 = (bf16[4,512,256]{2,1,0:T(8,128)(2,1)}, bf16[4,512,256]{2,1,0:T(8,128)(2,1)S(1)}, u32[]{:S(2)}, u32[]{:S(2)}) collective-permute-start(bf16[4,512,256]{2,1,0:T(8,128)(2,1)} %bitcast.109), channel_id=1, source_target_pairs={{0,16},{4,12},{8,24},{12,4},{16,0},{20,28},{24,8},{28,20},{1,17},{... | collective-permute-start | bytes 3145736 | tf_op jit(solution)/shard_map/ppermute | solution.py:1193
  114.6 51.5 %collective-permute-start.27 = (bf16[4,512,256]{2,1,0:T(8,128)(2,1)}, bf16[4,512,256]{2,1,0:T(8,128)(2,1)S(1)}, u32[]{:S(2)}, u32[]{:S(2)}) collective-permute-start(bf16[4,512,256]{2,1,0:T(8,128)(2,1)} %bitcast.110), channel_id=1, source_target_pairs={{0,4},{4,0},{8,12},{12,8},{16,20},{20,16},{24,28},{28,24},{1,5},{5... | collective-permute-start | bytes 3145736 | tf_op jit(solution)/shard_map/ppermute | solution.py:1193
  144.5 20.6 %collective-permute-start.26 = (bf16[4,512,256]{2,1,0:T(8,128)(2,1)}, bf16[4,512,256]{2,1,0:T(8,128)(2,1)S(1)}, u32[]{:S(2)}, u32[]{:S(2)}) collective-permute-start(bf16[4,512,256]{2,1,0:T(8,128)(2,1)} %collective-permute-done.24.rest_18_.rest_1_), channel_id=1, source_target_pairs={{0,16},{4,12},{8,24},{12,4},{16,0},{20,28},{24,8},{28,20},{1,17},{... | collective-permute-start | bytes 3145736 | tf_op jit(solution)/shard_map/ppermute | solution.py:1193
  145.4 20.7 %collective-permute-start.28 = (bf16[4,512,256]{2,1,0:T(8,128)(2,1)}, bf16[4,512,256]{2,1,0:T(8,128)(2,1)}, u32[]{:S(2)}, u32[]{:S(2)}) collective-permute-start(bf16[4,512,256]{2,1,0:T(8,128)(2,1)} %collective-permute-done.24.rest_18_.rest_1_), channel_id=1, source_target_pairs={{0,4},{4,0},{8,12},{12,8},{16,20},{20,16},{24,28},{28,24},{1,5},{5... | collective-permute-start | bytes 3145736 | tf_op jit(solution)/shard_map/ppermute | solution.py:1193
  145.9 20.3 %collective-permute-start.29 = (bf16[4,512,256]{2,1,0:T(8,128)(2,1)S(1)}, bf16[4,512,256]{2,1,0:T(8,128)(2,1)}, u32[]{:S(2)}, u32[]{:S(2)}) collective-permute-start(bf16[4,512,256]{2,1,0:T(8,128)(2,1)S(1)} %collective-permute-done.25.rest_19_.rest_2_), channel_id=1, source_target_pairs={{0,4},{4,0},{8,12},{12,8},{16,20},{20,16},{24,28},{28,24},{1,5},{5... | collective-permute-start | bytes 3145736 | tf_op jit(solution)/shard_map/ppermute | solution.py:1193
  166.1 152.4 %reduce-scatter.5.cloned.1.call-start = ((), (), s32[]{:S(2)}) async-start(), calls=%async_computation.3 | async-start | bytes 1310720 | tf_op jit(solution)/shard_map/reduce_scatter | solution.py:1444
  216.1 10.9 %collective-permute-start.31 = (bf16[4,4,128,1280]{3,2,1,0:T(8,128)(2,1)}, bf16[4,4,128,1280]{3,2,1,0:T(8,128)(2,1)}, u32[]{:S(2)}, u32[]{:S(2)}) collective-permute-start(bf16[4,4,128,1280]{3,2,1,0:T(8,128)(2,1)} %get-tuple-element.143), channel_id=1, source_target_pairs={{0,4},{4,0},{8,12},{12,8},{16,20},{20,16},{24,28},{28,24},{1,5},{5... | collective-permute-start | bytes 15728648 | tf_op jit(solution)/shard_map/ppermute | solution.py:1193
  230.3 32.4 %collective-permute-start.32 = (bf16[2,4,128,1280]{3,2,1,0:T(8,128)(2,1)S(1)}, bf16[2,4,128,1280]{3,2,1,0:T(8,128)(2,1)}, u32[]{:S(2)}, u32[]{:S(2)}) collective-permute-start(bf16[2,4,128,1280]{3,2,1,0:T(8,128)(2,1)S(1)} %add_convert_fusion), channel_id=1, source_target_pairs={{0,16},{4,12},{8,24},{12,4},{16,0},{20,28},{24,8},{28,20},{1,17},{... | collective-permute-start | bytes 7864328 | tf_op jit(solution)/shard_map/ppermute | solution.py:1193
  265.3 17.7 %collective-permute-start.34 = (bf16[4,128,1280]{2,1,0:T(8,128)(2,1)S(1)}, bf16[4,128,1280]{2,1,0:T(8,128)(2,1)S(1)}, u32[]{:S(2)}, u32[]{:S(2)}) collective-permute-start(bf16[4,128,1280]{2,1,0:T(8,128)(2,1)S(1)} %fusion), channel_id=1, source_target_pairs={{0,8},{4,20},{8,0},{12,28},{16,24},{20,4},{24,16},{28,12},{1,9},{5... | collective-permute-start | bytes 3932168 | tf_op jit(solution)/shard_map/ppermute | solution.py:1193
  278.8 15.6 %collective-permute-start.33 = (bf16[4,4,128,768]{3,2,1,0:T(8,128)(2,1)}, bf16[4,4,128,768]{3,2,1,0:T(8,128)(2,1)}, u32[]{:S(2)}, u32[]{:S(2)}) collective-permute-start(bf16[4,4,128,768]{3,2,1,0:T(8,128)(2,1)} %get-tuple-element.152), channel_id=1, source_target_pairs={{0,4},{4,0},{8,12},{12,8},{16,20},{20,16},{24,28},{28,24},{1,5},{5... | collective-permute-start | bytes 9437192 | tf_op jit(solution)/shard_map/ppermute | solution.py:1193
  289.0 32.1 %collective-permute-start.37 = (bf16[128,1280]{1,0:T(8,128)(2,1)}, bf16[128,1280]{1,0:T(8,128)(2,1)S(1)}, u32[]{:S(2)}, u32[]{:S(2)}) collective-permute-start(bf16[128,1280]{1,0:T(8,128)(2,1)} %get-tuple-element.156), channel_id=1, source_target_pairs={{0,1},{1,2},{2,3},{3,0},{4,5},{5,6},{6,7},{7,4},{8,9},{9,10},{10,1... | collective-permute-start | bytes 983048 | tf_op jit(solution)/shard_map/ppermute | solution.py:1197
  290.5 33.0 %collective-permute-start.38 = (bf16[128,1280]{1,0:T(8,128)(2,1)}, bf16[128,1280]{1,0:T(8,128)(2,1)}, u32[]{:S(2)}, u32[]{:S(2)}) collective-permute-start(bf16[128,1280]{1,0:T(8,128)(2,1)} %get-tuple-element.157), channel_id=1, source_target_pairs={{0,2},{1,3},{2,0},{3,1},{4,6},{5,7},{6,4},{7,5},{8,10},{9,11},{10,... | collective-permute-start | bytes 983048 | tf_op jit(solution)/shard_map/ppermute | solution.py:1197
  292.9 47.3 %collective-permute-start.39 = (bf16[128,1280]{1,0:T(8,128)(2,1)}, bf16[128,1280]{1,0:T(8,128)(2,1)}, u32[]{:S(2)}, u32[]{:S(2)}) collective-permute-start(bf16[128,1280]{1,0:T(8,128)(2,1)} %get-tuple-element.158), channel_id=1, source_target_pairs={{0,3},{1,0},{2,1},{3,2},{4,7},{5,4},{6,5},{7,6},{8,11},{9,8},{10,9... | collective-permute-start | bytes 983048 | tf_op jit(solution)/shard_map/ppermute | solution.py:1197
  297.3 20.7 %collective-permute-start.35 = (bf16[2,4,128,768]{3,2,1,0:T(8,128)(2,1)}, bf16[2,4,128,768]{3,2,1,0:T(8,128)(2,1)}, u32[]{:S(2)}, u32[]{:S(2)}) collective-permute-start(bf16[2,4,128,768]{3,2,1,0:T(8,128)(2,1)} %add_convert_fusion.1), channel_id=1, source_target_pairs={{0,16},{4,12},{8,24},{12,4},{16,0},{20,28},{24,8},{28,20},{1,17},{... | collective-permute-start | bytes 4718600 | tf_op jit(solution)/shard_map/ppermute | solution.py:1193
  314.0 26.2 %collective-permute-start.40 = (f32[96,128]{1,0:T(8,128)}, f32[96,128]{1,0:T(8,128)}, u32[]{:S(2)}, u32[]{:S(2)}) collective-permute-start(f32[96,128]{1,0:T(8,128)} %get-tuple-element.174), channel_id=1, source_target_pairs={{0,1},{1,0},{2,3},{3,2},{4,5},{5,4},{6,7},{7,6},{8,9},{9,8},{10,11... | collective-permute-start | bytes 147464 | tf_op jit(solution)/shard_map/ppermute | solution.py:1289
  318.0 22.2 %collective-permute-start.41 = (f32[96,128]{1,0:T(8,128)}, f32[96,128]{1,0:T(8,128)}, u32[]{:S(2)}, u32[]{:S(2)}) collective-permute-start(f32[96,128]{1,0:T(8,128)} %get-tuple-element.174), channel_id=1, source_target_pairs={{0,2},{1,3},{2,0},{3,1},{4,6},{5,7},{6,4},{7,5},{8,10},{9,11},{10,... | collective-permute-start | bytes 147464 | tf_op jit(solution)/shard_map/ppermute | solution.py:1289
  321.1 19.1 %collective-permute-start.42 = (f32[96,128]{1,0:T(8,128)S(1)}, f32[96,128]{1,0:T(8,128)S(1)}, u32[]{:S(2)}, u32[]{:S(2)}) collective-permute-start(f32[96,128]{1,0:T(8,128)S(1)} %copy-done.26), channel_id=1, source_target_pairs={{0,3},{1,2},{2,1},{3,0},{4,7},{5,6},{6,5},{7,4},{8,11},{9,10},{10,... | collective-permute-start | bytes 147464 | tf_op jit(solution)/shard_map/ppermute | solution.py:1289
  323.5 16.7 %collective-permute-start.36 = (bf16[4,128,768]{2,1,0:T(8,128)(2,1)}, bf16[4,128,768]{2,1,0:T(8,128)(2,1)}, u32[]{:S(2)}, u32[]{:S(2)}) collective-permute-start(bf16[4,128,768]{2,1,0:T(8,128)(2,1)} %fusion.1), channel_id=1, source_target_pairs={{0,8},{4,20},{8,0},{12,28},{16,24},{20,4},{24,16},{28,12},{1,9},{5... | collective-permute-start | bytes 2359304 | tf_op jit(solution)/shard_map/ppermute | solution.py:1193
  344.4 9.6 %collective-permute-start.50 = (bf16[128,768]{1,0:T(8,128)(2,1)S(1)}, bf16[128,768]{1,0:T(8,128)(2,1)S(1)}, u32[]{:S(2)}, u32[]{:S(2)}) collective-permute-start(bf16[128,768]{1,0:T(8,128)(2,1)S(1)} %get-tuple-element.183), channel_id=1, source_target_pairs={{0,1},{1,2},{2,3},{3,0},{4,5},{5,6},{6,7},{7,4},{8,9},{9,10},{10,1... | collective-permute-start | bytes 589832 | tf_op jit(solution)/shard_map/ppermute | solution.py:1197
  345.0 13.3 %collective-permute-start.51 = (bf16[128,768]{1,0:T(8,128)(2,1)S(1)}, bf16[128,768]{1,0:T(8,128)(2,1)S(1)}, u32[]{:S(2)}, u32[]{:S(2)}) collective-permute-start(bf16[128,768]{1,0:T(8,128)(2,1)S(1)} %get-tuple-element.184), channel_id=1, source_target_pairs={{0,2},{1,3},{2,0},{3,1},{4,6},{5,7},{6,4},{7,5},{8,10},{9,11},{10,... | collective-permute-start | bytes 589832 | tf_op jit(solution)/shard_map/ppermute | solution.py:1197
  346.4 12.7 %collective-permute-start.52 = (bf16[128,768]{1,0:T(8,128)(2,1)S(1)}, bf16[128,768]{1,0:T(8,128)(2,1)S(1)}, u32[]{:S(2)}, u32[]{:S(2)}) collective-permute-start(bf16[128,768]{1,0:T(8,128)(2,1)S(1)} %get-tuple-element.185), channel_id=1, source_target_pairs={{0,3},{1,0},{2,1},{3,2},{4,7},{5,4},{6,5},{7,6},{8,11},{9,8},{10,9... | collective-permute-start | bytes 589832 | tf_op jit(solution)/shard_map/ppermute | solution.py:1197
  351.2 8.8 %collective-permute-start.45 = (f32[96,128]{1,0:T(8,128)S(1)}, f32[96,128]{1,0:T(8,128)S(1)}, u32[]{:S(2)}, u32[]{:S(2)}) collective-permute-start(f32[96,128]{1,0:T(8,128)S(1)} %add_add_fusion.refs_0_), channel_id=1, source_target_pairs={{0,12},{4,8},{8,4},{12,0},{16,28},{20,24},{24,20},{28,16},{1,13},{... | collective-permute-start | bytes 147464 | tf_op jit(solution)/shard_map/ppermute | solution.py:1289
  352.5 7.5 %collective-permute-start.46 = (f32[96,128]{1,0:T(8,128)S(1)}, f32[96,128]{1,0:T(8,128)S(1)}, u32[]{:S(2)}, u32[]{:S(2)}) collective-permute-start(f32[96,128]{1,0:T(8,128)S(1)} %add_add_fusion.refs_0_), channel_id=1, source_target_pairs={{0,16},{4,20},{8,24},{12,28},{16,0},{20,4},{24,8},{28,12},{1,17},{... | collective-permute-start | bytes 147464 | tf_op jit(solution)/shard_map/ppermute | solution.py:1289
  354.0 6.0 %collective-permute-start.47 = (f32[96,128]{1,0:T(8,128)S(1)}, f32[96,128]{1,0:T(8,128)S(1)}, u32[]{:S(2)}, u32[]{:S(2)}) collective-permute-start(f32[96,128]{1,0:T(8,128)S(1)} %add_add_fusion.refs_0_), channel_id=1, source_target_pairs={{0,20},{4,16},{8,28},{12,24},{16,4},{20,0},{24,12},{28,8},{1,21},{... | collective-permute-start | bytes 147464 | tf_op jit(solution)/shard_map/ppermute | solution.py:1289
  (41 other events, 472.4 us)
Sparse Core Ops, SparseCore 0:
  28.7 34.1 all-gather.4
  67.4 25.0 all-gather.6
  165.8 70.9 reduce-scatter.2
  267.0 26.2 reduce-scatter.4

commit v2 on v1

--- a/solution.py
+++ b/solution.py
@@ -10,7 +10,7 @@
 HEADS = 16
 HEAD = 64
 TILE = 1024
-ROWS = 256
+ROWS = 512
 LOG2E = 1.4426950408889634
 MASKED = -1e30
 SCALE = HEAD ** (-0.5)
@@ -1051,8 +1051,14 @@
     total = tree_sum(terms)
     place = 0
     for out in (a, b, c, d, e, f, g, h):
-        out[...] = total[place : place + out.shape[0], :]
-        place += out.shape[0]
+        if out.shape[1] == 128:
+            out[...] = total[place : place + out.shape[0], :]
+            place += out.shape[0]
+            continue
+        for row in range(out.shape[0]):
+            for column in range(0, out.shape[1], 128):
+                out[row : row + 1, column : column + 128] = total[place : place + 1, :]
+                place += 1
 
 
 def small_call(terms):
@@ -1060,7 +1066,10 @@
     sizes = [unit, unit, 2 * unit, unit, unit, unit, unit, 4 * unit]
     return pl.pallas_call(
         small_kernel,
-        out_shape=[jax.ShapeDtypeStruct((size, 128), F32) for size in sizes],
+        out_shape=[
+            jax.ShapeDtypeStruct((size, 128) if n != 2 else (2, size * 64), F32)
+            for n, size in enumerate(sizes)
+        ],
         name="small",
     )(*terms)
 
@@ -1476,7 +1485,10 @@
         attend_parts = add_third(attend_keep, attend_core, attend_link, attend_last)
         attend_parts, small = after((attend_parts, small), back_owned, small, attend_parts)
         others = shift_parts(attend_parts)
-        small_terms = exchange(small, "dp", 8)
+        small = small + lax.ppermute(small, "dp", [(i, i ^ 1) for i in range(8)])
+        small_terms = [small] + [
+            lax.ppermute(small, "dp", [(i, i ^ flip) for i in range(8)]) for flip in (2, 4, 6)
+        ]
         attend_owned = added(attend_parts[0], *others)
         small = small_call(after(small_terms, attend_owned))
         down_owned = down_owned.astype(F32)
@@ -1499,7 +1511,7 @@
         output_owned = scatter_plain(back_grads[1:])
         attend_owned = scatter_plain(attend_grads)
         small = small_call([lax.psum(small, ("dp", "inner"))])
-    small = [vector.reshape(-1) for vector in small]
+    small = [vector if n == 2 else vector.reshape(-1) for n, vector in enumerate(small)]
 
     return (
         frames_out.reshape(frames_in.shape),
@@ -1507,7 +1519,7 @@
         small[0],
         small[1],
         attend_owned,
-        small[2].reshape(2, model),
+        small[2],
         output_owned,
         small[3],
         small[4],

time: 377 us -> 372 us (0.987)
    ppermute x10 -> x3, waiting for transfers between devices: 4.07 us -> 0.01 us  [exchange(): lax.ppermute(values, axis, [(i, i ^ flip) for i in range(size)])]
  transfers between devices with their start and end apart: 57 -> 54, of which waited for: 19 -> 17; matrix products, arithmetic and copies ran while one was open for 4% -> 4% of each run, Pallas kernels for 58% -> 59%
where the time goes in v2:
time: 372 us; the launch traced here: 368 us
  Pallas kernels  217 us (58%)
  waiting for transfers between devices  66.4 us (18%)
  starting transfers between devices  42.7 us (11%)
  other arithmetic  19.6 us (5%)
  between operations  15.1 us (4%)
  local copies, waits for them, and re-layouts  7.34 us (2%)
    ppermute x34, waiting for transfers between devices, swap(): return lax.ppermute(value, 'dp', [(d, d ^ flips[d & 1]) for d in range(8)])  48.6 us
    pallas_call x1, Pallas kernels, back_call(): pl.pallas_call(functools.partial(back_kernel, (len(out_pieces), len(up_pi...  47.5 us
    pallas_call x2, Pallas kernels, up_call(): pl.pallas_call(functools.partial(up_kernel, (len(up_pieces), len(earlier)...  38.6 us
    pallas_call x2, Pallas kernels, attention_back_call(): pl.pallas_call(functools.partial(attention_back_kernel, group, block), gr...  36.8 us
    pallas_call x2, Pallas kernels, attention_call(): pl.pallas_call(functools.partial(attention_kernel, group, block), grid=(s...  22.9 us
    ppermute x34, starting transfers between devices, swap(): return lax.ppermute(value, 'dp', [(d, d ^ flips[d & 1]) for d in range(8)])  22.1 us
    pallas_call x1, Pallas kernels, first_call(): pl.pallas_call(functools.partial(first_kernel, len(pieces)), grid_spec=gr...  15.8 us
    pallas_call x1, Pallas kernels, down_call(): pl.pallas_call(functools.partial(down_kernel, len(pieces), len(earlier),...  15.1 us
  transfers between devices with their start and end apart: 54, of which 17 were waited for; matrix products, arithmetic and copies ran while one was open for 4% of the time, Pallas kernels for 59%

profile of v2, /device:TPU:0, one launch (start us, length us, event | category | flops | bytes accessed | tf_op | source)
XLA Modules:
  0.0 368.4 jit_solution(6774662672680898457)
XLA Ops:
  7.2 3.0 collective-permute-start.3
  10.3 1.5 collective-permute-start.4
  11.8 1.6 collective-permute-start
  13.3 2.6 collective-permute-start.1
  18.2 1.7 pad_maximum_fusion.1
  20.0 1.7 collective-permute-done
  21.7 6.8 %collective-permute-done.1 = bf16[128,768]{1,0:T(8,128)(2,1)S(1)} collective-permute-done((bf16[128,768]{1,0:T(8,128)(2,1)}, bf16[128,768]{1,0:T(8,128)(2,1)S(1)}, u32[]{:S(2)}, u32[]{:S(2)}) %collective-permute-start.1) | collective-permute-done | bytes 196640 | tf_op jit(solution)/shard_map/ppermute | solution.py:1206
  29.7 14.3 %collective-permute-done.10.rest_9_ = bf16[3,128,768]{2,1,0:T(8,128)(2,1)S(1)} collective-permute-done((bf16[3,128,768]{2,1,0:T(8,128)(2,1)S(1)}, bf16[3,128,768]{2,1,0:T(8,128)(2,1)S(1)}, u32[]{:S(2)}, u32[]{:S(2)}) %collective-permute-start.10) | collective-permute-done | bytes 589856 | tf_op jit(solution)/shard_map/ppermute | solution.py:1202
  47.5 6.6 %collective-permute-done.12.rest_11_ = bf16[3,128,768]{2,1,0:T(8,128)(2,1)S(1)} collective-permute-done((bf16[3,128,768]{2,1,0:T(8,128)(2,1)S(1)}, bf16[3,128,768]{2,1,0:T(8,128)(2,1)S(1)}, u32[]{:S(2)}, u32[]{:S(2)}) %collective-permute-start.12) | collective-permute-done | bytes 589856 | tf_op jit(solution)/shard_map/ppermute | solution.py:1202
  54.6 1.8 collective-permute-done.8.rest_6_
  59.5 3.4 all-gather.5.cloned.1.call-done
  62.9 1.5 collective-permute-start.17
  64.4 1.5 collective-permute-start.18
  68.2 12.9 %project.1 = (bf16[1024,1024]{1,0:T(8,128)(2,1)}, bf16[3072,1024]{1,0:T(8,128)(2,1)}) custom-call(s32[48]{0:T(128)} %stack.183.tab, bf16[1024,1024]{1,0:T(8,128)(2,1)} %bitcast.81, f32[1,1024]{1,0:T(1,128)} %bitcast.106, f32[1,1024]{1,0:T(1,128)} %bitcast.101, f32[1,3072]{1,0:T(1,128)} %bitcast.98, bf16[128,768]{1,0:T(8,128)(2,1)} %rest_0_.3, ...), custom_call_target="tpu_custom_call" | custom-call | flops 8000000 | bytes 80000 | tf_op jit(solution)/shard_map/project/pallas_call | solution.py:309
  81.1 11.5 %attention.2 = (bf16[1024,1024]{1,0:T(8,128)(2,1)}, f32[8,2,1024]{2,1,0:T(2,128)}) custom-call(s32[1]{0:T(128)S(6)} %copy.41.lengths, bf16[3072,1024]{1,0:T(8,128)(2,1)} %get-tuple-element.118.query.key.value, bf16[3072,1024]{1,0:T(8,128)(2,1)} %get-tuple-element.118.query.key.value, bf16[3072,1024]{1,0:T(8,128)(2,1)} %get-tuple-element.118.query.key.value), custom_call_target="tpu_custom_call" | custom-call | flops 42949672 | bytes 64000 | tf_op jit(solution)/shard_map/attention/pallas_call | solution.py:396
  92.6 1.6 collective-permute-done.17.rest_1_.rest_2_.rest_10_
  95.5 11.4 %attention.3 = (bf16[1024,1024]{1,0:T(8,128)(2,1)}, f32[8,2,1024]{2,1,0:T(2,128)}) custom-call(s32[1]{0:T(128)S(6)} %copy.41.lengths, bf16[3072,1024]{1,0:T(8,128)(2,1)} %get-tuple-element.118.query.key.value, bf16[3072,1024]{1,0:T(8,128)(2,1)} %get-tuple-element.118.query.key.value, ...), custom_call_target="tpu_custom_call", output_to_operand_aliasing={{0}: (4, {}), {1}: (5, {})} | custom-call | flops 42949672 | bytes 64000 | tf_op jit(solution)/shard_map/attention/pallas_call | solution.py:396
  106.9 5.0 %collective-permute-done.19.rest_3_.rest_4_.rest_12_ = bf16[4,128,1280]{2,1,0:T(8,128)(2,1)} collective-permute-done((bf16[4,128,1280]{2,1,0:T(8,128)(2,1)S(1)}, bf16[4,128,1280]{2,1,0:T(8,128)(2,1)}, u32[]{:S(2)}, u32[]{:S(2)}) %collective-permute-start.19) | collective-permute-done | bytes 1310752 | tf_op jit(solution)/shard_map/ppermute | solution.py:1202
  112.6 1.5 collective-permute-start.24
  115.3 9.7 %out.1 = (f32[1024,1024]{1,0:T(8,128)}, bf16[1024,1024]{1,0:T(8,128)(2,1)}, bf16[1024,1024]{1,0:T(8,128)(2,1)}, f32[1,1024]{1,0:T(1,128)}) custom-call(s32[48]{0:T(128)} %stack.178.tab, s32[1]{0:T(128)S(6)} %copy.41.lengths, bf16[1024,1024]{1,0:T(8,128)(2,1)} %get-tuple-element.120.mixture, bf16[1024,1024]{1,0:T(8,128)(2,1)} %bitcast.82, ...), custom_call_target="tpu_custom_call" | custom-call | flops 8 | bytes 8 | tf_op jit(solution)/shard_map/out/pallas_call | solution.py:468
  125.0 19.6 %up.2 = (bf16[1024,4096]{1,0:T(8,128)(2,1)}, bf16[1024,4096]{1,0:T(8,128)(2,1)}, bf16[4096,1024]{1,0:T(8,128)(2,1)}) custom-call(s32[48]{0:T(128)} %stack.178.tab, bf16[1024,1024]{1,0:T(8,128)(2,1)} %get-tuple-element.130.normed, bf16[1024,1024]{1,0:T(8,128)(2,1)} %get-tuple-element.125.result.d_result, f32[1,4096]{1,0:T(1,128)} %bitcast.113, ...), custom_call_target="tpu_custom_call" | custom-call | flops 68719476736 | bytes 400000000 | tf_op jit(solution)/shard_map/up/pallas_call | solution.py:564
  146.1 18.9 %up.3 = (bf16[1024,4096]{1,0:T(8,128)(2,1)}, bf16[1024,4096]{1,0:T(8,128)(2,1)}, bf16[4096,1024]{1,0:T(8,128)(2,1)}) custom-call(s32[48]{0:T(128)} %stack.178.tab, bf16[1024,1024]{1,0:T(8,128)(2,1)} %get-tuple-element.130.normed, ...), custom_call_target="tpu_custom_call", output_to_operand_aliasing={{0}: (12, {}), {1}: (13, {}), {2}: (14, {})} | custom-call | flops 68719476736 | bytes 400000000 | tf_op jit(solution)/shard_map/up/pallas_call | solution.py:564
  166.1 1.9 collective-permute-done.30.rest_24_.rest_7_
  168.0 47.5 %back.1 = (f32[1024,1024]{1,0:T(8,128)}, bf16[1024,1024]{1,0:T(8,128)(2,1)}, f32[1,4096]{1,0:T(1,128)}, f32[1,1024]{1,0:T(1,128)}, f32[1,1024]{1,0:T(1,128)}, /*...) custom-call(s32[48]{0:T(128)} %stack.178.tab, ...), custom_call_target="tpu_custom_call" | custom-call | flops 240518168576 | bytes 480000000 | tf_op jit(solution)/shard_map/back/pallas_call | solution.py:806
  216.2 10.3 %attention_back.2.rest_0_ = bf16[3,1024,1024]{2,1,0:T(8,128)(2,1)} custom-call(s32[1]{0:T(128)S(6)} %copy.41.lengths, bf16[3072,1024]{1,0:T(8,128)(2,1)} %get-tuple-element.118.query.key.value, bf16[3072,1024]{1,0:T(8,128)(2,1)} %get-tuple-element.118.query.key.value, bf16[3072,1024]{1,0:T(8,128)(2,1)} %get-tuple-element.118.query.key.value, ...), custom_call_target="tpu_custom_call" | custom-call | flops 5368709120 | bytes 8000000 | tf_op jit(solution)/shard_map/attention_back/pallas_call | solution.py:906
  226.5 3.2 add_convert_fusion
  229.8 26.5 %attention_back.3 = bf16[3,1024,1024]{2,1,0:T(8,128)(2,1)} custom-call(s32[1]{0:T(128)S(6)} %copy.41.lengths, bf16[3072,1024]{1,0:T(8,128)(2,1)} %get-tuple-element.118.query.key.value, bf16[3072,1024]{1,0:T(8,128)(2,1)} %get-tuple-element.118.query.key.value, bf16[3072,1024]{1,0:T(8,128)(2,1)} %get-tuple-element.118.query.key.value, ...), custom_call_target="tpu_custom_call", output_to_operand_aliasing={{}: (7, {})} | custom-call | flops 16106127360 | bytes 8000000 | tf_op jit(solution)/shard_map/attention_back/pallas_call | solution.py:906
  256.3 6.2 %collective-permute-done.32.refs_2_ = bf16[2,4,128,1280]{3,2,1,0:T(8,128)(2,1)} collective-permute-done((bf16[2,4,128,1280]{3,2,1,0:T(8,128)(2,1)S(1)}, bf16[2,4,128,1280]{3,2,1,0:T(8,128)(2,1)}, u32[]{:S(2)}, u32[]{:S(2)}) %collective-permute-start.32) | collective-permute-done | bytes 2621472 | tf_op jit(solution)/shard_map/ppermute | solution.py:1202
  262.6 2.6 fusion
  265.1 1.5 collective-permute-start.34
  266.7 11.6 %attend_grad.1 = (f32[1,3072]{1,0:T(1,128)}, bf16[4,4,128,768]{3,2,1,0:T(8,128)(2,1)}, bf16[4,4,128,768]{3,2,1,0:T(8,128)(2,1)}) custom-call(s32[48]{0:T(128)} %stack.183.tab, bf16[3072,1024]{1,0:T(8,128)(2,1)} %bitcast.84, bf16[1024,1024]{1,0:T(8,128)(2,1)} %get-tuple-element.146.normed), custom_call_target="tpu_custom_call" | custom-call | flops 51539607552 | bytes 112000000 | tf_op jit(solution)/shard_map/attend_grad/pallas_call | solution.py:966
  278.4 4.4 %collective-permute-done.34.refs_3_ = bf16[4,128,1280]{2,1,0:T(8,128)(2,1)S(1)} collective-permute-done((bf16[4,128,1280]{2,1,0:T(8,128)(2,1)S(1)}, bf16[4,128,1280]{2,1,0:T(8,128)(2,1)S(1)}, u32[]{:S(2)}, u32[]{:S(2)}) %collective-permute-start.34) | collective-permute-done | bytes 1310752 | tf_op jit(solution)/shard_map/ppermute | solution.py:1202
  283.9 5.0 %add.187 = (f32[128,1280]{1,0:T(8,128)}, bf16[128,1280]{1,0:T(8,128)(2,1)}, bf16[128,1280]{1,0:T(8,128)(2,1)}, bf16[128,1280]{1,0:T(8,128)(2,1)}) custom-call(bf16[4,4,128,1280]{3,2,1,0:T(8,128)(2,1)} %get-tuple-element.138.refs_0_, bf16[4,4,128,1280]{3,2,1,0:T(8,128)(2,1)} %collective-permute-done.31.refs_1_, ...), custom_call_target="tpu_custom_call" | custom-call | flops 80000000000 | bytes 80000000 | tf_op jit(solution)/shard_map/add/pallas_call | solution.py:1261
  288.9 1.5 collective-permute-start.37
  290.3 2.4 collective-permute-start.38
  294.2 2.9 add_convert_fusion.1
  297.7 15.8 %first.1 = (bf16[1024,1024]{1,0:T(8,128)(2,1)}, f32[96,128]{1,0:T(8,128)}) custom-call(s32[48]{0:T(128)} %stack.183.tab, bf16[3072,1024]{1,0:T(8,128)(2,1)} %bitcast.85, bf16[1024,1024]{1,0:T(8,128)(2,1)} %bitcast.83, f32[1024,1024]{1,0:T(8,128)} %get-tuple-element.157.d_middle, f32[1,1024]{1,0:T(1,128)} %bitcast.107, bf16[128,768]{1,0:T(8,128)(2,1)} %rest_0_.3, ...), custom_call_target="tpu_custom_call" | custom-call | flops 51539607552 | bytes 192000000 | tf_op jit(solution)/shard_map/first/pallas_call | solution.py:1097
  314.1 3.7 %collective-permute-done.35 = bf16[2,4,128,768]{3,2,1,0:T(8,128)(2,1)} collective-permute-done((bf16[2,4,128,768]{3,2,1,0:T(8,128)(2,1)}, bf16[2,4,128,768]{3,2,1,0:T(8,128)(2,1)}, u32[]{:S(2)}, u32[]{:S(2)}) %collective-permute-start.35) | collective-permute-done | bytes 1572896 | tf_op jit(solution)/shard_map/ppermute | solution.py:1202
  318.4 2.5 fusion.1
  320.9 2.4 collective-permute-start.42
  323.4 1.5 collective-permute-start.36
  324.8 15.1 %down.1 = bf16[1024,1024]{1,0:T(8,128)(2,1)} custom-call(s32[48]{0:T(128)} %stack.178.tab, bf16[1024,4096]{1,0:T(8,128)(2,1)} %get-tuple-element.166.active, f32[1024,1024]{1,0:T(8,128)} %get-tuple-element.167.middle, f32[1,1024]{1,0:T(1,128)} %bitcast.116, bf16[4,512,256]{2,1,0:T(8,128)(2,1)} %bitcast.112, ...), custom_call_target="tpu_custom_call" | custom-call | flops 68719476736 | bytes 192000000 | tf_op jit(solution)/shard_map/down/pallas_call | solution.py:1176
  340.0 2.1 fusion.2
  344.8 1.4 collective-permute-start.48
  346.2 1.8 collective-permute-start.49
  351.6 2.2 collective-permute-done.47
  354.5 3.6 collective-permute-done.48
  360.2 1.5 small.1
  (155 shorter events, 31.8 us)
Async XLA Ops:
  7.2 55.7 %all-gather.5.cloned.1.call-start = ((), (), s32[]{:S(2)}) async-start(), calls=%async_computation.4 | async-start | bytes 1638400 | tf_op jit(solution)/shard_map/all_gather | solution.py:1354
  7.2 10.0 %collective-permute-start.3 = (bf16[128,768]{1,0:T(8,128)(2,1)}, bf16[128,768]{1,0:T(8,128)(2,1)S(1)}, u32[]{:S(2)}, u32[]{:S(2)}) collective-permute-start(bf16[128,768]{1,0:T(8,128)(2,1)} %rest_0_.3), channel_id=1, source_target_pairs={{0,16},{4,12},{8,24},{12,4},{16,0},{20,28},{24,8},{28,20},{1,17},{... | collective-permute-start | bytes 589832 | tf_op jit(solution)/shard_map/ppermute | solution.py:1202
  10.3 7.0 %collective-permute-start.4 = (bf16[128,768]{1,0:T(8,128)(2,1)}, bf16[128,768]{1,0:T(8,128)(2,1)S(1)}, u32[]{:S(2)}, u32[]{:S(2)}) collective-permute-start(bf16[128,768]{1,0:T(8,128)(2,1)} %rest_0_.3), channel_id=1, source_target_pairs={{0,8},{4,20},{8,0},{12,28},{16,24},{20,4},{24,16},{28,12},{1,9},{5... | collective-permute-start | bytes 589832 | tf_op jit(solution)/shard_map/ppermute | solution.py:1202
  11.8 9.9 %collective-permute-start = (bf16[128,768]{1,0:T(8,128)(2,1)}, bf16[128,768]{1,0:T(8,128)(2,1)S(1)}, u32[]{:S(2)}, u32[]{:S(2)}) collective-permute-start(bf16[128,768]{1,0:T(8,128)(2,1)} %rest_0_.3), channel_id=1, source_target_pairs={{0,1},{1,2},{2,3},{3,0},{4,5},{5,6},{6,7},{7,4},{8,9},{9,10},{10,1... | collective-permute-start | bytes 589832 | tf_op jit(solution)/shard_map/ppermute | solution.py:1206
  13.3 15.1 %collective-permute-start.1 = (bf16[128,768]{1,0:T(8,128)(2,1)}, bf16[128,768]{1,0:T(8,128)(2,1)S(1)}, u32[]{:S(2)}, u32[]{:S(2)}) collective-permute-start(bf16[128,768]{1,0:T(8,128)(2,1)} %rest_0_.3), channel_id=1, source_target_pairs={{0,2},{1,3},{2,0},{3,1},{4,6},{5,7},{6,4},{7,5},{8,10},{9,11},{10,... | collective-permute-start | bytes 589832 | tf_op jit(solution)/shard_map/ppermute | solution.py:1206
  15.9 12.5 %collective-permute-start.2 = (bf16[128,768]{1,0:T(8,128)(2,1)}, bf16[128,768]{1,0:T(8,128)(2,1)S(1)}, u32[]{:S(2)}, u32[]{:S(2)}) collective-permute-start(bf16[128,768]{1,0:T(8,128)(2,1)} %rest_0_.3), channel_id=1, source_target_pairs={{0,3},{1,0},{2,1},{3,2},{4,7},{5,4},{6,5},{7,6},{8,11},{9,8},{10,9... | collective-permute-start | bytes 589832 | tf_op jit(solution)/shard_map/ppermute | solution.py:1206
  17.3 11.3 %collective-permute-start.5 = (bf16[128,768]{1,0:T(8,128)(2,1)S(1)}, bf16[128,768]{1,0:T(8,128)(2,1)S(1)}, u32[]{:S(2)}, u32[]{:S(2)}) collective-permute-start(bf16[128,768]{1,0:T(8,128)(2,1)S(1)} %collective-permute-done.4.rest_1_), channel_id=1, source_target_pairs={{0,16},{4,12},{8,24},{12,4},{16,0},{20,28},{24,8},{28,20},{1,17},{... | collective-permute-start | bytes 589832 | tf_op jit(solution)/shard_map/ppermute | solution.py:1202
  28.6 66.9 %all-gather.7.cloned.1.call-start = ((), (), s32[]{:S(2)}) async-start(), calls=%async_computation.5 | async-start | bytes 1310720 | tf_op jit(solution)/shard_map/all_gather | solution.py:1361
  28.6 15.4 %collective-permute-start.10 = (bf16[3,128,768]{2,1,0:T(8,128)(2,1)S(1)}, bf16[3,128,768]{2,1,0:T(8,128)(2,1)S(1)}, u32[]{:S(2)}, u32[]{:S(2)}) collective-permute-start(bf16[3,128,768]{2,1,0:T(8,128)(2,1)S(1)} %pad_maximum_fusion.rest_8_), channel_id=1, source_target_pairs={{0,8},{4,20},{8,0},{12,28},{16,24},{20,4},{24,16},{28,12},{1,9},{5... | collective-permute-start | bytes 1769480 | tf_op jit(solution)/shard_map/ppermute | solution.py:1202
  29.2 14.9 %collective-permute-start.11 = (bf16[3,128,768]{2,1,0:T(8,128)(2,1)S(1)}, bf16[3,128,768]{2,1,0:T(8,128)(2,1)S(1)}, u32[]{:S(2)}, u32[]{:S(2)}) collective-permute-start(bf16[3,128,768]{2,1,0:T(8,128)(2,1)S(1)} %pad_maximum_fusion.rest_8_), channel_id=1, source_target_pairs={{0,16},{4,12},{8,24},{12,4},{16,0},{20,28},{24,8},{28,20},{1,17},{... | collective-permute-start | bytes 1769480 | tf_op jit(solution)/shard_map/ppermute | solution.py:1202
  44.1 9.9 %collective-permute-start.12 = (bf16[3,128,768]{2,1,0:T(8,128)(2,1)S(1)}, bf16[3,128,768]{2,1,0:T(8,128)(2,1)S(1)}, u32[]{:S(2)}, u32[]{:S(2)}) collective-permute-start(bf16[3,128,768]{2,1,0:T(8,128)(2,1)S(1)} %collective-permute-done.10.rest_9_), channel_id=1, source_target_pairs={{0,16},{4,12},{8,24},{12,4},{16,0},{20,28},{24,8},{28,20},{1,17},{... | collective-permute-start | bytes 1769480 | tf_op jit(solution)/shard_map/ppermute | solution.py:1202
  45.3 8.8 %collective-permute-start.7 = (bf16[128,768]{1,0:T(8,128)(2,1)S(1)}, bf16[128,768]{1,0:T(8,128)(2,1)S(1)}, u32[]{:S(2)}, u32[]{:S(2)}) collective-permute-start(bf16[128,768]{1,0:T(8,128)(2,1)S(1)} %collective-permute-done.4.rest_1_), channel_id=1, source_target_pairs={{0,4},{4,0},{8,12},{12,8},{16,20},{20,16},{24,28},{28,24},{1,5},{5... | collective-permute-start | bytes 589832 | tf_op jit(solution)/shard_map/ppermute | solution.py:1202
  45.8 12.0 %collective-permute-start.13 = (bf16[3,128,768]{2,1,0:T(8,128)(2,1)S(1)}, bf16[3,128,768]{2,1,0:T(8,128)(2,1)S(1)}, u32[]{:S(2)}, u32[]{:S(2)}) collective-permute-start(bf16[3,128,768]{2,1,0:T(8,128)(2,1)S(1)} %pad_maximum_fusion.rest_8_), channel_id=1, source_target_pairs={{0,4},{4,0},{8,12},{12,8},{16,20},{20,16},{24,28},{28,24},{1,5},{5... | collective-permute-start | bytes 1769480 | tf_op jit(solution)/shard_map/ppermute | solution.py:1202
  45.8 12.0 %collective-permute-start.14 = (bf16[3,128,768]{2,1,0:T(8,128)(2,1)S(1)}, bf16[3,128,768]{2,1,0:T(8,128)(2,1)S(1)}, u32[]{:S(2)}, u32[]{:S(2)}) collective-permute-start(bf16[3,128,768]{2,1,0:T(8,128)(2,1)S(1)} %collective-permute-done.10.rest_9_), channel_id=1, source_target_pairs={{0,4},{4,0},{8,12},{12,8},{16,20},{20,16},{24,28},{28,24},{1,5},{5... | collective-permute-start | bytes 1769480 | tf_op jit(solution)/shard_map/ppermute | solution.py:1202
  47.3 10.5 %collective-permute-start.15 = (bf16[3,128,768]{2,1,0:T(8,128)(2,1)S(1)}, bf16[3,128,768]{2,1,0:T(8,128)(2,1)S(1)}, u32[]{:S(2)}, u32[]{:S(2)}) collective-permute-start(bf16[3,128,768]{2,1,0:T(8,128)(2,1)S(1)} %collective-permute-done.11.rest_10_), channel_id=1, source_target_pairs={{0,4},{4,0},{8,12},{12,8},{16,20},{20,16},{24,28},{28,24},{1,5},{5... | collective-permute-start | bytes 1769480 | tf_op jit(solution)/shard_map/ppermute | solution.py:1202
  54.0 5.4 %collective-permute-start.16 = (bf16[3,128,768]{2,1,0:T(8,128)(2,1)S(1)}, bf16[3,128,768]{2,1,0:T(8,128)(2,1)}, u32[]{:S(2)}, u32[]{:S(2)}) collective-permute-start(bf16[3,128,768]{2,1,0:T(8,128)(2,1)S(1)} %collective-permute-done.12.rest_11_), channel_id=1, source_target_pairs={{0,4},{4,0},{8,12},{12,8},{16,20},{20,16},{24,28},{28,24},{1,5},{5... | collective-permute-start | bytes 1769480 | tf_op jit(solution)/shard_map/ppermute | solution.py:1202
  62.9 31.3 %collective-permute-start.17 = (bf16[4,128,1280]{2,1,0:T(8,128)(2,1)}, bf16[4,128,1280]{2,1,0:T(8,128)(2,1)S(1)}, u32[]{:S(2)}, u32[]{:S(2)}) collective-permute-start(bf16[4,128,1280]{2,1,0:T(8,128)(2,1)} %bitcast.87), channel_id=1, source_target_pairs={{0,8},{4,20},{8,0},{12,28},{16,24},{20,4},{24,16},{28,12},{1,9},{5... | collective-permute-start | bytes 3932168 | tf_op jit(solution)/shard_map/ppermute | solution.py:1202
  64.4 29.8 %collective-permute-start.18 = (bf16[4,128,1280]{2,1,0:T(8,128)(2,1)}, bf16[4,128,1280]{2,1,0:T(8,128)(2,1)}, u32[]{:S(2)}, u32[]{:S(2)}) collective-permute-start(bf16[4,128,1280]{2,1,0:T(8,128)(2,1)} %bitcast.88), channel_id=1, source_target_pairs={{0,16},{4,12},{8,24},{12,4},{16,0},{20,28},{24,8},{28,20},{1,17},{... | collective-permute-start | bytes 3932168 | tf_op jit(solution)/shard_map/ppermute | solution.py:1202
  67.2 195.3 %reduce-scatter.3.cloned.1.call-start = ((), (), s32[]{:S(2)}) async-start(), calls=%async_computation.2 | async-start | bytes 9437184 | tf_op jit(solution)/shard_map/reduce_scatter | solution.py:1417
  94.2 17.7 %collective-permute-start.19 = (bf16[4,128,1280]{2,1,0:T(8,128)(2,1)S(1)}, bf16[4,128,1280]{2,1,0:T(8,128)(2,1)}, u32[]{:S(2)}, u32[]{:S(2)}) collective-permute-start(bf16[4,128,1280]{2,1,0:T(8,128)(2,1)S(1)} %collective-permute-done.17.rest_1_.rest_2_.rest_10_), channel_id=1, source_target_pairs={{0,16},{4,12},{8,24},{12,4},{16,0},{20,28},{24,8},{28,20},{1,17},{... | collective-permute-start | bytes 3932168 | tf_op jit(solution)/shard_map/ppermute | solution.py:1202
  94.8 19.3 %collective-permute-start.20 = (bf16[4,128,1280]{2,1,0:T(8,128)(2,1)S(1)}, bf16[4,128,1280]{2,1,0:T(8,128)(2,1)}, u32[]{:S(2)}, u32[]{:S(2)}) collective-permute-start(bf16[4,128,1280]{2,1,0:T(8,128)(2,1)S(1)} %bitcast.94), channel_id=1, source_target_pairs={{0,4},{4,0},{8,12},{12,8},{16,20},{20,16},{24,28},{28,24},{1,5},{5... | collective-permute-start | bytes 3932168 | tf_op jit(solution)/shard_map/ppermute | solution.py:1202
  94.9 19.7 %collective-permute-start.21 = (bf16[4,128,1280]{2,1,0:T(8,128)(2,1)S(1)}, bf16[4,128,1280]{2,1,0:T(8,128)(2,1)}, u32[]{:S(2)}, u32[]{:S(2)}) collective-permute-start(bf16[4,128,1280]{2,1,0:T(8,128)(2,1)S(1)} %collective-permute-done.17.rest_1_.rest_2_.rest_10_), channel_id=1, source_target_pairs={{0,4},{4,0},{8,12},{12,8},{16,20},{20,16},{24,28},{28,24},{1,5},{5... | collective-permute-start | bytes 3932168 | tf_op jit(solution)/shard_map/ppermute | solution.py:1202
  95.3 19.4 %collective-permute-start.22 = (bf16[4,128,1280]{2,1,0:T(8,128)(2,1)}, bf16[4,128,1280]{2,1,0:T(8,128)(2,1)}, u32[]{:S(2)}, u32[]{:S(2)}) collective-permute-start(bf16[4,128,1280]{2,1,0:T(8,128)(2,1)} %collective-permute-done.18.rest_2_.rest_3_.rest_11_), channel_id=1, source_target_pairs={{0,4},{4,0},{8,12},{12,8},{16,20},{20,16},{24,28},{28,24},{1,5},{5... | collective-permute-start | bytes 3932168 | tf_op jit(solution)/shard_map/ppermute | solution.py:1202
  112.6 32.0 %collective-permute-start.24 = (bf16[4,512,256]{2,1,0:T(8,128)(2,1)}, bf16[4,512,256]{2,1,0:T(8,128)(2,1)}, u32[]{:S(2)}, u32[]{:S(2)}) collective-permute-start(bf16[4,512,256]{2,1,0:T(8,128)(2,1)} %bitcast.108), channel_id=1, source_target_pairs={{0,8},{4,20},{8,0},{12,28},{16,24},{20,4},{24,16},{28,12},{1,9},{5... | collective-permute-start | bytes 3145736 | tf_op jit(solution)/shard_map/ppermute | solution.py:1202
  114.1 30.5 %collective-permute-start.25 = (bf16[4,512,256]{2,1,0:T(8,128)(2,1)}, bf16[4,512,256]{2,1,0:T(8,128)(2,1)S(1)}, u32[]{:S(2)}, u32[]{:S(2)}) collective-permute-start(bf16[4,512,256]{2,1,0:T(8,128)(2,1)} %bitcast.109), channel_id=1, source_target_pairs={{0,16},{4,12},{8,24},{12,4},{16,0},{20,28},{24,8},{28,20},{1,17},{... | collective-permute-start | bytes 3145736 | tf_op jit(solution)/shard_map/ppermute | solution.py:1202
  114.7 51.4 %collective-permute-start.27 = (bf16[4,512,256]{2,1,0:T(8,128)(2,1)}, bf16[4,512,256]{2,1,0:T(8,128)(2,1)S(1)}, u32[]{:S(2)}, u32[]{:S(2)}) collective-permute-start(bf16[4,512,256]{2,1,0:T(8,128)(2,1)} %bitcast.110), channel_id=1, source_target_pairs={{0,4},{4,0},{8,12},{12,8},{16,20},{20,16},{24,28},{28,24},{1,5},{5... | collective-permute-start | bytes 3145736 | tf_op jit(solution)/shard_map/ppermute | solution.py:1202
  144.6 20.4 %collective-permute-start.26 = (bf16[4,512,256]{2,1,0:T(8,128)(2,1)}, bf16[4,512,256]{2,1,0:T(8,128)(2,1)S(1)}, u32[]{:S(2)}, u32[]{:S(2)}) collective-permute-start(bf16[4,512,256]{2,1,0:T(8,128)(2,1)} %collective-permute-done.24.rest_18_.rest_1_), channel_id=1, source_target_pairs={{0,16},{4,12},{8,24},{12,4},{16,0},{20,28},{24,8},{28,20},{1,17},{... | collective-permute-start | bytes 3145736 | tf_op jit(solution)/shard_map/ppermute | solution.py:1202
  145.6 20.5 %collective-permute-start.28 = (bf16[4,512,256]{2,1,0:T(8,128)(2,1)}, bf16[4,512,256]{2,1,0:T(8,128)(2,1)}, u32[]{:S(2)}, u32[]{:S(2)}) collective-permute-start(bf16[4,512,256]{2,1,0:T(8,128)(2,1)} %collective-permute-done.24.rest_18_.rest_1_), channel_id=1, source_target_pairs={{0,4},{4,0},{8,12},{12,8},{16,20},{20,16},{24,28},{28,24},{1,5},{5... | collective-permute-start | bytes 3145736 | tf_op jit(solution)/shard_map/ppermute | solution.py:1202
  146.0 20.0 %collective-permute-start.29 = (bf16[4,512,256]{2,1,0:T(8,128)(2,1)S(1)}, bf16[4,512,256]{2,1,0:T(8,128)(2,1)}, u32[]{:S(2)}, u32[]{:S(2)}) collective-permute-start(bf16[4,512,256]{2,1,0:T(8,128)(2,1)S(1)} %collective-permute-done.25.rest_19_.rest_2_), channel_id=1, source_target_pairs={{0,4},{4,0},{8,12},{12,8},{16,20},{20,16},{24,28},{28,24},{1,5},{5... | collective-permute-start | bytes 3145736 | tf_op jit(solution)/shard_map/ppermute | solution.py:1202
  166.0 152.4 %reduce-scatter.5.cloned.1.call-start = ((), (), s32[]{:S(2)}) async-start(), calls=%async_computation.3 | async-start | bytes 1310720 | tf_op jit(solution)/shard_map/reduce_scatter | solution.py:1453
  215.5 11.0 %collective-permute-start.31 = (bf16[4,4,128,1280]{3,2,1,0:T(8,128)(2,1)}, bf16[4,4,128,1280]{3,2,1,0:T(8,128)(2,1)}, u32[]{:S(2)}, u32[]{:S(2)}) collective-permute-start(bf16[4,4,128,1280]{3,2,1,0:T(8,128)(2,1)} %get-tuple-element.139), channel_id=1, source_target_pairs={{0,4},{4,0},{8,12},{12,8},{16,20},{20,16},{24,28},{28,24},{1,5},{5... | collective-permute-start | bytes 15728648 | tf_op jit(solution)/shard_map/ppermute | solution.py:1202
  229.7 32.8 %collective-permute-start.32 = (bf16[2,4,128,1280]{3,2,1,0:T(8,128)(2,1)S(1)}, bf16[2,4,128,1280]{3,2,1,0:T(8,128)(2,1)}, u32[]{:S(2)}, u32[]{:S(2)}) collective-permute-start(bf16[2,4,128,1280]{3,2,1,0:T(8,128)(2,1)S(1)} %add_convert_fusion), channel_id=1, source_target_pairs={{0,16},{4,12},{8,24},{12,4},{16,0},{20,28},{24,8},{28,20},{1,17},{... | collective-permute-start | bytes 7864328 | tf_op jit(solution)/shard_map/ppermute | solution.py:1202
  265.1 17.7 %collective-permute-start.34 = (bf16[4,128,1280]{2,1,0:T(8,128)(2,1)S(1)}, bf16[4,128,1280]{2,1,0:T(8,128)(2,1)S(1)}, u32[]{:S(2)}, u32[]{:S(2)}) collective-permute-start(bf16[4,128,1280]{2,1,0:T(8,128)(2,1)S(1)} %fusion), channel_id=1, source_target_pairs={{0,8},{4,20},{8,0},{12,28},{16,24},{20,4},{24,16},{28,12},{1,9},{5... | collective-permute-start | bytes 3932168 | tf_op jit(solution)/shard_map/ppermute | solution.py:1202
  278.4 15.8 %collective-permute-start.33 = (bf16[4,4,128,768]{3,2,1,0:T(8,128)(2,1)}, bf16[4,4,128,768]{3,2,1,0:T(8,128)(2,1)}, u32[]{:S(2)}, u32[]{:S(2)}) collective-permute-start(bf16[4,4,128,768]{3,2,1,0:T(8,128)(2,1)} %get-tuple-element.148), channel_id=1, source_target_pairs={{0,4},{4,0},{8,12},{12,8},{16,20},{20,16},{24,28},{28,24},{1,5},{5... | collective-permute-start | bytes 9437192 | tf_op jit(solution)/shard_map/ppermute | solution.py:1202
  288.9 32.1 %collective-permute-start.37 = (bf16[128,1280]{1,0:T(8,128)(2,1)}, bf16[128,1280]{1,0:T(8,128)(2,1)S(1)}, u32[]{:S(2)}, u32[]{:S(2)}) collective-permute-start(bf16[128,1280]{1,0:T(8,128)(2,1)} %get-tuple-element.152), channel_id=1, source_target_pairs={{0,1},{1,2},{2,3},{3,0},{4,5},{5,6},{6,7},{7,4},{8,9},{9,10},{10,1... | collective-permute-start | bytes 983048 | tf_op jit(solution)/shard_map/ppermute | solution.py:1206
  290.3 33.0 %collective-permute-start.38 = (bf16[128,1280]{1,0:T(8,128)(2,1)}, bf16[128,1280]{1,0:T(8,128)(2,1)}, u32[]{:S(2)}, u32[]{:S(2)}) collective-permute-start(bf16[128,1280]{1,0:T(8,128)(2,1)} %get-tuple-element.153), channel_id=1, source_target_pairs={{0,2},{1,3},{2,0},{3,1},{4,6},{5,7},{6,4},{7,5},{8,10},{9,11},{10,... | collective-permute-start | bytes 983048 | tf_op jit(solution)/shard_map/ppermute | solution.py:1206
  292.7 47.2 %collective-permute-start.39 = (bf16[128,1280]{1,0:T(8,128)(2,1)}, bf16[128,1280]{1,0:T(8,128)(2,1)}, u32[]{:S(2)}, u32[]{:S(2)}) collective-permute-start(bf16[128,1280]{1,0:T(8,128)(2,1)} %get-tuple-element.154), channel_id=1, source_target_pairs={{0,3},{1,0},{2,1},{3,2},{4,7},{5,4},{6,5},{7,6},{8,11},{9,8},{10,9... | collective-permute-start | bytes 983048 | tf_op jit(solution)/shard_map/ppermute | solution.py:1206
  297.1 20.7 %collective-permute-start.35 = (bf16[2,4,128,768]{3,2,1,0:T(8,128)(2,1)}, bf16[2,4,128,768]{3,2,1,0:T(8,128)(2,1)}, u32[]{:S(2)}, u32[]{:S(2)}) collective-permute-start(bf16[2,4,128,768]{3,2,1,0:T(8,128)(2,1)} %add_convert_fusion.1), channel_id=1, source_target_pairs={{0,16},{4,12},{8,24},{12,4},{16,0},{20,28},{24,8},{28,20},{1,17},{... | collective-permute-start | bytes 4718600 | tf_op jit(solution)/shard_map/ppermute | solution.py:1202
  313.5 26.4 %collective-permute-start.40 = (f32[96,128]{1,0:T(8,128)}, f32[96,128]{1,0:T(8,128)}, u32[]{:S(2)}, u32[]{:S(2)}) collective-permute-start(f32[96,128]{1,0:T(8,128)} %get-tuple-element.170), channel_id=1, source_target_pairs={{0,1},{1,0},{2,3},{3,2},{4,5},{5,4},{6,7},{7,6},{8,9},{9,8},{10,11... | collective-permute-start | bytes 147464 | tf_op jit(solution)/shard_map/ppermute | solution.py:1298
  317.9 22.1 %collective-permute-start.41 = (f32[96,128]{1,0:T(8,128)}, f32[96,128]{1,0:T(8,128)}, u32[]{:S(2)}, u32[]{:S(2)}) collective-permute-start(f32[96,128]{1,0:T(8,128)} %get-tuple-element.170), channel_id=1, source_target_pairs={{0,2},{1,3},{2,0},{3,1},{4,6},{5,7},{6,4},{7,5},{8,10},{9,11},{10,... | collective-permute-start | bytes 147464 | tf_op jit(solution)/shard_map/ppermute | solution.py:1298
  320.9 19.0 %collective-permute-start.42 = (f32[96,128]{1,0:T(8,128)S(1)}, f32[96,128]{1,0:T(8,128)S(1)}, u32[]{:S(2)}, u32[]{:S(2)}) collective-permute-start(f32[96,128]{1,0:T(8,128)S(1)} %copy-done.22), channel_id=1, source_target_pairs={{0,3},{1,2},{2,1},{3,0},{4,7},{5,6},{6,5},{7,4},{8,11},{9,10},{10,... | collective-permute-start | bytes 147464 | tf_op jit(solution)/shard_map/ppermute | solution.py:1298
  323.4 16.6 %collective-permute-start.36 = (bf16[4,128,768]{2,1,0:T(8,128)(2,1)}, bf16[4,128,768]{2,1,0:T(8,128)(2,1)}, u32[]{:S(2)}, u32[]{:S(2)}) collective-permute-start(bf16[4,128,768]{2,1,0:T(8,128)(2,1)} %fusion.1), channel_id=1, source_target_pairs={{0,8},{4,20},{8,0},{12,28},{16,24},{20,4},{24,16},{28,12},{1,9},{5... | collective-permute-start | bytes 2359304 | tf_op jit(solution)/shard_map/ppermute | solution.py:1202
  344.2 9.6 %collective-permute-start.47 = (bf16[128,768]{1,0:T(8,128)(2,1)S(1)}, bf16[128,768]{1,0:T(8,128)(2,1)S(1)}, u32[]{:S(2)}, u32[]{:S(2)}) collective-permute-start(bf16[128,768]{1,0:T(8,128)(2,1)S(1)} %get-tuple-element.179), channel_id=1, source_target_pairs={{0,1},{1,2},{2,3},{3,0},{4,5},{5,6},{6,7},{7,4},{8,9},{9,10},{10,1... | collective-permute-start | bytes 589832 | tf_op jit(solution)/shard_map/ppermute | solution.py:1206
  344.8 13.3 %collective-permute-start.48 = (bf16[128,768]{1,0:T(8,128)(2,1)S(1)}, bf16[128,768]{1,0:T(8,128)(2,1)S(1)}, u32[]{:S(2)}, u32[]{:S(2)}) collective-permute-start(bf16[128,768]{1,0:T(8,128)(2,1)S(1)} %get-tuple-element.180), channel_id=1, source_target_pairs={{0,2},{1,3},{2,0},{3,1},{4,6},{5,7},{6,4},{7,5},{8,10},{9,11},{10,... | collective-permute-start | bytes 589832 | tf_op jit(solution)/shard_map/ppermute | solution.py:1206
  346.2 11.9 %collective-permute-start.49 = (bf16[128,768]{1,0:T(8,128)(2,1)S(1)}, bf16[128,768]{1,0:T(8,128)(2,1)S(1)}, u32[]{:S(2)}, u32[]{:S(2)}) collective-permute-start(bf16[128,768]{1,0:T(8,128)(2,1)S(1)} %get-tuple-element.181), channel_id=1, source_target_pairs={{0,3},{1,0},{2,1},{3,2},{4,7},{5,4},{6,5},{7,6},{8,11},{9,8},{10,9... | collective-permute-start | bytes 589832 | tf_op jit(solution)/shard_map/ppermute | solution.py:1206
  350.5 8.5 %collective-permute-start.44 = (f32[96,128]{1,0:T(8,128)S(1)}, f32[96,128]{1,0:T(8,128)S(1)}, u32[]{:S(2)}, u32[]{:S(2)}) collective-permute-start(f32[96,128]{1,0:T(8,128)S(1)} %add.140.refs_0_), channel_id=1, source_target_pairs={{0,8},{4,12},{8,0},{12,4},{16,24},{20,28},{24,16},{28,20},{1,9},{5... | collective-permute-start | bytes 147464 | tf_op jit(solution)/shard_map/ppermute | solution.py:1490
  351.1 7.9 %collective-permute-start.45 = (f32[96,128]{1,0:T(8,128)S(1)}, f32[96,128]{1,0:T(8,128)S(1)}, u32[]{:S(2)}, u32[]{:S(2)}) collective-permute-start(f32[96,128]{1,0:T(8,128)S(1)} %add.140.refs_0_), channel_id=1, source_target_pairs={{0,16},{4,20},{8,24},{12,28},{16,0},{20,4},{24,8},{28,12},{1,17},{... | collective-permute-start | bytes 147464 | tf_op jit(solution)/shard_map/ppermute | solution.py:1490
  353.8 5.2 %collective-permute-start.46 = (f32[96,128]{1,0:T(8,128)S(1)}, f32[96,128]{1,0:T(8,128)S(1)}, u32[]{:S(2)}, u32[]{:S(2)}) collective-permute-start(f32[96,128]{1,0:T(8,128)S(1)} %add.140.refs_0_), channel_id=1, source_target_pairs={{0,24},{4,28},{8,16},{12,20},{16,8},{20,12},{24,0},{28,4},{1,25},{... | collective-permute-start | bytes 147464 | tf_op jit(solution)/shard_map/ppermute | solution.py:1490
  (34 other events, 409.8 us)
Sparse Core Ops, SparseCore 0:
  28.7 34.1 all-gather.4
  67.3 25.0 all-gather.6
  165.7 71.1 reduce-scatter.2
  266.8 26.1 reduce-scatter.4

commit v3 on v2

--- a/solution.py
+++ b/solution.py
@@ -1456,15 +1456,14 @@
         d_rows = after(d_project, back_second, down_wide).reshape(3 * model, extent)
         grad_bias, attend_keep, attend_send = attend_grad_call(tab, d_rows, normed, spread, sizes)
         attend_core = swap(attend_send, CORE)
-        back_last = after(back_last, grad_bias)
+        attend_first = add_first(attend_keep, attend_core)
+        attend_link = swap(attend_first, FAR)
+        back_last = after(back_last, grad_bias, attend_first)
         back_parts = add_third_kernel(back_keep, back_core, back_link, back_last)
         back_others = shift_parts(back_parts)
-        attend_core = after(attend_core, back_parts)
-        attend_first = add_first(attend_keep, attend_core)
-        attend_link = swap(attend_first, FAR)
         d_frames, small = first_call(
             tab,
-            after(d_rows, attend_first),
+            after(d_rows, attend_first, back_parts),
             frames,
             d_middle,
             row(first_gain),

time: 372 us -> 392 us (1.054)
  waiting for transfers between devices: 66.4 us -> 82.6 us
    ppermute x3, waiting for transfers between devices: 0.01 us -> 9.67 us  [exchange(): lax.ppermute(values, axis, [(i, i ^ flip) for i in range(size)])]
    ppermute x34, waiting for transfers between devices: 48.6 us -> 57.4 us  [swap(): return lax.ppermute(value, 'dp', [(d, d ^ flips[d & 1]) for d in range(8)])]
  transfers between devices with their start and end apart: 54 -> 54, of which waited for: 17 -> 18; matrix products, arithmetic and copies ran while one was open for 4% -> 4% of each run, Pallas kernels for 59% -> 53%
where the time goes in v3:
time: 392 us; the launch traced here: 387 us
  Pallas kernels  218 us (56%)
  waiting for transfers between devices  82.6 us (21%)
  starting transfers between devices  44 us (11%)
  other arithmetic  21.9 us (6%)
  between operations  15.1 us (4%)
  local copies, waits for them, and re-layouts  5.88 us (2%)
    ppermute x34, waiting for transfers between devices, swap(): return lax.ppermute(value, 'dp', [(d, d ^ flips[d & 1]) for d in range(8)])  57.4 us
    pallas_call x1, Pallas kernels, back_call(): pl.pallas_call(functools.partial(back_kernel, (len(out_pieces), len(up_pi...  47.9 us
    pallas_call x2, Pallas kernels, up_call(): pl.pallas_call(functools.partial(up_kernel, (len(up_pieces), len(earlier)...  38.4 us
    pallas_call x2, Pallas kernels, attention_back_call(): pl.pallas_call(functools.partial(attention_back_kernel, group, block), gr...  36.7 us
    pallas_call x2, Pallas kernels, attention_call(): pl.pallas_call(functools.partial(attention_kernel, group, block), grid=(s...  22.9 us
    ppermute x34, starting transfers between devices, swap(): return lax.ppermute(value, 'dp', [(d, d ^ flips[d & 1]) for d in range(8)])  22.2 us
    pallas_call x1, Pallas kernels, first_call(): pl.pallas_call(functools.partial(first_kernel, len(pieces)), grid_spec=gr...  15.9 us
    pallas_call x1, Pallas kernels, down_call(): pl.pallas_call(functools.partial(down_kernel, len(pieces), len(earlier),...  15.2 us
  transfers between devices with their start and end apart: 54, of which 18 were waited for; matrix products, arithmetic and copies ran while one was open for 4% of the time, Pallas kernels for 53%

profile of v3, /device:TPU:0, one launch (start us, length us, event | category | flops | bytes accessed | tf_op | source)
XLA Modules:
  0.0 387.1 jit_solution(17116237930442520288)
XLA Ops:
  7.2 3.0 collective-permute-start.3
  10.3 1.5 collective-permute-start.4
  11.8 1.6 collective-permute-start
  13.3 2.6 collective-permute-start.1
  18.2 1.7 pad_maximum_fusion.1
  20.0 1.7 collective-permute-done
  21.7 6.8 %collective-permute-done.1 = bf16[128,768]{1,0:T(8,128)(2,1)S(1)} collective-permute-done((bf16[128,768]{1,0:T(8,128)(2,1)}, bf16[128,768]{1,0:T(8,128)(2,1)S(1)}, u32[]{:S(2)}, u32[]{:S(2)}) %collective-permute-start.1) | collective-permute-done | bytes 196640 | tf_op jit(solution)/shard_map/ppermute | solution.py:1206
  29.7 14.3 %collective-permute-done.10.rest_9_ = bf16[3,128,768]{2,1,0:T(8,128)(2,1)S(1)} collective-permute-done((bf16[3,128,768]{2,1,0:T(8,128)(2,1)S(1)}, bf16[3,128,768]{2,1,0:T(8,128)(2,1)S(1)}, u32[]{:S(2)}, u32[]{:S(2)}) %collective-permute-start.10) | collective-permute-done | bytes 589856 | tf_op jit(solution)/shard_map/ppermute | solution.py:1202
  47.4 6.6 %collective-permute-done.12.rest_11_ = bf16[3,128,768]{2,1,0:T(8,128)(2,1)S(1)} collective-permute-done((bf16[3,128,768]{2,1,0:T(8,128)(2,1)S(1)}, bf16[3,128,768]{2,1,0:T(8,128)(2,1)S(1)}, u32[]{:S(2)}, u32[]{:S(2)}) %collective-permute-start.12) | collective-permute-done | bytes 589856 | tf_op jit(solution)/shard_map/ppermute | solution.py:1202
  54.6 1.8 collective-permute-done.8.rest_6_
  56.5 1.5 collective-permute-done.9.rest_7_
  59.7 3.2 all-gather.5.cloned.1.call-done
  62.9 1.5 collective-permute-start.17
  64.4 1.5 collective-permute-start.18
  68.3 12.9 %project.1 = (bf16[1024,1024]{1,0:T(8,128)(2,1)}, bf16[3072,1024]{1,0:T(8,128)(2,1)}) custom-call(s32[48]{0:T(128)} %stack.183.tab, bf16[1024,1024]{1,0:T(8,128)(2,1)} %bitcast.81, f32[1,1024]{1,0:T(1,128)} %bitcast.106, f32[1,1024]{1,0:T(1,128)} %bitcast.101, f32[1,3072]{1,0:T(1,128)} %bitcast.98, bf16[128,768]{1,0:T(8,128)(2,1)} %rest_0_.3, ...), custom_call_target="tpu_custom_call" | custom-call | flops 8000000 | bytes 80000 | tf_op jit(solution)/shard_map/project/pallas_call | solution.py:309
  81.2 11.5 %attention.2 = (bf16[1024,1024]{1,0:T(8,128)(2,1)}, f32[8,2,1024]{2,1,0:T(2,128)}) custom-call(s32[1]{0:T(128)S(6)} %copy.41.lengths, bf16[3072,1024]{1,0:T(8,128)(2,1)} %get-tuple-element.117.query.key.value, bf16[3072,1024]{1,0:T(8,128)(2,1)} %get-tuple-element.117.query.key.value, bf16[3072,1024]{1,0:T(8,128)(2,1)} %get-tuple-element.117.query.key.value), custom_call_target="tpu_custom_call" | custom-call | flops 42949672 | bytes 64000 | tf_op jit(solution)/shard_map/attention/pallas_call | solution.py:396
  92.7 1.5 collective-permute-done.17.rest_1_.rest_2_.rest_10_
  95.5 11.4 %attention.3 = (bf16[1024,1024]{1,0:T(8,128)(2,1)}, f32[8,2,1024]{2,1,0:T(2,128)}) custom-call(s32[1]{0:T(128)S(6)} %copy.41.lengths, bf16[3072,1024]{1,0:T(8,128)(2,1)} %get-tuple-element.117.query.key.value, bf16[3072,1024]{1,0:T(8,128)(2,1)} %get-tuple-element.117.query.key.value, ...), custom_call_target="tpu_custom_call", output_to_operand_aliasing={{0}: (4, {}), {1}: (5, {})} | custom-call | flops 42949672 | bytes 64000 | tf_op jit(solution)/shard_map/attention/pallas_call | solution.py:396
  106.9 5.1 %collective-permute-done.19.rest_3_.rest_4_.rest_12_ = bf16[4,128,1280]{2,1,0:T(8,128)(2,1)} collective-permute-done((bf16[4,128,1280]{2,1,0:T(8,128)(2,1)S(1)}, bf16[4,128,1280]{2,1,0:T(8,128)(2,1)}, u32[]{:S(2)}, u32[]{:S(2)}) %collective-permute-start.19) | collective-permute-done | bytes 1310752 | tf_op jit(solution)/shard_map/ppermute | solution.py:1202
  112.6 1.5 collective-permute-start.24
  115.3 9.7 %out.1 = (f32[1024,1024]{1,0:T(8,128)}, bf16[1024,1024]{1,0:T(8,128)(2,1)}, bf16[1024,1024]{1,0:T(8,128)(2,1)}, f32[1,1024]{1,0:T(1,128)}) custom-call(s32[48]{0:T(128)} %stack.178.tab, s32[1]{0:T(128)S(6)} %copy.41.lengths, bf16[1024,1024]{1,0:T(8,128)(2,1)} %get-tuple-element.119.mixture, bf16[1024,1024]{1,0:T(8,128)(2,1)} %bitcast.82, ...), custom_call_target="tpu_custom_call" | custom-call | flops 8 | bytes 8 | tf_op jit(solution)/shard_map/out/pallas_call | solution.py:468
  125.0 19.5 %up.2 = (bf16[1024,4096]{1,0:T(8,128)(2,1)}, bf16[1024,4096]{1,0:T(8,128)(2,1)}, bf16[4096,1024]{1,0:T(8,128)(2,1)}) custom-call(s32[48]{0:T(128)} %stack.178.tab, bf16[1024,1024]{1,0:T(8,128)(2,1)} %get-tuple-element.129.normed, bf16[1024,1024]{1,0:T(8,128)(2,1)} %get-tuple-element.124.result.d_result, f32[1,4096]{1,0:T(1,128)} %bitcast.113, ...), custom_call_target="tpu_custom_call" | custom-call | flops 68719476736 | bytes 400000000 | tf_op jit(solution)/shard_map/up/pallas_call | solution.py:564
  145.9 19.0 %up.3 = (bf16[1024,4096]{1,0:T(8,128)(2,1)}, bf16[1024,4096]{1,0:T(8,128)(2,1)}, bf16[4096,1024]{1,0:T(8,128)(2,1)}) custom-call(s32[48]{0:T(128)} %stack.178.tab, bf16[1024,1024]{1,0:T(8,128)(2,1)} %get-tuple-element.129.normed, ...), custom_call_target="tpu_custom_call", output_to_operand_aliasing={{0}: (12, {}), {1}: (13, {}), {2}: (14, {})} | custom-call | flops 68719476736 | bytes 400000000 | tf_op jit(solution)/shard_map/up/pallas_call | solution.py:564
  165.6 2.5 collective-permute-done.30.rest_24_.rest_7_
  168.1 47.9 %back.1 = (f32[1024,1024]{1,0:T(8,128)}, bf16[1024,1024]{1,0:T(8,128)(2,1)}, f32[1,4096]{1,0:T(1,128)}, f32[1,1024]{1,0:T(1,128)}, f32[1,1024]{1,0:T(1,128)}, /*...) custom-call(s32[48]{0:T(128)} %stack.178.tab, ...), custom_call_target="tpu_custom_call" | custom-call | flops 240518168576 | bytes 480000000 | tf_op jit(solution)/shard_map/back/pallas_call | solution.py:806
  216.5 10.3 %attention_back.2.rest_0_ = bf16[3,1024,1024]{2,1,0:T(8,128)(2,1)} custom-call(s32[1]{0:T(128)S(6)} %copy.41.lengths, bf16[3072,1024]{1,0:T(8,128)(2,1)} %get-tuple-element.117.query.key.value, bf16[3072,1024]{1,0:T(8,128)(2,1)} %get-tuple-element.117.query.key.value, bf16[3072,1024]{1,0:T(8,128)(2,1)} %get-tuple-element.117.query.key.value, ...), custom_call_target="tpu_custom_call" | custom-call | flops 5368709120 | bytes 8000000 | tf_op jit(solution)/shard_map/attention_back/pallas_call | solution.py:906
  226.8 3.2 add_convert_fusion
  230.1 26.5 %attention_back.3 = bf16[3,1024,1024]{2,1,0:T(8,128)(2,1)} custom-call(s32[1]{0:T(128)S(6)} %copy.41.lengths, bf16[3072,1024]{1,0:T(8,128)(2,1)} %get-tuple-element.117.query.key.value, bf16[3072,1024]{1,0:T(8,128)(2,1)} %get-tuple-element.117.query.key.value, bf16[3072,1024]{1,0:T(8,128)(2,1)} %get-tuple-element.117.query.key.value, ...), custom_call_target="tpu_custom_call", output_to_operand_aliasing={{}: (7, {})} | custom-call | flops 16106127360 | bytes 8000000 | tf_op jit(solution)/shard_map/attention_back/pallas_call | solution.py:906
  256.6 5.9 %collective-permute-done.32.refs_2_ = bf16[2,4,128,1280]{3,2,1,0:T(8,128)(2,1)} collective-permute-done((bf16[2,4,128,1280]{3,2,1,0:T(8,128)(2,1)S(1)}, bf16[2,4,128,1280]{3,2,1,0:T(8,128)(2,1)}, u32[]{:S(2)}, u32[]{:S(2)}) %collective-permute-start.32) | collective-permute-done | bytes 2621472 | tf_op jit(solution)/shard_map/ppermute | solution.py:1202
  262.5 3.7 fusion
  266.1 11.6 %attend_grad.1 = (f32[1,3072]{1,0:T(1,128)}, bf16[4,4,128,768]{3,2,1,0:T(8,128)(2,1)}, bf16[4,4,128,768]{3,2,1,0:T(8,128)(2,1)}) custom-call(s32[48]{0:T(128)} %stack.183.tab, bf16[3072,1024]{1,0:T(8,128)(2,1)} %bitcast.84, bf16[1024,1024]{1,0:T(8,128)(2,1)} %get-tuple-element.145.normed), custom_call_target="tpu_custom_call" | custom-call | flops 51539607552 | bytes 112000000 | tf_op jit(solution)/shard_map/attend_grad/pallas_call | solution.py:966
  277.9 1.4 collective-permute-start.35
  279.3 4.3 %collective-permute-done.33 = bf16[4,4,128,768]{3,2,1,0:T(8,128)(2,1)S(1)} collective-permute-done((bf16[4,4,128,768]{3,2,1,0:T(8,128)(2,1)}, bf16[4,4,128,768]{3,2,1,0:T(8,128)(2,1)S(1)}, u32[]{:S(2)}, u32[]{:S(2)}) %collective-permute-start.33) | collective-permute-done | bytes 3145760 | tf_op jit(solution)/shard_map/ppermute | solution.py:1202
  283.6 4.1 %add_convert_fusion.1 = bf16[2,4,128,768]{3,2,1,0:T(8,128)(2,1)} fusion(bf16[4,4,128,768]{3,2,1,0:T(8,128)(2,1)S(1)} %collective-permute-done.33, bf16[4,4,128,768]{3,2,1,0:T(8,128)(2,1)} %get-tuple-element.146), kind=kLoop, calls=%fused_computation.1 | loop fusion | flops 3145728 | bytes 4718592 | tf_op jit(solution)/shard_map/convert_element_type | solution.py:1274
  288.6 12.2 %collective-permute-done.35.refs_3_ = bf16[4,128,1280]{2,1,0:T(8,128)(2,1)} collective-permute-done((bf16[4,128,1280]{2,1,0:T(8,128)(2,1)}, bf16[4,128,1280]{2,1,0:T(8,128)(2,1)}, u32[]{:S(2)}, u32[]{:S(2)}) %collective-permute-start.35) | collective-permute-done | bytes 1310752 | tf_op jit(solution)/shard_map/ppermute | solution.py:1202
  300.8 4.8 %add.187 = (f32[128,1280]{1,0:T(8,128)}, bf16[128,1280]{1,0:T(8,128)(2,1)}, bf16[128,1280]{1,0:T(8,128)(2,1)}, bf16[128,1280]{1,0:T(8,128)(2,1)}) custom-call(bf16[4,4,128,1280]{3,2,1,0:T(8,128)(2,1)} %get-tuple-element.137.refs_0_, bf16[4,4,128,1280]{3,2,1,0:T(8,128)(2,1)} %collective-permute-done.31.refs_1_, ...), custom_call_target="tpu_custom_call" | custom-call | flops 80000000000 | bytes 80000000 | tf_op jit(solution)/shard_map/add/pallas_call | solution.py:1261
  305.7 15.9 %first.1 = (bf16[1024,1024]{1,0:T(8,128)(2,1)}, f32[96,128]{1,0:T(8,128)}) custom-call(s32[48]{0:T(128)} %stack.183.tab, bf16[3072,1024]{1,0:T(8,128)(2,1)} %bitcast.85, bf16[1024,1024]{1,0:T(8,128)(2,1)} %bitcast.83, f32[1024,1024]{1,0:T(8,128)} %get-tuple-element.155.d_middle, f32[1,1024]{1,0:T(1,128)} %bitcast.107, bf16[128,768]{1,0:T(8,128)(2,1)} %rest_0_.3, ...), custom_call_target="tpu_custom_call" | custom-call | flops 51539607552 | bytes 192000000 | tf_op jit(solution)/shard_map/first/pallas_call | solution.py:1097
  321.6 1.5 collective-permute-start.40
  323.1 2.4 collective-permute-start.41
  326.6 3.3 collective-permute-start.38
  330.0 2.6 fusion.1
  333.0 9.7 %collective-permute-done.41 = f32[96,128]{1,0:T(8,128)} collective-permute-done((f32[96,128]{1,0:T(8,128)}, f32[96,128]{1,0:T(8,128)}, u32[]{:S(2)}, u32[]{:S(2)}) %collective-permute-start.41) | collective-permute-done | bytes 49184 | tf_op jit(solution)/shard_map/ppermute | solution.py:1298
  344.0 15.2 %down.1 = bf16[1024,1024]{1,0:T(8,128)(2,1)} custom-call(s32[48]{0:T(128)} %stack.178.tab, bf16[1024,4096]{1,0:T(8,128)(2,1)} %get-tuple-element.164.active, f32[1024,1024]{1,0:T(8,128)} %get-tuple-element.165.middle, f32[1,1024]{1,0:T(1,128)} %bitcast.116, bf16[4,512,256]{2,1,0:T(8,128)(2,1)} %bitcast.112, ...), custom_call_target="tpu_custom_call" | custom-call | flops 68719476736 | bytes 192000000 | tf_op jit(solution)/shard_map/down/pallas_call | solution.py:1176
  361.6 2.1 fusion.2
  364.4 3.1 collective-permute-start.49
  372.1 1.4 collective-permute-start.46
  373.5 3.3 collective-permute-done.48
  378.9 1.5 small.1
  (151 shorter events, 30.4 us)
Async XLA Ops:
  7.2 55.7 %all-gather.5.cloned.1.call-start = ((), (), s32[]{:S(2)}) async-start(), calls=%async_computation.4 | async-start | bytes 1638400 | tf_op jit(solution)/shard_map/all_gather | solution.py:1354
  7.2 10.0 %collective-permute-start.3 = (bf16[128,768]{1,0:T(8,128)(2,1)}, bf16[128,768]{1,0:T(8,128)(2,1)S(1)}, u32[]{:S(2)}, u32[]{:S(2)}) collective-permute-start(bf16[128,768]{1,0:T(8,128)(2,1)} %rest_0_.3), channel_id=1, source_target_pairs={{0,16},{4,12},{8,24},{12,4},{16,0},{20,28},{24,8},{28,20},{1,17},{... | collective-permute-start | bytes 589832 | tf_op jit(solution)/shard_map/ppermute | solution.py:1202
  10.3 7.0 %collective-permute-start.4 = (bf16[128,768]{1,0:T(8,128)(2,1)}, bf16[128,768]{1,0:T(8,128)(2,1)S(1)}, u32[]{:S(2)}, u32[]{:S(2)}) collective-permute-start(bf16[128,768]{1,0:T(8,128)(2,1)} %rest_0_.3), channel_id=1, source_target_pairs={{0,8},{4,20},{8,0},{12,28},{16,24},{20,4},{24,16},{28,12},{1,9},{5... | collective-permute-start | bytes 589832 | tf_op jit(solution)/shard_map/ppermute | solution.py:1202
  11.8 9.9 %collective-permute-start = (bf16[128,768]{1,0:T(8,128)(2,1)}, bf16[128,768]{1,0:T(8,128)(2,1)S(1)}, u32[]{:S(2)}, u32[]{:S(2)}) collective-permute-start(bf16[128,768]{1,0:T(8,128)(2,1)} %rest_0_.3), channel_id=1, source_target_pairs={{0,1},{1,2},{2,3},{3,0},{4,5},{5,6},{6,7},{7,4},{8,9},{9,10},{10,1... | collective-permute-start | bytes 589832 | tf_op jit(solution)/shard_map/ppermute | solution.py:1206
  13.3 15.1 %collective-permute-start.1 = (bf16[128,768]{1,0:T(8,128)(2,1)}, bf16[128,768]{1,0:T(8,128)(2,1)S(1)}, u32[]{:S(2)}, u32[]{:S(2)}) collective-permute-start(bf16[128,768]{1,0:T(8,128)(2,1)} %rest_0_.3), channel_id=1, source_target_pairs={{0,2},{1,3},{2,0},{3,1},{4,6},{5,7},{6,4},{7,5},{8,10},{9,11},{10,... | collective-permute-start | bytes 589832 | tf_op jit(solution)/shard_map/ppermute | solution.py:1206
  15.9 12.5 %collective-permute-start.2 = (bf16[128,768]{1,0:T(8,128)(2,1)}, bf16[128,768]{1,0:T(8,128)(2,1)S(1)}, u32[]{:S(2)}, u32[]{:S(2)}) collective-permute-start(bf16[128,768]{1,0:T(8,128)(2,1)} %rest_0_.3), channel_id=1, source_target_pairs={{0,3},{1,0},{2,1},{3,2},{4,7},{5,4},{6,5},{7,6},{8,11},{9,8},{10,9... | collective-permute-start | bytes 589832 | tf_op jit(solution)/shard_map/ppermute | solution.py:1206
  17.3 11.3 %collective-permute-start.5 = (bf16[128,768]{1,0:T(8,128)(2,1)S(1)}, bf16[128,768]{1,0:T(8,128)(2,1)S(1)}, u32[]{:S(2)}, u32[]{:S(2)}) collective-permute-start(bf16[128,768]{1,0:T(8,128)(2,1)S(1)} %collective-permute-done.4.rest_1_), channel_id=1, source_target_pairs={{0,16},{4,12},{8,24},{12,4},{16,0},{20,28},{24,8},{28,20},{1,17},{... | collective-permute-start | bytes 589832 | tf_op jit(solution)/shard_map/ppermute | solution.py:1202
  28.6 66.9 %all-gather.7.cloned.1.call-start = ((), (), s32[]{:S(2)}) async-start(), calls=%async_computation.5 | async-start | bytes 1310720 | tf_op jit(solution)/shard_map/all_gather | solution.py:1361
  28.6 15.4 %collective-permute-start.10 = (bf16[3,128,768]{2,1,0:T(8,128)(2,1)S(1)}, bf16[3,128,768]{2,1,0:T(8,128)(2,1)S(1)}, u32[]{:S(2)}, u32[]{:S(2)}) collective-permute-start(bf16[3,128,768]{2,1,0:T(8,128)(2,1)S(1)} %pad_maximum_fusion.rest_8_), channel_id=1, source_target_pairs={{0,8},{4,20},{8,0},{12,28},{16,24},{20,4},{24,16},{28,12},{1,9},{5... | collective-permute-start | bytes 1769480 | tf_op jit(solution)/shard_map/ppermute | solution.py:1202
  29.2 14.9 %collective-permute-start.11 = (bf16[3,128,768]{2,1,0:T(8,128)(2,1)S(1)}, bf16[3,128,768]{2,1,0:T(8,128)(2,1)S(1)}, u32[]{:S(2)}, u32[]{:S(2)}) collective-permute-start(bf16[3,128,768]{2,1,0:T(8,128)(2,1)S(1)} %pad_maximum_fusion.rest_8_), channel_id=1, source_target_pairs={{0,16},{4,12},{8,24},{12,4},{16,0},{20,28},{24,8},{28,20},{1,17},{... | collective-permute-start | bytes 1769480 | tf_op jit(solution)/shard_map/ppermute | solution.py:1202
  44.1 9.9 %collective-permute-start.12 = (bf16[3,128,768]{2,1,0:T(8,128)(2,1)S(1)}, bf16[3,128,768]{2,1,0:T(8,128)(2,1)S(1)}, u32[]{:S(2)}, u32[]{:S(2)}) collective-permute-start(bf16[3,128,768]{2,1,0:T(8,128)(2,1)S(1)} %collective-permute-done.10.rest_9_), channel_id=1, source_target_pairs={{0,16},{4,12},{8,24},{12,4},{16,0},{20,28},{24,8},{28,20},{1,17},{... | collective-permute-start | bytes 1769480 | tf_op jit(solution)/shard_map/ppermute | solution.py:1202
  45.3 8.8 %collective-permute-start.7 = (bf16[128,768]{1,0:T(8,128)(2,1)S(1)}, bf16[128,768]{1,0:T(8,128)(2,1)S(1)}, u32[]{:S(2)}, u32[]{:S(2)}) collective-permute-start(bf16[128,768]{1,0:T(8,128)(2,1)S(1)} %collective-permute-done.4.rest_1_), channel_id=1, source_target_pairs={{0,4},{4,0},{8,12},{12,8},{16,20},{20,16},{24,28},{28,24},{1,5},{5... | collective-permute-start | bytes 589832 | tf_op jit(solution)/shard_map/ppermute | solution.py:1202
  45.8 12.2 %collective-permute-start.13 = (bf16[3,128,768]{2,1,0:T(8,128)(2,1)S(1)}, bf16[3,128,768]{2,1,0:T(8,128)(2,1)S(1)}, u32[]{:S(2)}, u32[]{:S(2)}) collective-permute-start(bf16[3,128,768]{2,1,0:T(8,128)(2,1)S(1)} %pad_maximum_fusion.rest_8_), channel_id=1, source_target_pairs={{0,4},{4,0},{8,12},{12,8},{16,20},{20,16},{24,28},{28,24},{1,5},{5... | collective-permute-start | bytes 1769480 | tf_op jit(solution)/shard_map/ppermute | solution.py:1202
  45.8 12.2 %collective-permute-start.14 = (bf16[3,128,768]{2,1,0:T(8,128)(2,1)S(1)}, bf16[3,128,768]{2,1,0:T(8,128)(2,1)S(1)}, u32[]{:S(2)}, u32[]{:S(2)}) collective-permute-start(bf16[3,128,768]{2,1,0:T(8,128)(2,1)S(1)} %collective-permute-done.10.rest_9_), channel_id=1, source_target_pairs={{0,4},{4,0},{8,12},{12,8},{16,20},{20,16},{24,28},{28,24},{1,5},{5... | collective-permute-start | bytes 1769480 | tf_op jit(solution)/shard_map/ppermute | solution.py:1202
  47.3 10.7 %collective-permute-start.15 = (bf16[3,128,768]{2,1,0:T(8,128)(2,1)S(1)}, bf16[3,128,768]{2,1,0:T(8,128)(2,1)S(1)}, u32[]{:S(2)}, u32[]{:S(2)}) collective-permute-start(bf16[3,128,768]{2,1,0:T(8,128)(2,1)S(1)} %collective-permute-done.11.rest_10_), channel_id=1, source_target_pairs={{0,4},{4,0},{8,12},{12,8},{16,20},{20,16},{24,28},{28,24},{1,5},{5... | collective-permute-start | bytes 1769480 | tf_op jit(solution)/shard_map/ppermute | solution.py:1202
  54.0 5.7 %collective-permute-start.16 = (bf16[3,128,768]{2,1,0:T(8,128)(2,1)S(1)}, bf16[3,128,768]{2,1,0:T(8,128)(2,1)}, u32[]{:S(2)}, u32[]{:S(2)}) collective-permute-start(bf16[3,128,768]{2,1,0:T(8,128)(2,1)S(1)} %collective-permute-done.12.rest_11_), channel_id=1, source_target_pairs={{0,4},{4,0},{8,12},{12,8},{16,20},{20,16},{24,28},{28,24},{1,5},{5... | collective-permute-start | bytes 1769480 | tf_op jit(solution)/shard_map/ppermute | solution.py:1202
  62.9 31.3 %collective-permute-start.17 = (bf16[4,128,1280]{2,1,0:T(8,128)(2,1)}, bf16[4,128,1280]{2,1,0:T(8,128)(2,1)S(1)}, u32[]{:S(2)}, u32[]{:S(2)}) collective-permute-start(bf16[4,128,1280]{2,1,0:T(8,128)(2,1)} %bitcast.87), channel_id=1, source_target_pairs={{0,8},{4,20},{8,0},{12,28},{16,24},{20,4},{24,16},{28,12},{1,9},{5... | collective-permute-start | bytes 3932168 | tf_op jit(solution)/shard_map/ppermute | solution.py:1202
  64.4 29.8 %collective-permute-start.18 = (bf16[4,128,1280]{2,1,0:T(8,128)(2,1)}, bf16[4,128,1280]{2,1,0:T(8,128)(2,1)}, u32[]{:S(2)}, u32[]{:S(2)}) collective-permute-start(bf16[4,128,1280]{2,1,0:T(8,128)(2,1)} %bitcast.88), channel_id=1, source_target_pairs={{0,16},{4,12},{8,24},{12,4},{16,0},{20,28},{24,8},{28,20},{1,17},{... | collective-permute-start | bytes 3932168 | tf_op jit(solution)/shard_map/ppermute | solution.py:1202
  67.3 195.2 %reduce-scatter.3.cloned.1.call-start = ((), (), s32[]{:S(2)}) async-start(), calls=%async_computation.2 | async-start | bytes 9437184 | tf_op jit(solution)/shard_map/reduce_scatter | solution.py:1417
  94.2 17.7 %collective-permute-start.19 = (bf16[4,128,1280]{2,1,0:T(8,128)(2,1)S(1)}, bf16[4,128,1280]{2,1,0:T(8,128)(2,1)}, u32[]{:S(2)}, u32[]{:S(2)}) collective-permute-start(bf16[4,128,1280]{2,1,0:T(8,128)(2,1)S(1)} %collective-permute-done.17.rest_1_.rest_2_.rest_10_), channel_id=1, source_target_pairs={{0,16},{4,12},{8,24},{12,4},{16,0},{20,28},{24,8},{28,20},{1,17},{... | collective-permute-start | bytes 3932168 | tf_op jit(solution)/shard_map/ppermute | solution.py:1202
  94.8 19.3 %collective-permute-start.20 = (bf16[4,128,1280]{2,1,0:T(8,128)(2,1)S(1)}, bf16[4,128,1280]{2,1,0:T(8,128)(2,1)}, u32[]{:S(2)}, u32[]{:S(2)}) collective-permute-start(bf16[4,128,1280]{2,1,0:T(8,128)(2,1)S(1)} %bitcast.94), channel_id=1, source_target_pairs={{0,4},{4,0},{8,12},{12,8},{16,20},{20,16},{24,28},{28,24},{1,5},{5... | collective-permute-start | bytes 3932168 | tf_op jit(solution)/shard_map/ppermute | solution.py:1202
  94.9 19.7 %collective-permute-start.21 = (bf16[4,128,1280]{2,1,0:T(8,128)(2,1)S(1)}, bf16[4,128,1280]{2,1,0:T(8,128)(2,1)}, u32[]{:S(2)}, u32[]{:S(2)}) collective-permute-start(bf16[4,128,1280]{2,1,0:T(8,128)(2,1)S(1)} %collective-permute-done.17.rest_1_.rest_2_.rest_10_), channel_id=1, source_target_pairs={{0,4},{4,0},{8,12},{12,8},{16,20},{20,16},{24,28},{28,24},{1,5},{5... | collective-permute-start | bytes 3932168 | tf_op jit(solution)/shard_map/ppermute | solution.py:1202
  95.3 19.4 %collective-permute-start.22 = (bf16[4,128,1280]{2,1,0:T(8,128)(2,1)}, bf16[4,128,1280]{2,1,0:T(8,128)(2,1)}, u32[]{:S(2)}, u32[]{:S(2)}) collective-permute-start(bf16[4,128,1280]{2,1,0:T(8,128)(2,1)} %collective-permute-done.18.rest_2_.rest_3_.rest_11_), channel_id=1, source_target_pairs={{0,4},{4,0},{8,12},{12,8},{16,20},{20,16},{24,28},{28,24},{1,5},{5... | collective-permute-start | bytes 3932168 | tf_op jit(solution)/shard_map/ppermute | solution.py:1202
  112.6 31.9 %collective-permute-start.24 = (bf16[4,512,256]{2,1,0:T(8,128)(2,1)}, bf16[4,512,256]{2,1,0:T(8,128)(2,1)}, u32[]{:S(2)}, u32[]{:S(2)}) collective-permute-start(bf16[4,512,256]{2,1,0:T(8,128)(2,1)} %bitcast.108), channel_id=1, source_target_pairs={{0,8},{4,20},{8,0},{12,28},{16,24},{20,4},{24,16},{28,12},{1,9},{5... | collective-permute-start | bytes 3145736 | tf_op jit(solution)/shard_map/ppermute | solution.py:1202
  114.1 30.4 %collective-permute-start.25 = (bf16[4,512,256]{2,1,0:T(8,128)(2,1)}, bf16[4,512,256]{2,1,0:T(8,128)(2,1)S(1)}, u32[]{:S(2)}, u32[]{:S(2)}) collective-permute-start(bf16[4,512,256]{2,1,0:T(8,128)(2,1)} %bitcast.109), channel_id=1, source_target_pairs={{0,16},{4,12},{8,24},{12,4},{16,0},{20,28},{24,8},{28,20},{1,17},{... | collective-permute-start | bytes 3145736 | tf_op jit(solution)/shard_map/ppermute | solution.py:1202
  114.6 50.9 %collective-permute-start.27 = (bf16[4,512,256]{2,1,0:T(8,128)(2,1)}, bf16[4,512,256]{2,1,0:T(8,128)(2,1)S(1)}, u32[]{:S(2)}, u32[]{:S(2)}) collective-permute-start(bf16[4,512,256]{2,1,0:T(8,128)(2,1)} %bitcast.110), channel_id=1, source_target_pairs={{0,4},{4,0},{8,12},{12,8},{16,20},{20,16},{24,28},{28,24},{1,5},{5... | collective-permute-start | bytes 3145736 | tf_op jit(solution)/shard_map/ppermute | solution.py:1202
  144.5 20.4 %collective-permute-start.26 = (bf16[4,512,256]{2,1,0:T(8,128)(2,1)}, bf16[4,512,256]{2,1,0:T(8,128)(2,1)}, u32[]{:S(2)}, u32[]{:S(2)}) collective-permute-start(bf16[4,512,256]{2,1,0:T(8,128)(2,1)} %collective-permute-done.24.rest_18_.rest_1_), channel_id=1, source_target_pairs={{0,16},{4,12},{8,24},{12,4},{16,0},{20,28},{24,8},{28,20},{1,17},{... | collective-permute-start | bytes 3145736 | tf_op jit(solution)/shard_map/ppermute | solution.py:1202
  145.4 20.1 %collective-permute-start.28 = (bf16[4,512,256]{2,1,0:T(8,128)(2,1)}, bf16[4,512,256]{2,1,0:T(8,128)(2,1)}, u32[]{:S(2)}, u32[]{:S(2)}) collective-permute-start(bf16[4,512,256]{2,1,0:T(8,128)(2,1)} %collective-permute-done.24.rest_18_.rest_1_), channel_id=1, source_target_pairs={{0,4},{4,0},{8,12},{12,8},{16,20},{20,16},{24,28},{28,24},{1,5},{5... | collective-permute-start | bytes 3145736 | tf_op jit(solution)/shard_map/ppermute | solution.py:1202
  145.9 19.7 %collective-permute-start.29 = (bf16[4,512,256]{2,1,0:T(8,128)(2,1)S(1)}, bf16[4,512,256]{2,1,0:T(8,128)(2,1)}, u32[]{:S(2)}, u32[]{:S(2)}) collective-permute-start(bf16[4,512,256]{2,1,0:T(8,128)(2,1)S(1)} %collective-permute-done.25.rest_19_.rest_2_), channel_id=1, source_target_pairs={{0,4},{4,0},{8,12},{12,8},{16,20},{20,16},{24,28},{28,24},{1,5},{5... | collective-permute-start | bytes 3145736 | tf_op jit(solution)/shard_map/ppermute | solution.py:1202
  165.5 164.5 %reduce-scatter.5.cloned.1.call-start = ((), (), s32[]{:S(2)}) async-start(), calls=%async_computation.3 | async-start | bytes 1310720 | tf_op jit(solution)/shard_map/reduce_scatter | solution.py:1453
  216.0 10.8 %collective-permute-start.31 = (bf16[4,4,128,1280]{3,2,1,0:T(8,128)(2,1)}, bf16[4,4,128,1280]{3,2,1,0:T(8,128)(2,1)}, u32[]{:S(2)}, u32[]{:S(2)}) collective-permute-start(bf16[4,4,128,1280]{3,2,1,0:T(8,128)(2,1)} %get-tuple-element.138), channel_id=1, source_target_pairs={{0,4},{4,0},{8,12},{12,8},{16,20},{20,16},{24,28},{28,24},{1,5},{5... | collective-permute-start | bytes 15728648 | tf_op jit(solution)/shard_map/ppermute | solution.py:1202
  230.1 32.4 %collective-permute-start.32 = (bf16[2,4,128,1280]{3,2,1,0:T(8,128)(2,1)S(1)}, bf16[2,4,128,1280]{3,2,1,0:T(8,128)(2,1)}, u32[]{:S(2)}, u32[]{:S(2)}) collective-permute-start(bf16[2,4,128,1280]{3,2,1,0:T(8,128)(2,1)S(1)} %add_convert_fusion), channel_id=1, source_target_pairs={{0,16},{4,12},{8,24},{12,4},{16,0},{20,28},{24,8},{28,20},{1,17},{... | collective-permute-start | bytes 7864328 | tf_op jit(solution)/shard_map/ppermute | solution.py:1202
  277.7 5.9 %collective-permute-start.33 = (bf16[4,4,128,768]{3,2,1,0:T(8,128)(2,1)}, bf16[4,4,128,768]{3,2,1,0:T(8,128)(2,1)S(1)}, u32[]{:S(2)}, u32[]{:S(2)}) collective-permute-start(bf16[4,4,128,768]{3,2,1,0:T(8,128)(2,1)} %get-tuple-element.147), channel_id=1, source_target_pairs={{0,4},{4,0},{8,12},{12,8},{16,20},{20,16},{24,28},{28,24},{1,5},{5... | collective-permute-start | bytes 9437192 | tf_op jit(solution)/shard_map/ppermute | solution.py:1202
  277.9 22.9 %collective-permute-start.35 = (bf16[4,128,1280]{2,1,0:T(8,128)(2,1)}, bf16[4,128,1280]{2,1,0:T(8,128)(2,1)}, u32[]{:S(2)}, u32[]{:S(2)}) collective-permute-start(bf16[4,128,1280]{2,1,0:T(8,128)(2,1)} %fusion), channel_id=1, source_target_pairs={{0,8},{4,20},{8,0},{12,28},{16,24},{20,4},{24,16},{28,12},{1,9},{5... | collective-permute-start | bytes 3932168 | tf_op jit(solution)/shard_map/ppermute | solution.py:1202
  287.7 38.9 %collective-permute-start.34 = (bf16[2,4,128,768]{3,2,1,0:T(8,128)(2,1)}, bf16[2,4,128,768]{3,2,1,0:T(8,128)(2,1)}, u32[]{:S(2)}, u32[]{:S(2)}) collective-permute-start(bf16[2,4,128,768]{3,2,1,0:T(8,128)(2,1)} %add_convert_fusion.1), channel_id=1, source_target_pairs={{0,16},{4,12},{8,24},{12,4},{16,0},{20,28},{24,8},{28,20},{1,17},{... | collective-permute-start | bytes 4718600 | tf_op jit(solution)/shard_map/ppermute | solution.py:1202
  321.6 10.9 %collective-permute-start.40 = (f32[96,128]{1,0:T(8,128)}, f32[96,128]{1,0:T(8,128)S(1)}, u32[]{:S(2)}, u32[]{:S(2)}) collective-permute-start(f32[96,128]{1,0:T(8,128)} %get-tuple-element.168), channel_id=1, source_target_pairs={{0,1},{1,0},{2,3},{3,2},{4,5},{5,4},{6,7},{7,6},{8,9},{9,8},{10,11... | collective-permute-start | bytes 147464 | tf_op jit(solution)/shard_map/ppermute | solution.py:1298
  323.1 19.5 %collective-permute-start.41 = (f32[96,128]{1,0:T(8,128)}, f32[96,128]{1,0:T(8,128)}, u32[]{:S(2)}, u32[]{:S(2)}) collective-permute-start(f32[96,128]{1,0:T(8,128)} %get-tuple-element.168), channel_id=1, source_target_pairs={{0,2},{1,3},{2,0},{3,1},{4,6},{5,7},{6,4},{7,5},{8,10},{9,11},{10,... | collective-permute-start | bytes 147464 | tf_op jit(solution)/shard_map/ppermute | solution.py:1298
  325.6 33.7 %collective-permute-start.42 = (f32[96,128]{1,0:T(8,128)}, f32[96,128]{1,0:T(8,128)}, u32[]{:S(2)}, u32[]{:S(2)}) collective-permute-start(f32[96,128]{1,0:T(8,128)} %get-tuple-element.168), channel_id=1, source_target_pairs={{0,3},{1,2},{2,1},{3,0},{4,7},{5,6},{6,5},{7,4},{8,11},{9,10},{10,... | collective-permute-start | bytes 147464 | tf_op jit(solution)/shard_map/ppermute | solution.py:1298
  326.1 33.2 %collective-permute-start.37 = (bf16[128,1280]{1,0:T(8,128)(2,1)}, bf16[128,1280]{1,0:T(8,128)(2,1)S(1)}, u32[]{:S(2)}, u32[]{:S(2)}) collective-permute-start(bf16[128,1280]{1,0:T(8,128)(2,1)} %get-tuple-element.151), channel_id=1, source_target_pairs={{0,1},{1,2},{2,3},{3,0},{4,5},{5,6},{6,7},{7,4},{8,9},{9,10},{10,1... | collective-permute-start | bytes 983048 | tf_op jit(solution)/shard_map/ppermute | solution.py:1206
  326.6 32.7 %collective-permute-start.38 = (bf16[128,1280]{1,0:T(8,128)(2,1)}, bf16[128,1280]{1,0:T(8,128)(2,1)}, u32[]{:S(2)}, u32[]{:S(2)}) collective-permute-start(bf16[128,1280]{1,0:T(8,128)(2,1)} %get-tuple-element.152), channel_id=1, source_target_pairs={{0,2},{1,3},{2,0},{3,1},{4,6},{5,7},{6,4},{7,5},{8,10},{9,11},{10,... | collective-permute-start | bytes 983048 | tf_op jit(solution)/shard_map/ppermute | solution.py:1206
  332.5 26.8 %collective-permute-start.39 = (bf16[128,1280]{1,0:T(8,128)(2,1)}, bf16[128,1280]{1,0:T(8,128)(2,1)S(1)}, u32[]{:S(2)}, u32[]{:S(2)}) collective-permute-start(bf16[128,1280]{1,0:T(8,128)(2,1)} %get-tuple-element.153), channel_id=1, source_target_pairs={{0,3},{1,0},{2,1},{3,2},{4,7},{5,4},{6,5},{7,6},{8,11},{9,8},{10,9... | collective-permute-start | bytes 983048 | tf_op jit(solution)/shard_map/ppermute | solution.py:1206
  342.7 16.6 %collective-permute-start.36 = (bf16[4,128,768]{2,1,0:T(8,128)(2,1)}, bf16[4,128,768]{2,1,0:T(8,128)(2,1)}, u32[]{:S(2)}, u32[]{:S(2)}) collective-permute-start(bf16[4,128,768]{2,1,0:T(8,128)(2,1)} %fusion.1), channel_id=1, source_target_pairs={{0,8},{4,20},{8,0},{12,28},{16,24},{20,4},{24,16},{28,12},{1,9},{5... | collective-permute-start | bytes 2359304 | tf_op jit(solution)/shard_map/ppermute | solution.py:1202
  363.6 8.5 %collective-permute-start.47 = (bf16[128,768]{1,0:T(8,128)(2,1)S(1)}, bf16[128,768]{1,0:T(8,128)(2,1)S(1)}, u32[]{:S(2)}, u32[]{:S(2)}) collective-permute-start(bf16[128,768]{1,0:T(8,128)(2,1)S(1)} %get-tuple-element.177), channel_id=1, source_target_pairs={{0,1},{1,2},{2,3},{3,0},{4,5},{5,6},{6,7},{7,4},{8,9},{9,10},{10,1... | collective-permute-start | bytes 589832 | tf_op jit(solution)/shard_map/ppermute | solution.py:1206
  363.7 13.1 %collective-permute-start.48 = (bf16[128,768]{1,0:T(8,128)(2,1)S(1)}, bf16[128,768]{1,0:T(8,128)(2,1)S(1)}, u32[]{:S(2)}, u32[]{:S(2)}) collective-permute-start(bf16[128,768]{1,0:T(8,128)(2,1)S(1)} %get-tuple-element.178), channel_id=1, source_target_pairs={{0,2},{1,3},{2,0},{3,1},{4,6},{5,7},{6,4},{7,5},{8,10},{9,11},{10,... | collective-permute-start | bytes 589832 | tf_op jit(solution)/shard_map/ppermute | solution.py:1206
  364.4 12.4 %collective-permute-start.49 = (bf16[128,768]{1,0:T(8,128)(2,1)S(1)}, bf16[128,768]{1,0:T(8,128)(2,1)S(1)}, u32[]{:S(2)}, u32[]{:S(2)}) collective-permute-start(bf16[128,768]{1,0:T(8,128)(2,1)S(1)} %get-tuple-element.179), channel_id=1, source_target_pairs={{0,3},{1,0},{2,1},{3,2},{4,7},{5,4},{6,5},{7,6},{8,11},{9,8},{10,9... | collective-permute-start | bytes 589832 | tf_op jit(solution)/shard_map/ppermute | solution.py:1206
  369.9 7.7 %collective-permute-start.44 = (f32[96,128]{1,0:T(8,128)S(1)}, f32[96,128]{1,0:T(8,128)S(1)}, u32[]{:S(2)}, u32[]{:S(2)}) collective-permute-start(f32[96,128]{1,0:T(8,128)S(1)} %add.140.refs_0_), channel_id=1, source_target_pairs={{0,8},{4,12},{8,0},{12,4},{16,24},{20,28},{24,16},{28,20},{1,9},{5... | collective-permute-start | bytes 147464 | tf_op jit(solution)/shard_map/ppermute | solution.py:1489
  370.6 7.0 %collective-permute-start.45 = (f32[96,128]{1,0:T(8,128)S(1)}, f32[96,128]{1,0:T(8,128)S(1)}, u32[]{:S(2)}, u32[]{:S(2)}) collective-permute-start(f32[96,128]{1,0:T(8,128)S(1)} %add.140.refs_0_), channel_id=1, source_target_pairs={{0,16},{4,20},{8,24},{12,28},{16,0},{20,4},{24,8},{28,12},{1,17},{... | collective-permute-start | bytes 147464 | tf_op jit(solution)/shard_map/ppermute | solution.py:1489
  372.1 5.5 %collective-permute-start.46 = (f32[96,128]{1,0:T(8,128)S(1)}, f32[96,128]{1,0:T(8,128)S(1)}, u32[]{:S(2)}, u32[]{:S(2)}) collective-permute-start(f32[96,128]{1,0:T(8,128)S(1)} %add.140.refs_0_), channel_id=1, source_target_pairs={{0,24},{4,28},{8,16},{12,20},{16,8},{20,12},{24,0},{28,4},{1,25},{... | collective-permute-start | bytes 147464 | tf_op jit(solution)/shard_map/ppermute | solution.py:1489
  (32 other events, 432.6 us)
Sparse Core Ops, SparseCore 0:
  28.7 34.1 all-gather.4
  67.4 25.2 all-gather.6
  165.6 70.9 reduce-scatter.2
  279.5 26.9 reduce-scatter.4
